TPU v7x, 32 devices: a whole 2x2x4 slice. The times are simulated.
32 devices in a mesh: dp: 32 (over z, y, x, core), mp: 1.
Axes of the slice: x: 2, y: 2, z: 4, core: 2. Of those that a mesh axis runs over, the one named last changes fastest.
Arguments:
- features: bfloat16 [131072, 1024], P('dp'), may hold values from -6 to 6
- w_in: bfloat16 [1024, 1024], P(None, 'mp'), may hold values from -0.1875 to 0.1875
- w_out: bfloat16 [1024, 128], P('mp'), may hold values from -0.1875 to 0.1875
- send_rows: int32 [65536], P(('dp', 'mp')), may hold values from 0 to 4095
- pair_src: int32 [131072, 16], P(('dp', 'mp')), may hold values from 0 to 2047
- pair_weight: float32 [131072, 16], P(('dp', 'mp')), may hold values from 0.1 to 1
- pair_mask: int32 [131072, 16], P(('dp', 'mp')), may hold values 0 or 1
Outputs:
- grad_in: float32 [1024, 1024], P(None, 'mp')
- grad_out: float32 [1024, 128], P('mp')
Inputs may be any that keep to these rules, and one draw needn't show every extreme that they name: `send_rows`: local row indices of the sending device.
All inputs are finite; a program needn't handle non-finite values. No bound on the sum of `pair_mask` on one device may be relied on, other than what follows from the above.
Results may differ from a plain program's by a relative error of at most 0.0062.
Values may be sent and summed in bfloat16 or wider, within the bound.
No kernel may reach another device: no remote copies, remote signals or barrier semaphores. Data moves between devices by JAX's collectives and lax.ppermute only.
A program may use at most 192 MiB of HBM per device.

v0:
```python
import math

import jax
import jax.numpy as jnp
from jax import lax
from jax.sharding import PartitionSpec as P


def shards(features, w_in, w_out, send_rows, pair_src, pair_weight, pair_mask):
    high = lax.Precision.HIGHEST
    n_dp = lax.axis_size("dp")
    n_mp = lax.axis_size("mp")
    group_rows = features.shape[0]
    nodes = group_rows * n_dp
    rows = group_rows // n_mp
    width = w_out.shape[1]
    pairs = pair_src.shape[1]
    scale = 1.0 / (pairs * math.sqrt(nodes))
    pre = jnp.dot(features, w_in, preferred_element_type=jnp.float32)
    hidden = jax.nn.silu(pre).astype(jnp.bfloat16)
    embed = lax.psum_scatter(
        jnp.dot(hidden, w_out, preferred_element_type=jnp.float32),
        "mp",
        scatter_dimension=0,
        tiled=True,
    )
    coef = pair_weight * pair_mask.astype(jnp.float32) * scale
    gram_part = jnp.dot(embed.T, embed, precision=high)
    recv_count = send_rows.shape[0]
    arrived = lax.all_to_all(embed[send_rows], "dp", split_axis=0, concat_axis=0, tiled=True)
    diff = embed[:, None, :] - arrived[pair_src]
    weighted = coef[:, :, None] * diff
    spread_part = jnp.dot(weighted.reshape(-1, width).T, diff.reshape(-1, width), precision=high)
    own = jnp.sum(weighted, axis=1)
    back_terms = jax.ops.segment_sum(
        (-weighted).reshape(-1, width), pair_src.reshape(-1), num_segments=recv_count
    )
    returned = lax.all_to_all(back_terms, "dp", split_axis=0, concat_axis=0, tiled=True)
    nearby = own + jax.ops.segment_sum(returned, send_rows, num_segments=rows)
    gram_sum, spread = lax.psum((gram_part, spread_part), ("dp", "mp"))
    chol = jnp.linalg.cholesky(gram_sum / nodes)
    eye = jnp.eye(width, dtype=jnp.float32)
    lower_inv = lax.linalg.triangular_solve(
        chol, eye, left_side=True, lower=True, transpose_a=False
    )
    inverse = jnp.dot(lower_inv.T, lower_inv, precision=high)
    sandwich = jnp.dot(jnp.dot(inverse, spread, precision=high), inverse, precision=high)
    grad_y = 2.0 * jnp.dot(nearby, inverse, precision=high) - 2.0 / nodes * jnp.dot(
        embed, sandwich, precision=high
    )
    grad_y = grad_y.astype(jnp.bfloat16)
    piece = lax.all_gather(grad_y, "mp", axis=0, tiled=True)
    g_out = jnp.dot(hidden.T, piece, preferred_element_type=jnp.float32)
    back_hidden = jnp.dot(piece, w_out.T, preferred_element_type=jnp.float32)
    sig = jax.nn.sigmoid(pre)
    grad_pre = (back_hidden * sig * (1.0 + pre * (1.0 - sig))).astype(jnp.bfloat16)
    g_in = jnp.dot(features.T, grad_pre, preferred_element_type=jnp.float32)
    g_in, g_out = (g_in, g_out)
    grad_in, grad_out = lax.psum((g_in, g_out), "dp")
    return (grad_in, grad_out)


def solution(mesh):
    return jax.shard_map(
        shards,
        mesh=mesh,
        in_specs=(
            P("dp", None),
            P(None, "mp"),
            P("mp", None),
            P(("dp", "mp")),
            P(("dp", "mp"), None),
            P(("dp", "mp"), None),
            P(("dp", "mp"), None),
        ),
        out_specs=(P(None, "mp"), P("mp", None)),
        check_vma=False,
    )
```

profile of v0, /device:TPU:0, one launch (start us, length us, event | category | flops | bytes accessed | tf_op | source)
XLA Modules:
  0.0 1124.5 jit_solution(17295232358317478732)
XLA Ops:
  8.8 16.5 %multiply_convert_fusion.1 = (bf16[4096,1024]{1,0:T(8,128)(2,1)S(1)}, f32[4096,1024]{1,0:T(8,128)}) fusion(bf16[4096,1024]{1,0:T(8,128)(2,1)} %param.7, bf16[1024,1024]{1,0:T(8,128)(2,1)S(1)} %copy-done), kind=kOutput, calls=%fused_computation.11 | convolution fusion | flops 8610906112 | bytes 35651584 | tf_op jit(solution)/shard_map/dot_general | solution.py:19
  25.3 3.2 copy-done.2
  30.9 7.6 gather_fusion
  38.5 7.8 all-to-all-start
  49.0 2.9 copy.14
  51.8 2.8 reshape.36
  60.4 2.8 reshape.44
  63.1 4.1 fusion.20
  68.2 4.3 all-to-all-done
  72.5 216.9 %gather_fusion.1 = f32[65536,128]{1,0:T(8,128)} fusion(f32[2048,128]{1,0:T(8,128)S(1)} %bitcast.47, s32[65536]{0:T(1024)S(1)} %broadcast_clamp_fusion), kind=kCustom, calls=%fused_computation.1 | custom fusion | bytes 67371008 | tf_op jit(solution)/shard_map/gather | solution.py:31
  289.5 29.2 %multiply_reduce_fusion = (f32[4096,128]{1,0:T(8,128)}, f32[4096,16,128]{2,1,0:T(8,128)}) fusion(f32[4096,16]{1,0:T(8,128)} %copy.13, f32[4096,128]{1,0:T(8,128)S(1)} %fusion.19, f32[65536,128]{1,0:T(8,128)} %gather_fusion.1), kind=kLoop, calls=%fused_computation.6 | loop fusion | flops 24641536 | bytes 71565312 | tf_op jit(solution)/shard_map/reduce_sum | solution.py:34
  318.7 23.1 %fusion.2 = f32[65536,128]{1,0:T(8,128)} fusion(f32[4096,16,128]{2,1,0:T(8,128)} %get-tuple-element.11, f32[65536]{0:T(1024)S(1)} %copy-done.3), kind=kLoop, calls=%fused_computation.8 | loop fusion | flops 16777216 | bytes 67371008 | tf_op jit(solution)/shard_map/neg | solution.py:36
  341.8 348.3 %scatter_custom_fusion = f32[2048,128]{1,0:T(8,128)} fusion(s32[65536]{0:T(1024)} %reshape.44, f32[65536,128]{1,0:T(8,128)} %fusion.2, f32[]{:T(128)} %constant.57.clone.1), kind=kCustom, calls=%fused_computation.22 | custom fusion | flops 8388608 | bytes 1049088 | tf_op jit(solution)/shard_map/scatter-add | solution.py:35
  690.1 3.6 all-to-all-start.1
  694.0 71.9 %fusion.8 = f32[128,128]{1,0:T(8,128)} fusion(f32[4096,16,128]{2,1,0:T(8,128)} %get-tuple-element.11, f32[4096,16]{1,0:T(8,128)} %copy.13), kind=kOutput, calls=%fused_computation.20 | convolution fusion | flops 12893290496 | bytes 33882112 | tf_op jit(solution)/shard_map/dot_general | solution.py:33
  766.0 124.1 %all-reduce.7.cloned.1.call-done = (f32[128,128]{0,1:T(8,128)}, f32[128,128]{1,0:T(8,128)}) async-done(((f32[128,128]{0,1:T(8,128)}, f32[128,128]{1,0:T(8,128)}), (f32[128,128]{0,1:T(8,128)}, f32[128,128]{1,0:T(8,128)})) %all-reduce.7.cloned.1.call-update) | async-done | bytes 131088 | tf_op jit(solution)/shard_map/psum | solution.py:40
  891.9 11.7 %cholesky.17 = f32[128,128]{1,0:T(8,128)S(1)} custom-call(f32[128,128]{1,0:T(8,128)S(1)} %fusion.16), custom_call_target="Cholesky" | custom-call | tf_op jit(solution)/shard_map/jit(cholesky)/cholesky | solution.py:41
  904.9 9.8 custom-call.6
  916.6 13.4 %scatter_fusion = f32[4096,128]{1,0:T(8,128)} fusion(f32[4096,128]{1,0:T(8,128)} %get-tuple-element.10, s32[2048]{0:T(1024)S(1)} %copy-done.8, f32[2048,128]{1,0:T(8,128)S(1)} %bitcast.48), kind=kCustom, calls=%fused_computation.3 | custom fusion | flops 262144 | bytes 3153920 | tf_op jit(solution)/shard_map/scatter-add | solution.py:39
  930.0 3.4 convolution_multiply_fusion.1
  935.3 6.5 fusion.24
  941.8 25.3 %fusion.7 = f32[1024,1024]{0,1:T(8,128)} fusion(bf16[4096,1024]{1,0:T(8,128)(2,1)} %param.7, f32[4096,1024]{1,0:T(8,128)} %get-tuple-element.13, bf16[4096,128]{1,0:T(8,128)(2,1)S(1)} %fusion.6, bf16[1024,128]{1,0:T(8,128)(2,1)S(1)} %copy-done.7), kind=kOutput, calls=%fused_computation.19 | convolution fusion | flops 9701425152 | bytes 30670848 | tf_op jit(solution)/shard_map/dot_general | solution.py:57
  967.1 143.9 %all-reduce.5.cloned.1.call-done = (f32[1024,1024]{0,1:T(8,128)}, f32[1024,128]{1,0:T(8,128)}) async-done(((f32[1024,1024]{0,1:T(8,128)}, f32[1024,128]{1,0:T(8,128)}), (f32[1024,1024]{0,1:T(8,128)}, f32[1024,128]{1,0:T(8,128)})) %all-reduce.5.cloned.1.call-update) | async-done | bytes 4718608 | tf_op jit(solution)/shard_map/psum | solution.py:59
  1111.0 5.4 copy.19
  (42 shorter events, 21.2 us)
Async XLA Ops:
  7.2 1.6 copy-start
  8.8 19.7 %copy-start.6 = (bf16[1024,128]{1,0:T(8,128)(2,1)S(1)}, bf16[1024,128]{1,0:T(8,128)(2,1)}, u32[]{:S(2)}) copy-start(bf16[1024,128]{1,0:T(8,128)(2,1)} %param.9) | copy-start | bytes 786436
  25.3 3.2 copy-start.2
  30.9 15.4 %copy-start.4 = (s32[4096,16]{0,1:T(8,128)S(1)}, s32[4096,16]{0,1:T(8,128)}, u32[]{:S(2)}) copy-start(s32[4096,16]{0,1:T(8,128)} %param.11) | copy-start | bytes 786436
  38.5 34.0 %all-to-all-start = ((f32[32,64,128]{2,1,0:T(8,128)}), f32[32,64,128]{2,1,0:T(8,128)S(1)}, u32[]{:S(2)}, u32[]{:S(2)}) async-start(f32[32,64,128]{2,1,0:T(8,128)} %bitcast.50), calls=%async_computation | async-start | bytes 2097152 | tf_op jit(solution)/shard_map/all_to_all | solution.py:30
  289.4 29.2 %copy-start.3 = (f32[65536]{0:T(1024)S(1)}, f32[65536]{0:T(1024)}, u32[]{:S(2)}) copy-start(f32[65536]{0:T(1024)} %mul.55) | copy-start | bytes 786436
  690.1 226.4 %all-to-all-start.1 = ((f32[32,64,128]{2,1,0:T(8,128)}), f32[32,64,128]{2,1,0:T(8,128)S(1)}, u32[]{:S(2)}, u32[]{:S(2)}) async-start(f32[32,64,128]{2,1,0:T(8,128)} %bitcast.49), calls=%async_computation.1 | async-start | bytes 2097152 | tf_op jit(solution)/shard_map/all_to_all | solution.py:38
  693.7 222.8 %copy-start.8 = (s32[2048]{0:T(1024)S(1)}, s32[2048]{0:T(1024)}, u32[]{:S(2)}) copy-start(s32[2048]{0:T(1024)} %param.10) | copy-start | bytes 24580
  693.7 196.3 %all-reduce.7.cloned.1.call-start = ((), (), s32[]{:S(2)}) async-start(), calls=%async_computation.3 | async-start | bytes 262144 | tf_op jit(solution)/shard_map/psum | solution.py:40
  765.9 345.1 %all-reduce.5.cloned.1.call-start = ((), (), s32[]{:S(2)}) async-start(), calls=%async_computation.2 | async-start | bytes 9437184 | tf_op jit(solution)/shard_map/psum | solution.py:59
  933.4 8.4 copy-start.7
  941.8 175.4 %copy-start.1 = (bf16[1024,1024]{1,0:T(8,128)(2,1)S(1)}, bf16[1024,1024]{1,0:T(8,128)(2,1)}, u32[]{:S(2)}) copy-start(bf16[1024,1024]{1,0:T(8,128)(2,1)} %param.8) | copy-start | bytes 6291460
  1111.0 5.4 copy-start.5
Sparse Core Ops, SparseCore 0:
  766.0 123.9 all-reduce.6
  967.2 143.7 all-reduce.4
where the time goes:
time: 1130 us; the launch traced here: 1120 us
  other arithmetic  442 us (39%)
  waiting for transfers between devices  272 us (24%)
  local copies, waits for them, and re-layouts  250 us (22%)
  matrix products  134 us (12%)
  between operations  14.7 us (1%)
  starting transfers between devices  11.6 us (1%)
    scatter-add x1, other arithmetic, shards(): jax.ops.segment_sum((-weighted).reshape(-1, width), pair_src.reshape(-1),...  348 us
    gather x1, local copies, waits for them, and re-layouts, shards(): diff = embed[:, None, :] - arrived[pair_src]  217 us
    psum x1, waiting for transfers between devices, shards(): grad_in, grad_out = lax.psum((g_in, g_out), 'dp')  144 us
    psum x1, waiting for transfers between devices, shards(): gram_sum, spread = lax.psum((gram_part, spread_part), ('dp', 'mp'))  124 us
    dot_general x1, matrix products, shards(): jnp.dot(weighted.reshape(-1, width).T, diff.reshape(-1, width), precision...  71.9 us
    reduce_sum x1, other arithmetic, shards(): own = jnp.sum(weighted, axis=1)  29.2 us
    dot_general x1, matrix products, shards(): g_in = jnp.dot(features.T, grad_pre, preferred_element_type=jnp.float32)  25.3 us
    neg x1, other arithmetic, shards(): -weighted  23.1 us
  transfers between devices with their start and end apart: 4, of which 3 were waited for; matrix products, arithmetic and copies ran while one was open for 11% of the time, Pallas kernels for 0%

commit v1 on v0

v1 whole, which is shorter than its diff:
```python
import functools
import math

import jax
import jax.numpy as jnp
from jax import lax
from jax.experimental import pallas as pl
from jax.experimental.pallas import tpu as pltpu
from jax.sharding import PartitionSpec as P

F32 = jnp.float32
BF16 = jnp.bfloat16
LANES = 128
WIDE = 256
STEPS = 8
VMEM_BYTES = 56 * 1024 * 1024


def params(steps=1):
    return pltpu.CompilerParams(
        dimension_semantics=("arbitrary",) * steps, vmem_limit_bytes=VMEM_BYTES
    )


def cost(flops, read):
    return pl.CostEstimate(flops=int(flops), bytes_accessed=int(read), transcendentals=0)


def dot_tn(a, b):
    return lax.dot_general(a, b, (((0,), (0,)), ((), ())), preferred_element_type=F32)


def dot_nt(a, b):
    return lax.dot_general(a, b, (((1,), (1,)), ((), ())), preferred_element_type=F32)


def dot(a, b):
    return jnp.dot(a, b, preferred_element_type=F32)


def forward_kernel(x_ref, w_in_ref, w_out_ref, hidden_ref, slope_ref, y_ref):
    units = w_in_ref.shape[1]
    step = min(512, units)
    x = x_ref[...]
    for at in range(0, units, step):
        pre = dot(x, w_in_ref[:, at:at + step])
        sig = jax.nn.sigmoid(pre)
        act = pre * sig
        hidden_ref[:, at:at + step] = act.astype(BF16)
        slope_ref[:, at:at + step] = sig + act * (1.0 - sig)
    y_ref[...] = dot(hidden_ref[...], w_out_ref[...]).astype(y_ref.dtype)


def forward(features, w_in, w_out, y_type):
    nodes, din = features.shape
    units = w_in.shape[1]
    width = w_out.shape[1]
    tile = min(1024, nodes)
    return pl.pallas_call(
        forward_kernel,
        grid=(nodes // tile,),
        in_specs=[
            pl.BlockSpec((tile, din), lambda i: (i, 0)),
            pl.BlockSpec((din, units), lambda i: (0, 0)),
            pl.BlockSpec((units, width), lambda i: (0, 0)),
        ],
        out_specs=[
            pl.BlockSpec((tile, units), lambda i: (i, 0)),
            pl.BlockSpec((tile, units), lambda i: (i, 0)),
            pl.BlockSpec((tile, width), lambda i: (i, 0)),
        ],
        out_shape=[
            jax.ShapeDtypeStruct((nodes, units), BF16),
            jax.ShapeDtypeStruct((nodes, units), F32),
            jax.ShapeDtypeStruct((nodes, width), y_type),
        ],
        compiler_params=params(),
        cost_estimate=cost(2 * nodes * units * (din + width), 2 * nodes * (din + 2 * units)),
        name="forward",
    )(features, w_in, w_out)


def send_kernel(y_ref, index_ref, sent_ref, gram_ref):
    rows = y_ref.shape[0]
    y = y_ref[...]
    gram_ref[...] = dot_tn(y, y)
    columns = index_ref[...].T
    each = 4 if index_ref.shape[0] % 4 == 0 else 1
    place = lax.broadcasted_iota(jnp.int32, (LANES, rows), 1)
    for at in range(0, index_ref.shape[0], each):
        spots = [
            jnp.where(place == columns[:, k:k + 1], 1.0, 0.0).astype(BF16)
            for k in range(at, at + each)
        ]
        spots = jnp.concatenate(spots, axis=0)
        sent_ref[at * LANES:(at + each) * LANES, :] = dot(spots, y).astype(BF16)


def send(y, send_rows):
    rows, width = y.shape
    count = send_rows.shape[0]
    return pl.pallas_call(
        send_kernel,
        out_shape=[
            jax.ShapeDtypeStruct((count, width), BF16),
            jax.ShapeDtypeStruct((width, width), F32),
        ],
        compiler_params=pltpu.CompilerParams(vmem_limit_bytes=VMEM_BYTES),
        cost_estimate=cost(2 * rows * count * width, 2 * width * (rows + count)),
        name="send",
    )(y, send_rows.reshape(count // LANES, LANES))


def weights_kernel(pairs, first, *refs):
    if first:
        src_ref, coef_ref, y_ref, weights_ref, scaled_ref, back_ref, square_ref = refs
    else:
        src_ref, coef_ref, y_ref, back_in, square_in = refs[:5]
        weights_ref, scaled_ref, back_ref, square_ref = refs[5:]
    groups, per = src_ref.shape
    count = weights_ref.shape[1]
    members = per // pairs
    high = count // WIDE

    @pl.when(pl.program_id(0) == 0)
    def _():
        if first:
            back_ref[...] = jnp.zeros_like(back_ref)
            square_ref[...] = jnp.zeros_like(square_ref)
        else:
            back_ref[...] = back_in[...]
            square_ref[...] = square_in[...]

    member = lax.broadcasted_iota(jnp.int32, (1, per), 1) // pairs
    row = lax.broadcasted_iota(jnp.int32, (high * members, per), 0)
    lane = lax.broadcasted_iota(jnp.int32, (WIDE, per), 0)
    for g in range(groups):
        src = src_ref[g:g + 1, :]
        target = (src // WIDE) * members + member
        left = jnp.where(row == target, coef_ref[g:g + 1, :], 0.0).astype(BF16)
        right = jnp.where(lane == src % WIDE, 1.0, 0.0).astype(BF16)
        part = dot_nt(left, right).astype(BF16)
        sums = None
        at = slice(g * members, (g + 1) * members)
        for h in range(high):
            piece = part[h * members:(h + 1) * members, :]
            weights_ref[at, h * WIDE:(h + 1) * WIDE] = piece
            sums = piece.astype(F32) if sums is None else sums + piece.astype(F32)
        scaled_ref[at, :] = jnp.sum(sums, axis=1, keepdims=True) * y_ref[at, :].astype(F32)
    y = y_ref[...]
    left = jnp.concatenate([y.astype(F32).T.astype(BF16), jnp.ones((16, y.shape[0]), BF16)], axis=0)
    back_ref[...] += dot(left, weights_ref[...])
    square_ref[...] += dot_tn(y, scaled_ref[...].astype(BF16))


def weights_of(src, coef, y, carry, pairs, count, part, parts):
    rows, width = y.shape[0] // parts, y.shape[1]
    per = src.shape[1]
    members = per // pairs
    groups = min(16, src.shape[0] // parts)
    tile = groups * members
    skip = part * (rows // tile)
    sums = [
        jax.ShapeDtypeStruct((width + 16, count), F32),
        jax.ShapeDtypeStruct((width, width), F32),
    ]
    sum_specs = [pl.BlockSpec(x.shape, lambda i: (0, 0)) for x in sums]
    return pl.pallas_call(
        functools.partial(weights_kernel, pairs, part == 0),
        grid=(rows // tile,),
        in_specs=[
            pl.BlockSpec((groups, per), lambda i: (i + skip, 0)),
            pl.BlockSpec((groups, per), lambda i: (i + skip, 0)),
            pl.BlockSpec((tile, width), lambda i: (i + skip, 0)),
        ]
        + (sum_specs if part else []),
        out_specs=[
            pl.BlockSpec((tile, count), lambda i: (i, 0)),
            pl.BlockSpec((tile, width), lambda i: (i, 0)),
        ]
        + sum_specs,
        out_shape=[
            jax.ShapeDtypeStruct((rows, count), BF16),
            jax.ShapeDtypeStruct((rows, width), F32),
        ]
        + sums,
        compiler_params=params(),
        cost_estimate=cost(4 * rows * count * width, 2 * rows * count),
        name="weights",
    )(src, coef, y, *carry)


def back_kernel(got_ref, sums_ref, square_ref, back_ref, spread_ref):
    width = got_ref.shape[1]
    got = got_ref[...]
    sums = sums_ref[...].T
    back = (sums[:, width:width + 1] * got.astype(F32) - sums[:, :width]).astype(BF16)
    back_ref[...] = back
    cross = dot(sums_ref[:width, :].astype(BF16), got)
    spread_ref[...] = square_ref[...] - cross + dot_tn(got, back)


def back_of(got, sums, square):
    count, width = got.shape
    return pl.pallas_call(
        back_kernel,
        out_shape=[
            jax.ShapeDtypeStruct((count, width), BF16),
            jax.ShapeDtypeStruct((width, width), F32),
        ],
        compiler_params=pltpu.CompilerParams(vmem_limit_bytes=VMEM_BYTES),
        cost_estimate=cost(4 * count * width * width, 6 * count * width),
        name="back",
    )(got, sums, square)


def own_kernel(parts, nodes, *refs):
    weights_refs = refs[:parts]
    scaled_refs = refs[parts:2 * parts]
    got_ref, gram_ref, own_ref, inverse_ref = refs[2 * parts:]
    steps = pl.num_programs(0)
    each = steps // parts
    width = gram_ref.shape[0]
    split_by = width // STEPS

    @pl.when(pl.program_id(0) == 0)
    def _():
        inverse_ref[...] = gram_ref[...] * (1.0 / nodes)

    for part in range(parts):

        @pl.when(pl.program_id(0) // each == part)
        def _():
            own_ref[...] = scaled_refs[part][...] - dot(weights_refs[part][...], got_ref[...])
            matrix = inverse_ref[...]
            matrix = eliminate(matrix, pl.program_id(0) * split_by, split_by)
            inverse_ref[...] = matrix


def eliminate(matrix, start, count):
    width = matrix.shape[0]
    rows = lax.broadcasted_iota(jnp.int32, (width, width), 0)
    lanes = lax.broadcasted_iota(jnp.int32, (width, width), 1)
    for step in range(count):
        k = start + step
        at_row = rows == k
        at_lane = lanes == k
        row = jnp.sum(jnp.where(at_row, matrix, 0.0), axis=0, keepdims=True)
        column = jnp.sum(jnp.where(at_lane, matrix, 0.0), axis=1, keepdims=True)
        pivot = 1.0 / jnp.sum(jnp.where(at_lane[:1], row, 0.0), axis=1, keepdims=True)
        scaled = jnp.where(at_lane[:1], pivot, row * pivot)
        rest = jnp.where(at_lane, 0.0, matrix) - column * scaled
        matrix = jnp.where(at_row, scaled, rest)
    return matrix


def part_block(tile, count, part, each):
    return pl.BlockSpec((tile, count), lambda i: (jnp.clip(i - part * each, 0, each - 1), 0))


def own_of(weights, scaled, got, gram, nodes):
    count, width = got.shape
    parts = len(weights)
    rows = weights[0].shape[0] * parts
    tile = rows // STEPS
    each = STEPS // parts
    return pl.pallas_call(
        functools.partial(own_kernel, parts, nodes),
        grid=(STEPS,),
        in_specs=[part_block(tile, count, part, each) for part in range(parts)]
        + [part_block(tile, width, part, each) for part in range(parts)]
        + [
            pl.BlockSpec((count, width), lambda i: (0, 0)),
            pl.BlockSpec((width, width), lambda i: (0, 0)),
        ],
        out_specs=[
            pl.BlockSpec((tile, width), lambda i: (i, 0)),
            pl.BlockSpec((width, width), lambda i: (0, 0)),
        ],
        out_shape=[
            jax.ShapeDtypeStruct((rows, width), F32),
            jax.ShapeDtypeStruct((width, width), F32),
        ],
        compiler_params=params(),
        cost_estimate=cost(2 * rows * count * width, 2 * rows * count),
        name="own",
    )(*weights, *scaled, got, gram)


def split(value):
    first = value.astype(BF16)
    return first, (value - first.astype(F32)).astype(BF16)


def grad_y_kernel(
    nodes, scale, own_ref, y_ref, index_ref, returned_ref, inverse_ref, spread_ref, out_ref, right_ref
):
    tile, width = own_ref.shape
    count = returned_ref.shape[0]

    @pl.when(pl.program_id(0) == 0)
    def _():
        high = lax.Precision.HIGHEST
        inverse = inverse_ref[...]
        half = jnp.dot(inverse, spread_ref[...], precision=high, preferred_element_type=F32)
        sandwich = jnp.dot(half, inverse, precision=high, preferred_element_type=F32)
        for at, value in ((0, 2.0 * scale * inverse), (width, -2.0 * scale / nodes * sandwich)):
            first, second = split(value)
            right_ref[at:at + width, :width] = first
            right_ref[at:at + width, width:] = second

    at = lax.broadcasted_iota(jnp.int32, (tile, count), 0) + pl.program_id(0) * tile
    spots = jnp.where(at == index_ref[...], 1.0, 0.0).astype(BF16)
    nearby = own_ref[...] + dot(spots, returned_ref[...])
    first, second = split(nearby)
    both = dot(jnp.concatenate([first, y_ref[...]], axis=1), right_ref[...])
    total = both[:, :width] + both[:, width:] + dot(second, right_ref[:width, :width])
    out_ref[...] = total.astype(BF16)


def grad_y_of(own, y, send_rows, returned, inverse, spread, nodes, scale):
    rows, width = y.shape
    count = returned.shape[0]
    tile = min(512, rows)
    return pl.pallas_call(
        functools.partial(grad_y_kernel, nodes, scale),
        grid=(rows // tile,),
        in_specs=[
            pl.BlockSpec((tile, width), lambda i: (i, 0)),
            pl.BlockSpec((tile, width), lambda i: (i, 0)),
            pl.BlockSpec((1, count), lambda i: (0, 0)),
            pl.BlockSpec((count, width), lambda i: (0, 0)),
            pl.BlockSpec((width, width), lambda i: (0, 0)),
            pl.BlockSpec((width, width), lambda i: (0, 0)),
        ],
        out_specs=pl.BlockSpec((tile, width), lambda i: (i, 0)),
        out_shape=jax.ShapeDtypeStruct((rows, width), BF16),
        scratch_shapes=[pltpu.VMEM((2 * width, 2 * width), BF16)],
        compiler_params=params(),
        cost_estimate=cost(2 * rows * count * width, 8 * rows * width),
        name="grad_y",
    )(own, y, send_rows.reshape(1, count), returned, inverse, spread)


def radices(n):
    result, shift = [], 0
    while 1 << shift < n:
        bits = 1 if shift == 0 else min(2, n.bit_length() - 1 - shift)
        result.append((shift, 1 << bits))
        shift += bits
    return result


def position(relative, n):
    total = 0
    for shift, radix in radices(n):
        total = total * radix + ((relative >> shift) & (radix - 1))
    return total


def backward_kernel(n, x_ref, hidden_ref, slope_ref, gy_ref, w_out_ref, me_ref, *rest):
    *outs, g_in, g_out = rest
    gy = gy_ref[...]
    x = x_ref[...]

    @pl.when(pl.program_id(0) == 0)
    def _():
        g_in[...] = jnp.zeros_like(g_in)
        g_out[...] = jnp.zeros_like(g_out)

    units = g_in.shape[1]
    step = min(512, units)
    for at in range(0, units, step):
        back = dot_nt(gy, w_out_ref[at:at + step, :])
        grad = (back * slope_ref[:, at:at + step].astype(F32)).astype(BF16)
        g_in[:, at:at + step] += dot_tn(x, grad)
    g_out[...] += dot_tn(hidden_ref[...], gy)

    @pl.when(pl.program_id(0) == pl.num_programs(0) - 1)
    def _():
        if n is None:
            outs[0][...] = g_in[...]
            outs[1][...] = g_out[...]
        else:
            me = me_ref[0]
            chunk = g_in.shape[0] // n
            for pair in range(n // 2):
                for side, out in enumerate(outs):
                    c = 2 * pair + (me + side) % 2
                    at = pl.multiple_of((position(me ^ c, n) % (n // 2)) * chunk, chunk)
                    rows = pl.ds(pl.multiple_of(c * chunk, chunk), chunk)
                    out[pl.ds(at, chunk), :units] = g_in[rows, :].astype(out.dtype)
                    out[pl.ds(at, chunk), units:] = g_out[rows, :].astype(out.dtype)


def backward(features, hidden, slope, gy, w_out, me, n):
    nodes, din = features.shape
    units, width = w_out.shape
    tile = min(1024, nodes)
    if n is None:
        outs = [jax.ShapeDtypeStruct((din, units), F32), jax.ShapeDtypeStruct((units, width), F32)]
    else:
        outs = [
            jax.ShapeDtypeStruct((din // 2, units + width), F32),
            jax.ShapeDtypeStruct((din // 2, units + width), BF16),
        ]
    return pl.pallas_call(
        functools.partial(backward_kernel, n),
        grid=(nodes // tile,),
        in_specs=[
            pl.BlockSpec((tile, din), lambda i: (i, 0)),
            pl.BlockSpec((tile, units), lambda i: (i, 0)),
            pl.BlockSpec((tile, units), lambda i: (i, 0)),
            pl.BlockSpec((tile, width), lambda i: (i, 0)),
            pl.BlockSpec((units, width), lambda i: (0, 0)),
            pl.BlockSpec(memory_space=pltpu.SMEM),
        ],
        out_specs=[pl.BlockSpec(o.shape, lambda i: (0, 0)) for o in outs],
        out_shape=outs,
        scratch_shapes=[pltpu.VMEM((din, units), F32), pltpu.VMEM((units, width), F32)],
        compiler_params=params(),
        cost_estimate=cost(2 * nodes * units * (din + 2 * width), 2 * nodes * (din + 2 * units)),
        name="backward",
    )(features, hidden, slope, gy, w_out, me)


def unpack_kernel(n, packed_ref, me_ref, g_in_ref, g_out_ref):
    units = g_in_ref.shape[1]
    rows = g_in_ref.shape[0]
    chunk = packed_ref.shape[0] // n
    me = me_ref[0]
    first = pl.program_id(0) * (rows // chunk)
    for c in range(rows // chunk):
        at = pl.multiple_of(position(me ^ (first + c), n) * chunk, chunk)
        part = packed_ref[pl.ds(at, chunk), :].astype(F32)
        g_in_ref[c * chunk:(c + 1) * chunk, :] = part[:, :units]
        g_out_ref[c * chunk:(c + 1) * chunk, :] = part[:, units:]


def unpack(packed, me, n, width):
    din, both = packed.shape
    units = both - width
    tile = din // 4
    return pl.pallas_call(
        functools.partial(unpack_kernel, n),
        grid=(din // tile,),
        in_specs=[
            pl.BlockSpec((din, both), lambda i: (0, 0)),
            pl.BlockSpec(memory_space=pltpu.SMEM),
        ],
        out_specs=[
            pl.BlockSpec((tile, units), lambda i: (i, 0)),
            pl.BlockSpec((tile, width), lambda i: (i, 0)),
        ],
        out_shape=[
            jax.ShapeDtypeStruct((din, units), F32),
            jax.ShapeDtypeStruct((din, width), F32),
        ],
        compiler_params=params(),
        cost_estimate=cost(din * both, 6 * din * both),
        name="unpack",
    )(packed, me)


def exchange(value, axis, n, mask):
    return lax.ppermute(value, axis, [(i, i ^ mask) for i in range(n)])


def sum_small(value, axis, n, beside):
    if n & (n - 1):
        return lax.psum(value, axis)
    for k, (shift, radix) in enumerate(radices(n)):
        got = [exchange(value, axis, n, m << shift) for m in range(1, radix)]
        if k < len(beside):
            got, _ = lax.optimization_barrier((got, beside[k]))
        value = sum(got, value)
    return value


def reduce_packed(kept, sent, axis, n):
    steps = radices(n)
    value = kept + exchange(sent, axis, n, 1).astype(F32)
    for shift, radix in steps[1:]:
        size = value.shape[0] // radix
        total = value[:size]
        for m in range(1, radix):
            part = value[m * size:(m + 1) * size].astype(BF16)
            total = total + exchange(part, axis, n, m << shift).astype(F32)
        value = total
    value = value.astype(BF16)
    for shift, radix in reversed(steps):
        parts = [value] + [exchange(value, axis, n, m << shift) for m in range(1, radix)]
        value = jnp.concatenate(parts, axis=0)
    return value


def shards(features, w_in, w_out, send_rows, pair_src, pair_weight, pair_mask):
    n_dp = lax.axis_size("dp")
    n_mp = lax.axis_size("mp")
    group_rows, din = features.shape
    nodes = group_rows * n_dp
    rows = group_rows // n_mp
    units, width = w_out.shape
    pairs = pair_src.shape[1]
    count = send_rows.shape[0]
    scale = 1.0 / (pairs * math.sqrt(nodes))
    me = lax.axis_index("dp").astype(jnp.int32).reshape(1)

    per = 256
    src = pair_src.reshape(rows * pairs // per, per)
    coef = (pair_weight * pair_mask.astype(F32)).reshape(rows * pairs // per, per)

    hidden, slope, y = forward(features, w_in, w_out, BF16 if n_mp == 1 else F32)
    if n_mp > 1:
        y = lax.psum_scatter(y, "mp", scatter_dimension=0, tiled=True).astype(BF16)
    sent, gram = send(y, send_rows)
    got = lax.all_to_all(sent, "dp", split_axis=0, concat_axis=0, tiled=True)
    parts = 4 if rows % (4 * 256) == 0 else 1
    weights, scaled, carry, marks = [], [], (), []
    for part in range(parts):
        piece, with_y, *carry = weights_of(src, coef, y, carry, pairs, count, part, parts)
        weights.append(piece)
        scaled.append(with_y)
        marks.append(carry[1])
    gram = sum_small(gram, "dp", n_dp, marks)
    if n_mp > 1:
        gram = lax.psum(gram, "mp")
    back, spread = back_of(got, *carry)
    returned = lax.all_to_all(back, "dp", split_axis=0, concat_axis=0, tiled=True)
    gram, _ = lax.optimization_barrier((gram, back))
    own, inverse = own_of(weights, scaled, got, gram, nodes)
    spread = sum_small(spread, "dp", n_dp, [inverse])
    if n_mp > 1:
        spread = lax.psum(spread, "mp")
    gy = grad_y_of(own, y, send_rows, returned, inverse, spread, nodes, scale)
    if n_mp > 1:
        gy = lax.all_gather(gy, "mp", axis=0, tiled=True)

    packable = n_dp & (n_dp - 1) == 0 and n_dp > 1 and din == units and din % (16 * n_dp) == 0
    if packable:
        kept, given = backward(features, hidden, slope, gy, w_out, me, n_dp)
        return tuple(unpack(reduce_packed(kept, given, "dp", n_dp), me, n_dp, width))
    return lax.psum(tuple(backward(features, hidden, slope, gy, w_out, me, None)), "dp")


def solution(mesh):
    return jax.shard_map(
        shards,
        mesh=mesh,
        in_specs=(
            P("dp", None),
            P(None, "mp"),
            P("mp", None),
            P(("dp", "mp")),
            P(("dp", "mp"), None),
            P(("dp", "mp"), None),
            P(("dp", "mp"), None),
        ),
        out_specs=(P(None, "mp"), P("mp", None)),
        check_vma=False,
    )
```

time: 1130 us -> 222 us (0.20)
  other arithmetic: 442 us -> 3.54 us
  local copies, waits for them, and re-layouts: 250 us -> 7.81 us
  waiting for transfers between devices: 272 us -> 47.8 us
  matrix products: 134 us -> 0 us
  Pallas kernels: 0 us -> 116 us
  starting transfers between devices: 11.6 us -> 45.7 us
  between operations: 14.7 us -> 0.95 us
    scatter-add x2 -> x0, other arithmetic: 362 us -> none  [the longest x1 348 us: shards(): jax.ops.segment_sum((-weighted).reshape(-1, width), pair_src.reshape(-1),...]
    psum x2 -> x0, waiting for transfers between devices: 268 us -> none  [the longest x1 144 us: shards(): grad_in, grad_out = lax.psum((g_in, g_out), 'dp')]
    gather x2 -> x0, local copies, waits for them, and re-layouts: 225 us -> none  [the longest x1 217 us: shards(): diff = embed[:, None, :] - arrived[pair_src]]
    dot_general x11 -> x0, matrix products: 134 us -> none  [the longest x1 71.9 us: shards(): jnp.dot(weighted.reshape(-1, width).T, diff.reshape(-1, width), precision...]
    pallas_call x0 -> x11, Pallas kernels: none -> 116 us  [the longest x4 31.9 us: weights_of(): pl.pallas_call(functools.partial(weights_kernel, pairs, part == 0), grid=...]
    ppermute x0 -> x28, waiting for transfers between devices: none -> 47.8 us  [exchange(): return lax.ppermute(value, axis, [(i, i ^ mask) for i in range(n)])]
    ppermute x0 -> x28, starting transfers between devices: none -> 32.3 us  [exchange(): return lax.ppermute(value, axis, [(i, i ^ mask) for i in range(n)])]
    reduce_sum x1 -> x0, other arithmetic: 29.2 us -> none  [shards(): own = jnp.sum(weighted, axis=1)]
  transfers between devices with their start and end apart: 4 -> 30, of which waited for: 3 -> 17; matrix products, arithmetic and copies ran while one was open for 11% -> 3% of each run, Pallas kernels for 0% -> 23%
where the time goes in v1:
time: 222 us
  Pallas kernels  116 us (52%)
  waiting for transfers between devices  47.8 us (22%)
  starting transfers between devices  45.7 us (21%)
  local copies, waits for them, and re-layouts  7.81 us (4%)
  other arithmetic  3.54 us (2%)
    ppermute x28, waiting for transfers between devices, exchange(): return lax.ppermute(value, axis, [(i, i ^ mask) for i in range(n)])  47.8 us
    ppermute x28, starting transfers between devices, exchange(): return lax.ppermute(value, axis, [(i, i ^ mask) for i in range(n)])  32.3 us
    pallas_call x4, Pallas kernels, weights_of(): pl.pallas_call(functools.partial(weights_kernel, pairs, part == 0), grid=...  31.9 us
    pallas_call x1, Pallas kernels, backward(): pl.pallas_call(functools.partial(backward_kernel, n), grid=(nodes // tile...  22.2 us
    pallas_call x1, Pallas kernels, own_of(): pl.pallas_call(functools.partial(own_kernel, parts, nodes), grid=(STEPS,)...  19.9 us
    pallas_call x1, Pallas kernels, forward(): pl.pallas_call(forward_kernel, grid=(nodes // tile,), in_specs=[pl.BlockS...  17.5 us
    pallas_call x1, Pallas kernels, grad_y_of(): pl.pallas_call(functools.partial(grad_y_kernel, nodes, scale), grid=(rows...  9.97 us
    all_to_all x1, starting transfers between devices, shards(): got = lax.all_to_all(sent, 'dp', split_axis=0, concat_axis=0, tiled=True)  7.48 us
  transfers between devices with their start and end apart: 30, of which 17 were waited for; matrix products, arithmetic and copies ran while one was open for 3% of the time, Pallas kernels for 23%

profile of v1, /device:TPU:0, one launch (start us, length us, event | category | flops | bytes accessed | tf_op | source)
XLA Modules:
  0.0 221.7 jit_solution(4057843501546325508)
XLA Ops:
  0.6 17.5 %forward.1 = (bf16[4096,1024]{1,0:T(8,128)(2,1)}, f32[4096,1024]{1,0:T(8,128)}, bf16[4096,128]{1,0:T(8,128)(2,1)}) custom-call(bf16[4096,1024]{1,0:T(8,128)(2,1)} %x_ref.3, bf16[1024,1024]{1,0:T(8,128)(2,1)} %w_in_ref.1, bf16[1024,128]{1,0:T(8,128)(2,1)} %w_out_ref.3), custom_call_target="tpu_custom_call" | custom-call | flops 9663676416 | bytes 25165824 | tf_op jit(solution)/shard_map/forward/pallas_call | solution.py:59
  18.1 7.0 %send.1 = (bf16[2048,128]{1,0:T(8,128)(2,1)}, f32[128,128]{1,0:T(8,128)}) custom-call(bf16[4096,128]{1,0:T(8,128)(2,1)} %get-tuple-element.40.refs_2_.y_ref, s32[16,128]{1,0:T(8,128)} %bitcast.12), custom_call_target="tpu_custom_call" | custom-call | flops 2147483648 | bytes 1572864 | tf_op jit(solution)/shard_map/send/pallas_call | solution.py:102
  25.1 7.5 %all-to-all-start = ((bf16[32,64,128]{2,1,0:T(8,128)(2,1)}), bf16[32,64,128]{2,1,0:T(8,128)(2,1)S(1)}, u32[]{:S(2)}, u32[]{:S(2)}) async-start(bf16[32,64,128]{2,1,0:T(8,128)(2,1)} %bitcast.10), calls=%async_computation | async-start | bytes 1048576 | tf_op jit(solution)/shard_map/all_to_all | solution.py:517
  37.1 7.6 %weights.4 = (bf16[1024,2048]{1,0:T(8,128)(2,1)}, f32[1024,128]{1,0:T(8,128)}, f32[144,2048]{1,0:T(8,128)}, f32[128,128]{1,0:T(8,128)}) custom-call(s32[256,256]{1,0:T(8,128)} %reshape.23.refs_0_, f32[256,256]{1,0:T(8,128)} %reshape.24.refs_1_, bf16[4096,128]{1,0:T(8,128)(2,1)} %get-tuple-element.40.refs_2_.y_ref), custom_call_target="tpu_custom_call" | custom-call | flops 1073741824 | bytes 4194304 | tf_op jit(solution)/shard_map/weights/pallas_call | solution.py:168
  44.7 8.1 %weights.5 = (bf16[1024,2048]{1,0:T(8,128)(2,1)}, f32[1024,128]{1,0:T(8,128)}, f32[144,2048]{1,0:T(8,128)}, f32[128,128]{1,0:T(8,128)}) custom-call(s32[256,256]{1,0:T(8,128)} %reshape.23.refs_0_, f32[256,256]{1,0:T(8,128)} %reshape.24.refs_1_, bf16[4096,128]{1,0:T(8,128)(2,1)} %get-tuple-element.40.refs_2_.y_ref, f32[144,2048]{1,0:T(8,128)} %get-tuple-element.42.refs_3_, ...), custom_call_target="tpu_custom_call" | custom-call | flops 1073741824 | bytes 4194304 | tf_op jit(solution)/shard_map/weights/pallas_call | solution.py:168
  56.4 8.1 %weights.6 = (bf16[1024,2048]{1,0:T(8,128)(2,1)}, f32[1024,128]{1,0:T(8,128)}, f32[144,2048]{1,0:T(8,128)}, f32[128,128]{1,0:T(8,128)}) custom-call(s32[256,256]{1,0:T(8,128)} %reshape.23.refs_0_, f32[256,256]{1,0:T(8,128)} %reshape.24.refs_1_, bf16[4096,128]{1,0:T(8,128)(2,1)} %get-tuple-element.40.refs_2_.y_ref, f32[144,2048]{1,0:T(8,128)} %get-tuple-element.45.refs_3_, ...), custom_call_target="tpu_custom_call" | custom-call | flops 1073741824 | bytes 4194304 | tf_op jit(solution)/shard_map/weights/pallas_call | solution.py:168
  69.0 8.1 %weights.7 = (bf16[1024,2048]{1,0:T(8,128)(2,1)}, f32[1024,128]{1,0:T(8,128)}, f32[144,2048]{1,0:T(8,128)}, f32[128,128]{1,0:T(8,128)}) custom-call(s32[256,256]{1,0:T(8,128)} %reshape.23.refs_0_, f32[256,256]{1,0:T(8,128)} %reshape.24.refs_1_, bf16[4096,128]{1,0:T(8,128)(2,1)} %get-tuple-element.40.refs_2_.y_ref, f32[144,2048]{1,0:T(8,128)} %get-tuple-element.48.refs_3_, ...), custom_call_target="tpu_custom_call" | custom-call | flops 1073741824 | bytes 4194304 | tf_op jit(solution)/shard_map/weights/pallas_call | solution.py:168
  78.0 3.3 %back.1 = (bf16[2048,128]{1,0:T(8,128)(2,1)}, f32[128,128]{1,0:T(8,128)}) custom-call(bf16[2048,128]{1,0:T(8,128)(2,1)} %bitcast.7, f32[144,2048]{1,0:T(8,128)} %get-tuple-element.64.sums_ref, f32[128,128]{1,0:T(8,128)} %get-tuple-element.65.square_ref), custom_call_target="tpu_custom_call" | custom-call | flops 134217728 | bytes 1572864 | tf_op jit(solution)/shard_map/back/pallas_call | solution.py:205
  81.3 6.0 %all-to-all-start.1 = ((bf16[32,64,128]{2,1,0:T(8,128)(2,1)}), bf16[32,64,128]{2,1,0:T(8,128)(2,1)S(1)}, u32[]{:S(2)}, u32[]{:S(2)}) async-start(bf16[32,64,128]{2,1,0:T(8,128)(2,1)} %bitcast.11), calls=%async_computation.1 | async-start | bytes 1048576 | tf_op jit(solution)/shard_map/all_to_all | solution.py:529
  87.9 19.9 %own.1 = (f32[4096,128]{1,0:T(8,128)}, f32[128,128]{1,0:T(8,128)}) custom-call(bf16[1024,2048]{1,0:T(8,128)(2,1)} %get-tuple-element.41.refs_0_, bf16[1024,2048]{1,0:T(8,128)(2,1)} %get-tuple-element.44.refs_1_, bf16[1024,2048]{1,0:T(8,128)(2,1)} %get-tuple-element.47.refs_2_, bf16[1024,2048]{1,0:T(8,128)(2,1)} %get-tuple-element.50.refs_3_, ...), custom_call_target="tpu_custom_call" | custom-call | flops 2147483648 | bytes 16777216 | tf_op jit(solution)/shard_map/own/pallas_call | solution.py:267
  107.9 2.6 %collective-permute-start.10 = (f32[128,128]{1,0:T(8,128)S(1)}, f32[128,128]{1,0:T(8,128)S(1)}, u32[]{:S(2)}, u32[]{:S(2)}) collective-permute-start(f32[128,128]{1,0:T(8,128)S(1)} %add.70), channel_id=1, source_target_pairs={{0,6},{1,7},{2,4},{3,5},{4,2},{5,3},{6,0},{7,1},{8,14},{9,15},{10,... | collective-permute-start | bytes 196616 | tf_op jit(solution)/shard_map/ppermute | solution.py:466
  115.3 3.4 %collective-permute-start.13 = (f32[128,128]{1,0:T(8,128)S(1)}, f32[128,128]{1,0:T(8,128)S(1)}, u32[]{:S(2)}, u32[]{:S(2)}) collective-permute-start(f32[128,128]{1,0:T(8,128)S(1)} %add_add_fusion.1), channel_id=1, source_target_pairs={{0,24},{1,25},{2,26},{3,27},{4,28},{5,29},{6,30},{7,31},{8,16},{9,... | collective-permute-start | bytes 196616 | tf_op jit(solution)/shard_map/ppermute | solution.py:466
  125.6 10.0 %grad_y.1.gy_ref = bf16[4096,128]{1,0:T(8,128)(2,1)} custom-call(f32[4096,128]{1,0:T(8,128)} %get-tuple-element.68.own_ref, bf16[4096,128]{1,0:T(8,128)(2,1)} %get-tuple-element.40.refs_2_.y_ref, s32[1,2048]{1,0:T(1,128)} %bitcast.13, bf16[2048,128]{1,0:T(8,128)(2,1)} %bitcast.9, f32[128,128]{1,0:T(8,128)} %get-tuple-element.69.inverse_ref, ...), custom_call_target="tpu_custom_call" | custom-call | flops 2147483648 | bytes 4194304 | tf_op jit(solution)/shard_map/grad_y/pallas_call | solution.py:325
  135.5 22.2 %backward.1 = (f32[512,1152]{1,0:T(8,128)}, bf16[512,1152]{1,0:T(8,128)(2,1)}) custom-call(bf16[4096,1024]{1,0:T(8,128)(2,1)} %x_ref.3, bf16[4096,1024]{1,0:T(8,128)(2,1)} %get-tuple-element.38.hidden_ref, f32[4096,1024]{1,0:T(8,128)} %get-tuple-element.39.slope_ref, bf16[4096,128]{1,0:T(8,128)(2,1)} %grad_y.1.gy_ref, bf16[1024,128]{1,0:T(8,128)(2,1)} %w_out_ref.3, ...), custom_call_target="tpu_custom_call" | custom-call | flops 10737418240 | bytes 25165824 | tf_op jit(solution)/shard_map/backward/pallas_call | solution.py:407
  157.7 3.1 %collective-permute-done.14 = bf16[512,1152]{1,0:T(8,128)(2,1)S(1)} collective-permute-done((bf16[512,1152]{1,0:T(8,128)(2,1)}, bf16[512,1152]{1,0:T(8,128)(2,1)S(1)}, u32[]{:S(2)}, u32[]{:S(2)}) %collective-permute-start.14) | collective-permute-done | bytes 1179680 | tf_op jit(solution)/shard_map/ppermute | solution.py:466
  166.3 7.3 %collective-permute-done.17 = bf16[128,1152]{1,0:T(8,128)(2,1)S(1)} collective-permute-done((bf16[128,1152]{1,0:T(8,128)(2,1)S(1)}, bf16[128,1152]{1,0:T(8,128)(2,1)S(1)}, u32[]{:S(2)}, u32[]{:S(2)}) %collective-permute-start.17) | collective-permute-done | bytes 294944 | tf_op jit(solution)/shard_map/ppermute | solution.py:466
  173.6 5.5 %collective-permute-done.16 = bf16[128,1152]{1,0:T(8,128)(2,1)S(1)} collective-permute-done((bf16[128,1152]{1,0:T(8,128)(2,1)S(1)}, bf16[128,1152]{1,0:T(8,128)(2,1)S(1)}, u32[]{:S(2)}, u32[]{:S(2)}) %collective-permute-start.16) | collective-permute-done | bytes 294944 | tf_op jit(solution)/shard_map/ppermute | solution.py:466
  179.5 2.7 %collective-permute-start.20 = (bf16[32,1152]{1,0:T(8,128)(2,1)S(1)}, bf16[32,1152]{1,0:T(8,128)(2,1)S(1)}, u32[]{:S(2)}, u32[]{:S(2)}) collective-permute-start(bf16[32,1152]{1,0:T(8,128)(2,1)S(1)} %get-tuple-element.90), channel_id=1, source_target_pairs={{0,24},{1,25},{2,26},{3,27},{4,28},{5,29},{6,30},{7,31},{8,16},{9,... | collective-permute-start | bytes 221192 | tf_op jit(solution)/shard_map/ppermute | solution.py:466
  189.1 2.8 %collective-permute-start.22 = (bf16[32,1152]{1,0:T(8,128)(2,1)S(1)}, bf16[32,1152]{1,0:T(8,128)(2,1)S(1)}, u32[]{:S(2)}, u32[]{:S(2)}) collective-permute-start(bf16[32,1152]{1,0:T(8,128)(2,1)S(1)} %get-tuple-element.75), channel_id=1, source_target_pairs={{0,16},{1,17},{2,18},{3,19},{4,20},{5,21},{6,22},{7,23},{8,24},{9,... | collective-permute-start | bytes 221192 | tf_op jit(solution)/shard_map/ppermute | solution.py:466
  194.1 3.3 %collective-permute-done.22 = bf16[32,1152]{1,0:T(8,128)(2,1)S(1)} collective-permute-done((bf16[32,1152]{1,0:T(8,128)(2,1)S(1)}, bf16[32,1152]{1,0:T(8,128)(2,1)S(1)}, u32[]{:S(2)}, u32[]{:S(2)}) %collective-permute-start.22) | collective-permute-done | bytes 73760 | tf_op jit(solution)/shard_map/ppermute | solution.py:466
  201.8 6.4 %collective-permute-done.24 = bf16[128,1152]{1,0:T(8,128)(2,1)S(1)} collective-permute-done((bf16[128,1152]{1,0:T(8,128)(2,1)S(1)}, bf16[128,1152]{1,0:T(8,128)(2,1)S(1)}, u32[]{:S(2)}, u32[]{:S(2)}) %collective-permute-start.24) | collective-permute-done | bytes 294944 | tf_op jit(solution)/shard_map/ppermute | solution.py:466
  208.3 4.5 %collective-permute-done.25 = bf16[128,1152]{1,0:T(8,128)(2,1)S(1)} collective-permute-done((bf16[128,1152]{1,0:T(8,128)(2,1)S(1)}, bf16[128,1152]{1,0:T(8,128)(2,1)S(1)}, u32[]{:S(2)}, u32[]{:S(2)}) %collective-permute-start.25) | collective-permute-done | bytes 294944 | tf_op jit(solution)/shard_map/ppermute | solution.py:466
  213.0 2.8 %collective-permute-done.27 = bf16[512,1152]{1,0:T(8,128)(2,1)S(1)} collective-permute-done((bf16[512,1152]{1,0:T(8,128)(2,1)S(1)}, bf16[512,1152]{1,0:T(8,128)(2,1)S(1)}, u32[]{:S(2)}, u32[]{:S(2)}) %collective-permute-start.27) | collective-permute-done | bytes 1179680 | tf_op jit(solution)/shard_map/ppermute | solution.py:466
  217.4 4.2 %unpack.1 = (f32[1024,1024]{1,0:T(8,128)}, f32[1024,128]{1,0:T(8,128)}) custom-call(bf16[1024,1152]{1,0:T(8,128)(2,1)} %copy-done.1, s32[1]{0:T(128)} %bitcast.6.me_ref), custom_call_target="tpu_custom_call" | custom-call | flops 1179648 | bytes 7077888 | tf_op jit(solution)/shard_map/unpack/pallas_call | solution.py:444
  (88 shorter events, 46.9 us)
Async XLA Ops:
  25.1 52.0 %all-to-all-start = ((bf16[32,64,128]{2,1,0:T(8,128)(2,1)}), bf16[32,64,128]{2,1,0:T(8,128)(2,1)S(1)}, u32[]{:S(2)}, u32[]{:S(2)}) async-start(bf16[32,64,128]{2,1,0:T(8,128)(2,1)} %bitcast.10), calls=%async_computation | async-start | bytes 1048576 | tf_op jit(solution)/shard_map/all_to_all | solution.py:517
  32.6 20.2 %collective-permute-start = (f32[128,128]{1,0:T(8,128)}, f32[128,128]{1,0:T(8,128)S(1)}, u32[]{:S(2)}, u32[]{:S(2)}) collective-permute-start(f32[128,128]{1,0:T(8,128)} %get-tuple-element.56), channel_id=1, source_target_pairs={{0,1},{1,0},{2,3},{3,2},{4,5},{5,4},{6,7},{7,6},{8,9},{9,8},{10,11... | collective-permute-start | bytes 196616 | tf_op jit(solution)/shard_map/ppermute | solution.py:466
  52.9 11.6 %collective-permute-start.1 = (f32[128,128]{1,0:T(8,128)S(1)}, f32[128,128]{1,0:T(8,128)S(1)}, u32[]{:S(2)}, u32[]{:S(2)}) collective-permute-start(f32[128,128]{1,0:T(8,128)S(1)} %add.63), channel_id=1, source_target_pairs={{0,2},{1,3},{2,0},{3,1},{4,6},{5,7},{6,4},{7,5},{8,10},{9,11},{10,... | collective-permute-start | bytes 196616 | tf_op jit(solution)/shard_map/ppermute | solution.py:466
  54.6 9.9 %collective-permute-start.2 = (f32[128,128]{1,0:T(8,128)S(1)}, f32[128,128]{1,0:T(8,128)S(1)}, u32[]{:S(2)}, u32[]{:S(2)}) collective-permute-start(f32[128,128]{1,0:T(8,128)S(1)} %add.63), channel_id=1, source_target_pairs={{0,4},{1,5},{2,6},{3,7},{4,0},{5,1},{6,2},{7,3},{8,12},{9,13},{10,... | collective-permute-start | bytes 196616 | tf_op jit(solution)/shard_map/ppermute | solution.py:466
  56.1 8.5 %collective-permute-start.3 = (f32[128,128]{1,0:T(8,128)S(1)}, f32[128,128]{1,0:T(8,128)S(1)}, u32[]{:S(2)}, u32[]{:S(2)}) collective-permute-start(f32[128,128]{1,0:T(8,128)S(1)} %add.63), channel_id=1, source_target_pairs={{0,6},{1,7},{2,4},{3,5},{4,2},{5,3},{6,0},{7,1},{8,14},{9,15},{10,... | collective-permute-start | bytes 196616 | tf_op jit(solution)/shard_map/ppermute | solution.py:466
  64.5 12.6 %collective-permute-start.4 = (f32[128,128]{1,0:T(8,128)S(1)}, f32[128,128]{1,0:T(8,128)S(1)}, u32[]{:S(2)}, u32[]{:S(2)}) collective-permute-start(f32[128,128]{1,0:T(8,128)S(1)} %add_add_fusion.3), channel_id=1, source_target_pairs={{0,8},{1,9},{2,10},{3,11},{4,12},{5,13},{6,14},{7,15},{8,0},{9,1},... | collective-permute-start | bytes 196616 | tf_op jit(solution)/shard_map/ppermute | solution.py:466
  66.3 10.8 %collective-permute-start.5 = (f32[128,128]{1,0:T(8,128)S(1)}, f32[128,128]{1,0:T(8,128)S(1)}, u32[]{:S(2)}, u32[]{:S(2)}) collective-permute-start(f32[128,128]{1,0:T(8,128)S(1)} %add_add_fusion.3), channel_id=1, source_target_pairs={{0,16},{1,17},{2,18},{3,19},{4,20},{5,21},{6,22},{7,23},{8,24},{9,... | collective-permute-start | bytes 196616 | tf_op jit(solution)/shard_map/ppermute | solution.py:466
  68.7 8.4 %collective-permute-start.6 = (f32[128,128]{1,0:T(8,128)S(1)}, f32[128,128]{1,0:T(8,128)S(1)}, u32[]{:S(2)}, u32[]{:S(2)}) collective-permute-start(f32[128,128]{1,0:T(8,128)S(1)} %add_add_fusion.3), channel_id=1, source_target_pairs={{0,24},{1,25},{2,26},{3,27},{4,28},{5,29},{6,30},{7,31},{8,16},{9,... | collective-permute-start | bytes 196616 | tf_op jit(solution)/shard_map/ppermute | solution.py:466
  81.3 43.5 %all-to-all-start.1 = ((bf16[32,64,128]{2,1,0:T(8,128)(2,1)}), bf16[32,64,128]{2,1,0:T(8,128)(2,1)S(1)}, u32[]{:S(2)}, u32[]{:S(2)}) async-start(bf16[32,64,128]{2,1,0:T(8,128)(2,1)} %bitcast.11), calls=%async_computation.1 | async-start | bytes 1048576 | tf_op jit(solution)/shard_map/all_to_all | solution.py:529
  87.9 19.9 %collective-permute-start.7 = (f32[128,128]{1,0:T(8,128)}, f32[128,128]{1,0:T(8,128)S(1)}, u32[]{:S(2)}, u32[]{:S(2)}) collective-permute-start(f32[128,128]{1,0:T(8,128)} %get-tuple-element.70), channel_id=1, source_target_pairs={{0,1},{1,0},{2,3},{3,2},{4,5},{5,4},{6,7},{7,6},{8,9},{9,8},{10,11... | collective-permute-start | bytes 196616 | tf_op jit(solution)/shard_map/ppermute | solution.py:466
  107.9 5.5 %collective-permute-start.10 = (f32[128,128]{1,0:T(8,128)S(1)}, f32[128,128]{1,0:T(8,128)S(1)}, u32[]{:S(2)}, u32[]{:S(2)}) collective-permute-start(f32[128,128]{1,0:T(8,128)S(1)} %add.70), channel_id=1, source_target_pairs={{0,6},{1,7},{2,4},{3,5},{4,2},{5,3},{6,0},{7,1},{8,14},{9,15},{10,... | collective-permute-start | bytes 196616 | tf_op jit(solution)/shard_map/ppermute | solution.py:466
  115.3 6.1 %collective-permute-start.13 = (f32[128,128]{1,0:T(8,128)S(1)}, f32[128,128]{1,0:T(8,128)S(1)}, u32[]{:S(2)}, u32[]{:S(2)}) collective-permute-start(f32[128,128]{1,0:T(8,128)S(1)} %add_add_fusion.1), channel_id=1, source_target_pairs={{0,24},{1,25},{2,26},{3,27},{4,28},{5,29},{6,30},{7,31},{8,16},{9,... | collective-permute-start | bytes 196616 | tf_op jit(solution)/shard_map/ppermute | solution.py:466
  118.8 5.4 %collective-permute-start.11 = (f32[128,128]{1,0:T(8,128)S(1)}, f32[128,128]{1,0:T(8,128)S(1)}, u32[]{:S(2)}, u32[]{:S(2)}) collective-permute-start(f32[128,128]{1,0:T(8,128)S(1)} %add_add_fusion.1), channel_id=1, source_target_pairs={{0,8},{1,9},{2,10},{3,11},{4,12},{5,13},{6,14},{7,15},{8,0},{9,1},... | collective-permute-start | bytes 196616 | tf_op jit(solution)/shard_map/ppermute | solution.py:466
  162.8 10.9 %collective-permute-start.17 = (bf16[128,1152]{1,0:T(8,128)(2,1)S(1)}, bf16[128,1152]{1,0:T(8,128)(2,1)S(1)}, u32[]{:S(2)}, u32[]{:S(2)}) collective-permute-start(bf16[128,1152]{1,0:T(8,128)(2,1)S(1)} %get-tuple-element.81), channel_id=1, source_target_pairs={{0,6},{1,7},{2,4},{3,5},{4,2},{5,3},{6,0},{7,1},{8,14},{9,15},{10,... | collective-permute-start | bytes 884744 | tf_op jit(solution)/shard_map/ppermute | solution.py:466
  164.4 14.8 %collective-permute-start.16 = (bf16[128,1152]{1,0:T(8,128)(2,1)S(1)}, bf16[128,1152]{1,0:T(8,128)(2,1)S(1)}, u32[]{:S(2)}, u32[]{:S(2)}) collective-permute-start(bf16[128,1152]{1,0:T(8,128)(2,1)S(1)} %get-tuple-element.82), channel_id=1, source_target_pairs={{0,4},{1,5},{2,6},{3,7},{4,0},{5,1},{6,2},{7,3},{8,12},{9,13},{10,... | collective-permute-start | bytes 884744 | tf_op jit(solution)/shard_map/ppermute | solution.py:466
  165.9 13.4 %collective-permute-start.15 = (bf16[128,1152]{1,0:T(8,128)(2,1)S(1)}, bf16[128,1152]{1,0:T(8,128)(2,1)S(1)}, u32[]{:S(2)}, u32[]{:S(2)}) collective-permute-start(bf16[128,1152]{1,0:T(8,128)(2,1)S(1)} %get-tuple-element.80), channel_id=1, source_target_pairs={{0,2},{1,3},{2,0},{3,1},{4,6},{5,7},{6,4},{7,5},{8,10},{9,11},{10,... | collective-permute-start | bytes 884744 | tf_op jit(solution)/shard_map/ppermute | solution.py:466
  179.5 6.9 %collective-permute-start.20 = (bf16[32,1152]{1,0:T(8,128)(2,1)S(1)}, bf16[32,1152]{1,0:T(8,128)(2,1)S(1)}, u32[]{:S(2)}, u32[]{:S(2)}) collective-permute-start(bf16[32,1152]{1,0:T(8,128)(2,1)S(1)} %get-tuple-element.90), channel_id=1, source_target_pairs={{0,24},{1,25},{2,26},{3,27},{4,28},{5,29},{6,30},{7,31},{8,16},{9,... | collective-permute-start | bytes 221192 | tf_op jit(solution)/shard_map/ppermute | solution.py:466
  182.1 6.8 %collective-permute-start.19 = (bf16[32,1152]{1,0:T(8,128)(2,1)S(1)}, bf16[32,1152]{1,0:T(8,128)(2,1)S(1)}, u32[]{:S(2)}, u32[]{:S(2)}) collective-permute-start(bf16[32,1152]{1,0:T(8,128)(2,1)S(1)} %get-tuple-element.91), channel_id=1, source_target_pairs={{0,16},{1,17},{2,18},{3,19},{4,20},{5,21},{6,22},{7,23},{8,24},{9,... | collective-permute-start | bytes 221192 | tf_op jit(solution)/shard_map/ppermute | solution.py:466
  182.1 6.8 %collective-permute-start.18 = (bf16[32,1152]{1,0:T(8,128)(2,1)S(1)}, bf16[32,1152]{1,0:T(8,128)(2,1)S(1)}, u32[]{:S(2)}, u32[]{:S(2)}) collective-permute-start(bf16[32,1152]{1,0:T(8,128)(2,1)S(1)} %get-tuple-element.89), channel_id=1, source_target_pairs={{0,8},{1,9},{2,10},{3,11},{4,12},{5,13},{6,14},{7,15},{8,0},{9,1},... | collective-permute-start | bytes 221192 | tf_op jit(solution)/shard_map/ppermute | solution.py:466
  189.1 8.3 %collective-permute-start.22 = (bf16[32,1152]{1,0:T(8,128)(2,1)S(1)}, bf16[32,1152]{1,0:T(8,128)(2,1)S(1)}, u32[]{:S(2)}, u32[]{:S(2)}) collective-permute-start(bf16[32,1152]{1,0:T(8,128)(2,1)S(1)} %get-tuple-element.75), channel_id=1, source_target_pairs={{0,16},{1,17},{2,18},{3,19},{4,20},{5,21},{6,22},{7,23},{8,24},{9,... | collective-permute-start | bytes 221192 | tf_op jit(solution)/shard_map/ppermute | solution.py:466
  191.9 6.3 %collective-permute-start.23 = (bf16[32,1152]{1,0:T(8,128)(2,1)S(1)}, bf16[32,1152]{1,0:T(8,128)(2,1)S(1)}, u32[]{:S(2)}, u32[]{:S(2)}) collective-permute-start(bf16[32,1152]{1,0:T(8,128)(2,1)S(1)} %get-tuple-element.75), channel_id=1, source_target_pairs={{0,24},{1,25},{2,26},{3,27},{4,28},{5,29},{6,30},{7,31},{8,16},{9,... | collective-permute-start | bytes 221192 | tf_op jit(solution)/shard_map/ppermute | solution.py:466
  198.2 10.0 %collective-permute-start.24 = (bf16[128,1152]{1,0:T(8,128)(2,1)S(1)}, bf16[128,1152]{1,0:T(8,128)(2,1)S(1)}, u32[]{:S(2)}, u32[]{:S(2)}) collective-permute-start(bf16[128,1152]{1,0:T(8,128)(2,1)S(1)} %pad_maximum_fusion), channel_id=1, source_target_pairs={{0,2},{1,3},{2,0},{3,1},{4,6},{5,7},{6,4},{7,5},{8,10},{9,11},{10,... | collective-permute-start | bytes 884744 | tf_op jit(solution)/shard_map/ppermute | solution.py:466
  199.9 12.9 %collective-permute-start.25 = (bf16[128,1152]{1,0:T(8,128)(2,1)S(1)}, bf16[128,1152]{1,0:T(8,128)(2,1)S(1)}, u32[]{:S(2)}, u32[]{:S(2)}) collective-permute-start(bf16[128,1152]{1,0:T(8,128)(2,1)S(1)} %pad_maximum_fusion), channel_id=1, source_target_pairs={{0,4},{1,5},{2,6},{3,7},{4,0},{5,1},{6,2},{7,3},{8,12},{9,13},{10,... | collective-permute-start | bytes 884744 | tf_op jit(solution)/shard_map/ppermute | solution.py:466
  200.3 12.6 %collective-permute-start.26 = (bf16[128,1152]{1,0:T(8,128)(2,1)S(1)}, bf16[128,1152]{1,0:T(8,128)(2,1)S(1)}, u32[]{:S(2)}, u32[]{:S(2)}) collective-permute-start(bf16[128,1152]{1,0:T(8,128)(2,1)S(1)} %pad_maximum_fusion), channel_id=1, source_target_pairs={{0,6},{1,7},{2,4},{3,5},{4,2},{5,3},{6,0},{7,1},{8,14},{9,15},{10,... | collective-permute-start | bytes 884744 | tf_op jit(solution)/shard_map/ppermute | solution.py:466
  (14 other events, 100.0 us)

commit v2 on v1

v2 whole, which is shorter than its diff:
```python
import functools
import math

import jax
import jax.numpy as jnp
from jax import lax
from jax.experimental import pallas as pl
from jax.experimental.pallas import tpu as pltpu
from jax.sharding import PartitionSpec as P

F32 = jnp.float32
BF16 = jnp.bfloat16
LANES = 128
STEPS = 8
SHIFT = 0.3
VMEM_BYTES = 56 * 1024 * 1024


def params(steps=1):
    return pltpu.CompilerParams(
        dimension_semantics=("arbitrary",) * steps, vmem_limit_bytes=VMEM_BYTES
    )


def cost(flops, read):
    return pl.CostEstimate(flops=int(flops), bytes_accessed=int(read), transcendentals=0)


def dot_tn(a, b):
    return lax.dot_general(a, b, (((0,), (0,)), ((), ())), preferred_element_type=F32)


def dot_nt(a, b):
    return lax.dot_general(a, b, (((1,), (1,)), ((), ())), preferred_element_type=F32)


def dot(a, b):
    return jnp.dot(a, b, preferred_element_type=F32)


def forward_kernel(x_ref, w_in_ref, w_out_ref, hidden_ref, slope_ref, y_ref, round_ref, gram_ref):
    units = w_in_ref.shape[1]
    step = min(512, units)
    x = x_ref[...]
    for at in range(0, units, step):
        pre = dot(x, w_in_ref[:, at:at + step])
        sig = jax.nn.sigmoid(pre)
        act = pre * sig
        hidden_ref[:, at:at + step] = act.astype(BF16)
        slope_ref[:, at:at + step] = sig + act * (1.0 - sig)
    y = dot(hidden_ref[...], w_out_ref[...])
    y_ref[...] = y
    y = y.astype(BF16)
    round_ref[...] = y

    @pl.when(pl.program_id(0) == 0)
    def _():
        gram_ref[...] = jnp.zeros_like(gram_ref)

    gram_ref[...] += dot_tn(y, y)


def forward(features, w_in, w_out):
    nodes, din = features.shape
    units = w_in.shape[1]
    width = w_out.shape[1]
    tile = min(1024, nodes)
    return pl.pallas_call(
        forward_kernel,
        grid=(nodes // tile,),
        in_specs=[
            pl.BlockSpec((tile, din), lambda i: (i, 0)),
            pl.BlockSpec((din, units), lambda i: (0, 0)),
            pl.BlockSpec((units, width), lambda i: (0, 0)),
        ],
        out_specs=[
            pl.BlockSpec((tile, units), lambda i: (i, 0)),
            pl.BlockSpec((tile, units), lambda i: (i, 0)),
            pl.BlockSpec((tile, width), lambda i: (i, 0)),
            pl.BlockSpec((tile, width), lambda i: (i, 0)),
            pl.BlockSpec((width, width), lambda i: (0, 0)),
        ],
        out_shape=[
            jax.ShapeDtypeStruct((nodes, units), BF16),
            jax.ShapeDtypeStruct((nodes, units), F32),
            jax.ShapeDtypeStruct((nodes, width), F32),
            jax.ShapeDtypeStruct((nodes, width), BF16),
            jax.ShapeDtypeStruct((width, width), F32),
        ],
        compiler_params=params(),
        cost_estimate=cost(2 * nodes * units * (din + width), 2 * nodes * (din + 2 * units)),
        name="forward",
    )(features, w_in, w_out)


def send_kernel(index_ref, y_ref, sent_ref, rows_ref):
    some = 16

    @pl.loop(0, sent_ref.shape[0] // some)
    def _(step):
        at = pl.multiple_of(step * some, some)
        for k in range(some):
            rows_ref[pl.ds(at + k, 1), :] = y_ref[pl.ds(index_ref[at + k], 1), :]

    sent_ref[...] = rows_ref[...].astype(BF16)


def send(y, send_rows):
    rows, width = y.shape
    count = send_rows.shape[0]
    return pl.pallas_call(
        send_kernel,
        in_specs=[
            pl.BlockSpec(memory_space=pltpu.SMEM),
            pl.BlockSpec(memory_space=pltpu.VMEM),
        ],
        out_shape=jax.ShapeDtypeStruct((count, width), BF16),
        scratch_shapes=[pltpu.VMEM((count, width), F32)],
        compiler_params=pltpu.CompilerParams(vmem_limit_bytes=VMEM_BYTES),
        cost_estimate=cost(2 * rows * count * width, 2 * width * (rows + count)),
        name="send",
    )(send_rows, y)


def weights_kernel(pairs, first, *refs):
    if first:
        src_ref, coef_ref, y_ref, round_ref, weights_ref, scaled_ref, back_ref, square_ref = refs
    else:
        src_ref, coef_ref, y_ref, round_ref, back_in, square_in = refs[:6]
        weights_ref, scaled_ref, back_ref, square_ref = refs[6:]
    groups, per = src_ref.shape
    count = weights_ref.shape[1]
    members = per // pairs
    high = count // LANES
    held = BF16 if high * members <= 256 else F32

    @pl.when(pl.program_id(0) == 0)
    def _():
        if first:
            back_ref[...] = jnp.zeros_like(back_ref)
            square_ref[...] = jnp.zeros_like(square_ref)
        else:
            back_ref[...] = back_in[...]
            square_ref[...] = square_in[...]

    member = lax.broadcasted_iota(jnp.int32, (1, per), 1) // pairs
    row = lax.broadcasted_iota(jnp.int32, (high * members, per), 0).astype(F32).astype(held)
    lane = lax.broadcasted_iota(jnp.int32, (LANES, per), 0).astype(F32).astype(held)
    src = src_ref[...]
    target = ((src // LANES) * members + member).astype(F32).astype(held)
    low = (src % LANES).astype(F32).astype(held)
    coef = coef_ref[...].astype(BF16).astype(held)
    zero, one = jnp.zeros((), held), jnp.ones((), held)
    for g in range(groups):
        left = jnp.where(row == target[g:g + 1, :], coef[g:g + 1, :], zero).astype(BF16)
        right = jnp.where(lane == low[g:g + 1, :], one, zero).astype(BF16)
        part = dot_nt(left, right).astype(BF16)
        sums = None
        at = slice(g * members, (g + 1) * members)
        for h in range(high):
            piece = part[h * members:(h + 1) * members, :]
            weights_ref[at, h * LANES:(h + 1) * LANES] = piece
            sums = piece.astype(F32) if sums is None else sums + piece.astype(F32)
        scaled_ref[at, :] = jnp.sum(sums, axis=1, keepdims=True) * y_ref[at, :]
    y = round_ref[...]
    left = jnp.concatenate([y.astype(F32).T.astype(BF16), jnp.ones((16, y.shape[0]), BF16)], axis=0)
    back_ref[...] += dot(left, weights_ref[...])
    square_ref[...] += dot_tn(y, scaled_ref[...].astype(BF16))


def weights_of(src, coef, y, rounded, carry, pairs, count, part, parts):
    rows, width = y.shape[0] // parts, y.shape[1]
    per = src.shape[1]
    members = per // pairs
    groups = min(32, src.shape[0] // parts)
    tile = groups * members
    skip = part * (rows // tile)
    sums = [
        jax.ShapeDtypeStruct((width + 16, count), F32),
        jax.ShapeDtypeStruct((width, width), F32),
    ]
    sum_specs = [pl.BlockSpec(x.shape, lambda i: (0, 0)) for x in sums]
    return pl.pallas_call(
        functools.partial(weights_kernel, pairs, part == 0),
        grid=(rows // tile,),
        in_specs=[
            pl.BlockSpec((groups, per), lambda i: (i + skip, 0)),
            pl.BlockSpec((groups, per), lambda i: (i + skip, 0)),
            pl.BlockSpec((tile, width), lambda i: (i + skip, 0)),
            pl.BlockSpec((tile, width), lambda i: (i + skip, 0)),
        ]
        + (sum_specs if part else []),
        out_specs=[
            pl.BlockSpec((tile, count), lambda i: (i, 0)),
            pl.BlockSpec((tile, width), lambda i: (i, 0)),
        ]
        + sum_specs,
        out_shape=[
            jax.ShapeDtypeStruct((rows, count), BF16),
            jax.ShapeDtypeStruct((rows, width), F32),
        ]
        + sums,
        compiler_params=params(),
        cost_estimate=cost(4 * rows * count * width, 2 * rows * count),
        name="weights",
    )(src, coef, y, rounded, *carry)


def back_kernel(shift, got_ref, sums_ref, square_ref, back_ref, spread_ref):
    width = got_ref.shape[1]
    got = got_ref[...]
    sums = sums_ref[...].T
    back = ((sums[:, width:width + 1] - shift) * got.astype(F32) - sums[:, :width]).astype(BF16)
    back_ref[...] = back
    cross = dot(sums_ref[:width, :].astype(BF16), got)
    spread_ref[...] = square_ref[...] - cross + dot_tn(got, back) + shift * dot_tn(got, got)


def back_of(got, sums, square, shift):
    count, width = got.shape
    return pl.pallas_call(
        functools.partial(back_kernel, shift),
        out_shape=[
            jax.ShapeDtypeStruct((count, width), BF16),
            jax.ShapeDtypeStruct((width, width), F32),
        ],
        compiler_params=pltpu.CompilerParams(vmem_limit_bytes=VMEM_BYTES),
        cost_estimate=cost(4 * count * width * width, 6 * count * width),
        name="back",
    )(got, sums, square)


def own_kernel(nodes, part, count, weights_ref, scaled_ref, got_ref, matrix_ref, own_ref, inverse_ref):
    width = inverse_ref.shape[0]
    each = width // STEPS

    @pl.when(pl.program_id(0) == 0)
    def _():
        matrix = matrix_ref[...]
        inverse_ref[...] = matrix * (1.0 / nodes) if part == 0 else matrix

    for step in range(count):

        @pl.when(pl.program_id(0) == step)
        def _():
            own_ref[...] = scaled_ref[...] - dot(weights_ref[...], got_ref[...])
            start = (part * count + step) * each
            inverse_ref[...] = eliminate(inverse_ref[...], start, each)


def eliminate(matrix, start, count, some=4):
    rows = lax.broadcasted_iota(jnp.int32, matrix.shape, 0)
    lanes = lax.broadcasted_iota(jnp.int32, matrix.shape, 1)
    for first in range(start, start + count, some):
        columns = [
            jnp.broadcast_to(matrix[:, k:k + 1], matrix.shape) for k in range(first, first + some)
        ]
        for at, k in enumerate(range(first, first + some)):
            here, column = rows == k, columns[at]
            pivot = 1.0 / column[k:k + 1, :]
            scaled = jnp.where(lanes[:1] == k, pivot, matrix[k:k + 1, :] * pivot)
            rest = jnp.where(lanes == k, 0.0, matrix) - column * scaled
            matrix = jnp.where(here, scaled, rest)
            for later in range(at + 1, some):
                value = columns[later][k:k + 1, :] * pivot
                columns[later] = jnp.where(here, value, columns[later] - column * value)
    return matrix


def own_of(weights, scaled, got, matrix, nodes, part, parts, skip, rows):
    count, width = got.shape
    steps = STEPS // parts
    tile = rows // steps
    return pl.pallas_call(
        functools.partial(own_kernel, nodes, part, steps),
        grid=(steps,),
        in_specs=[
            pl.BlockSpec((tile, count), lambda i: (i + skip // tile, 0)),
            pl.BlockSpec((tile, width), lambda i: (i + skip // tile, 0)),
            pl.BlockSpec((count, width), lambda i: (0, 0)),
            pl.BlockSpec((width, width), lambda i: (0, 0)),
        ],
        out_specs=[
            pl.BlockSpec((tile, width), lambda i: (i, 0)),
            pl.BlockSpec((width, width), lambda i: (0, 0)),
        ],
        out_shape=[
            jax.ShapeDtypeStruct((rows, width), F32),
            jax.ShapeDtypeStruct((width, width), F32),
        ],
        compiler_params=params(),
        cost_estimate=cost(2 * rows * count * width, 2 * rows * count),
        name="own",
    )(weights, scaled, got, matrix)


def split(value):
    first = value.astype(BF16)
    return first, (value - first.astype(F32)).astype(BF16)


def grad_y_kernel(
    nodes, scale, shift, parts, *refs
):
    own_refs = refs[:parts]
    y_ref, index_ref, returned_ref, inverse_ref, spread_ref, out_ref, right_ref = refs[parts:]
    tile, width = y_ref.shape
    count = returned_ref.shape[0]
    each = pl.num_programs(0) // parts

    @pl.when(pl.program_id(0) == 0)
    def _():
        high = lax.Precision.HIGHEST
        inverse = inverse_ref[...]
        half = jnp.dot(inverse, spread_ref[...], precision=high, preferred_element_type=F32)
        sandwich = jnp.dot(half, inverse, precision=high, preferred_element_type=F32)
        for at, value in ((0, 2.0 * scale * inverse), (width, -2.0 * scale / nodes * sandwich)):
            first, second = split(value)
            right_ref[at:at + width, :width] = first
            right_ref[at:at + width, width:] = second

    for part, own_ref in enumerate(own_refs):

        @pl.when(pl.program_id(0) // each == part)
        def _():
            at = lax.broadcasted_iota(jnp.int32, (tile, count), 0) + pl.program_id(0) * tile
            spots = jnp.where(at == index_ref[...], 1.0, 0.0)
            times = jnp.sum(spots, axis=1, keepdims=True)
            y = y_ref[...]
            nearby = own_ref[...] + dot(spots.astype(BF16), returned_ref[...]) + shift * times * y
            first, second = split(nearby)
            y_first, y_second = split(y)
            both = dot(jnp.concatenate([first, y_first], axis=1), right_ref[...])
            rest = dot(jnp.concatenate([second, y_second], axis=1), right_ref[:, :width])
            out_ref[...] = (both[:, :width] + both[:, width:] + rest).astype(BF16)


def part_block(tile, width, part, each):
    return pl.BlockSpec((tile, width), lambda i: (jnp.clip(i - part * each, 0, each - 1), 0))


def grad_y_of(own, y, send_rows, returned, inverse, spread, shift, nodes, scale):
    rows, width = y.shape
    count = returned.shape[0]
    parts = len(own)
    tile = min(512, rows // parts)
    each = rows // tile // parts
    return pl.pallas_call(
        functools.partial(grad_y_kernel, nodes, scale, shift, parts),
        grid=(rows // tile,),
        in_specs=[part_block(tile, width, part, each) for part in range(parts)]
        + [
            pl.BlockSpec((tile, width), lambda i: (i, 0)),
            pl.BlockSpec((1, count), lambda i: (0, 0)),
            pl.BlockSpec((count, width), lambda i: (0, 0)),
            pl.BlockSpec((width, width), lambda i: (0, 0)),
            pl.BlockSpec((width, width), lambda i: (0, 0)),
        ],
        out_specs=pl.BlockSpec((tile, width), lambda i: (i, 0)),
        out_shape=jax.ShapeDtypeStruct((rows, width), BF16),
        scratch_shapes=[pltpu.VMEM((2 * width, 2 * width), BF16)],
        compiler_params=params(),
        cost_estimate=cost(2 * rows * count * width, 8 * rows * width),
        name="grad_y",
    )(*own, y, send_rows.reshape(1, count), returned, inverse, spread)


def radices(n):
    result, shift = [], 0
    while 1 << shift < n:
        bits = 1 if shift == 0 else min(2, n.bit_length() - 1 - shift)
        result.append((shift, 1 << bits))
        shift += bits
    return result


def position(relative, n):
    total = 0
    for shift, radix in radices(n):
        total = total * radix + ((relative >> shift) & (radix - 1))
    return total


def backward_kernel(n, last, x_ref, slope_ref, gy_ref, w_out_ref, me_ref, *rest):
    if last:
        hidden_ref, *outs, g_in, g_out = rest
    else:
        *outs, g_in = rest
        g_out = None
    gy = gy_ref[...]
    x = x_ref[...]

    @pl.when(pl.program_id(0) == 0)
    def _():
        g_in[...] = jnp.zeros_like(g_in)
        if last:
            g_out[...] = jnp.zeros_like(g_out)

    units = g_in.shape[1]
    back = dot_nt(gy, w_out_ref[...])
    grad = (back * slope_ref[...]).astype(BF16)
    g_in[...] += dot_tn(x, grad)
    if last:
        g_out[...] += dot_tn(hidden_ref[...], gy)

    @pl.when(pl.program_id(0) == pl.num_programs(0) - 1)
    def _():
        if n is None:
            outs[0][...] = g_in[...]
            if last:
                outs[1][...] = g_out[...]
        else:
            me = me_ref[0]
            chunk = g_in.shape[0] // n
            for pair in range(n // 2):
                for side, out in enumerate(outs):
                    c = 2 * pair + (me + side) % 2
                    at = pl.multiple_of((position(me ^ c, n) % (n // 2)) * chunk, chunk)
                    rows = pl.ds(pl.multiple_of(c * chunk, chunk), chunk)
                    out[pl.ds(at, chunk), :units] = g_in[rows, :].astype(out.dtype)
                    if last:
                        out[pl.ds(at, chunk), units:] = g_out[rows, :].astype(out.dtype)


def backward(features, hidden, slope, gy, w_out, me, n, part, parts):
    nodes, din = features.shape
    all_units, width = w_out.shape
    units = all_units // parts
    last = part == parts - 1
    tile = min(1024, nodes)
    both = units + width if last else units
    if n is None:
        outs = [jax.ShapeDtypeStruct((din, units), F32)]
        outs += [jax.ShapeDtypeStruct((all_units, width), F32)] if last else []
    else:
        outs = [
            jax.ShapeDtypeStruct((din // 2, both), F32),
            jax.ShapeDtypeStruct((din // 2, both), BF16),
        ]
    return pl.pallas_call(
        functools.partial(backward_kernel, n, last),
        grid=(nodes // tile,),
        in_specs=[
            pl.BlockSpec((tile, din), lambda i: (i, 0)),
            pl.BlockSpec((tile, units), lambda i: (i, part)),
            pl.BlockSpec((tile, width), lambda i: (i, 0)),
            pl.BlockSpec((units, width), lambda i: (part, 0)),
            pl.BlockSpec(memory_space=pltpu.SMEM),
        ]
        + ([pl.BlockSpec((tile, all_units), lambda i: (i, 0))] if last else []),
        out_specs=[pl.BlockSpec(o.shape, lambda i: (0, 0)) for o in outs],
        out_shape=outs,
        scratch_shapes=[pltpu.VMEM((din, units), F32)]
        + ([pltpu.VMEM((all_units, width), F32)] if last else []),
        compiler_params=params(),
        cost_estimate=cost(2 * nodes * units * (din + 2 * width), 2 * nodes * (din + 2 * units)),
        name="backward",
    )(features, slope, gy, w_out, me, *([hidden] if last else []))


def unpack_kernel(n, packed_ref, me_ref, g_in_ref, g_out_ref):
    units = g_in_ref.shape[1]
    rows = g_in_ref.shape[0]
    chunk = packed_ref.shape[0] // n
    me = me_ref[0]
    first = pl.program_id(0) * (rows // chunk)
    for c in range(rows // chunk):
        at = pl.multiple_of(position(me ^ (first + c), n) * chunk, chunk)
        part = packed_ref[pl.ds(at, chunk), :].astype(F32)
        g_in_ref[c * chunk:(c + 1) * chunk, :] = part[:, :units]
        g_out_ref[c * chunk:(c + 1) * chunk, :] = part[:, units:]


def unpack(packed, me, n, width):
    din, both = packed.shape
    units = both - width
    tile = din // 4
    return pl.pallas_call(
        functools.partial(unpack_kernel, n),
        grid=(din // tile,),
        in_specs=[
            pl.BlockSpec((din, both), lambda i: (0, 0)),
            pl.BlockSpec(memory_space=pltpu.SMEM),
        ],
        out_specs=[
            pl.BlockSpec((tile, units), lambda i: (i, 0)),
            pl.BlockSpec((tile, width), lambda i: (i, 0)),
        ],
        out_shape=[
            jax.ShapeDtypeStruct((din, units), F32),
            jax.ShapeDtypeStruct((din, width), F32),
        ],
        compiler_params=params(),
        cost_estimate=cost(din * both, 6 * din * both),
        name="unpack",
    )(packed, me)


def exchange(value, axis, n, mask):
    return lax.ppermute(value, axis, [(i, i ^ mask) for i in range(n)])


def sum_step(value, axis, n, step, after=None):
    if step is None:
        return lax.psum(value, axis)
    shift, radix = step
    got = [exchange(value, axis, n, m << shift) for m in range(1, radix)]
    if after is not None:
        got, _ = lax.optimization_barrier((got, after))
    return sum(got, value)


def reduce_step(value, axis, n, step):
    shift, radix = step
    size = value.shape[0] // radix
    total = value[:size]
    for m in range(1, radix):
        part = value[m * size:(m + 1) * size].astype(BF16)
        total = total + exchange(part, axis, n, m << shift).astype(F32)
    return total


def gather_packed(value, axis, n):
    for shift, radix in reversed(radices(n)):
        parts = [value] + [exchange(value, axis, n, m << shift) for m in range(1, radix)]
        value = jnp.concatenate(parts, axis=0)
    return value


def shards(features, w_in, w_out, send_rows, pair_src, pair_weight, pair_mask):
    n_dp = lax.axis_size("dp")
    n_mp = lax.axis_size("mp")
    group_rows, din = features.shape
    nodes = group_rows * n_dp
    rows = group_rows // n_mp
    units, width = w_out.shape
    pairs = pair_src.shape[1]
    count = send_rows.shape[0]
    scale = 1.0 / (pairs * math.sqrt(nodes))
    me = lax.axis_index("dp").astype(jnp.int32).reshape(1)

    per = 256
    src = pair_src.reshape(rows * pairs // per, per)
    coef = (pair_weight * pair_mask.astype(F32)).reshape(rows * pairs // per, per)

    steps = [None] if n_dp & (n_dp - 1) else radices(n_dp)
    hidden, slope, y, rounded, gram = forward(features, w_in, w_out)
    if n_mp > 1:
        y = lax.psum_scatter(y, "mp", scatter_dimension=0, tiled=True)
        rounded = y.astype(BF16)
        gram = lax.psum(dot_tn(rounded, rounded), "mp")
    sent = send(y, send_rows)
    got = lax.all_to_all(sent, "dp", split_axis=0, concat_axis=0, tiled=True)
    parts = 2 if rows % (2 * 512) == 0 else 1
    weights, scaled, carry = [], [], ()
    for part in range(parts):
        if steps:
            gram = sum_step(gram, "dp", n_dp, steps[0], sent if part == 0 else None)
            steps = steps[1:]
            gram, rounded, carry = lax.optimization_barrier((gram, rounded, carry))
        piece, with_y, *carry = weights_of(
            src, coef, y, rounded, carry, pairs, count, part, parts
        )
        weights.append(piece)
        scaled.append(with_y)
    for step in steps:
        gram = sum_step(gram, "dp", n_dp, step, carry[1])
    gram, carry = lax.optimization_barrier((gram, carry))
    shift = SHIFT * pairs * rows / count
    back, spread = back_of(got, *carry, shift)
    returned = lax.all_to_all(back, "dp", split_axis=0, concat_axis=0, tiled=True)
    matrix, _ = lax.optimization_barrier((gram, back))
    own, marks = [], []
    cuts = 4 if rows % (4 * 256) == 0 else 1
    for cut in range(cuts):
        part, skip = divmod(cut * (rows // cuts), rows // parts)
        piece, matrix = own_of(
            weights[part], scaled[part], got, matrix, nodes, cut, cuts, skip, rows // cuts
        )
        own.append(piece)
        marks.append(matrix)
    steps = [None] if n_dp & (n_dp - 1) else radices(n_dp)
    for k, step in enumerate(steps):
        spread = sum_step(spread, "dp", n_dp, step, marks[min(k, cuts - 1)])
    if n_mp > 1:
        spread = lax.psum(spread, "mp")
    gy = grad_y_of(own, y, send_rows, returned, matrix, spread, shift, nodes, scale)
    if n_mp > 1:
        gy = lax.all_gather(gy, "mp", axis=0, tiled=True)

    packable = n_dp & (n_dp - 1) == 0 and n_dp > 1 and din == units and din % (16 * n_dp) == 0
    if not packable:
        grads = backward(features, hidden, slope, gy, w_out, me, None, 0, 1)
        return lax.psum(tuple(grads), "dp")
    kept, given = backward(features, hidden, slope, gy, w_out, me, n_dp, 0, 1)
    value = kept + exchange(given, "dp", n_dp, 1).astype(F32)
    for step in radices(n_dp)[1:]:
        value = reduce_step(value, "dp", n_dp, step)
    packed = gather_packed(value.astype(BF16), "dp", n_dp)
    return tuple(unpack(packed, me, n_dp, width))


def solution(mesh):
    return jax.shard_map(
        shards,
        mesh=mesh,
        in_specs=(
            P("dp", None),
            P(None, "mp"),
            P("mp", None),
            P(("dp", "mp")),
            P(("dp", "mp"), None),
            P(("dp", "mp"), None),
            P(("dp", "mp"), None),
        ),
        out_specs=(P(None, "mp"), P("mp", None)),
        check_vma=False,
    )
```

time: 222 us -> 197 us (0.89)
  Pallas kernels: 116 us -> 99.8 us
  waiting for transfers between devices: 47.8 us -> 38.1 us
    pallas_call x4 -> x2, Pallas kernels: 31.9 us -> 19.5 us  [weights_of(): pl.pallas_call(functools.partial(weights_kernel, pairs, part == 0), grid=...]
    ppermute x28, waiting for transfers between devices: 47.8 us -> 38.1 us  [exchange(): return lax.ppermute(value, axis, [(i, i ^ mask) for i in range(n)])]
    pallas_call x5 -> x8, Pallas kernels: 62.3 us -> 57.8 us  [the longest x1 22.8 us: backward(): pl.pallas_call(functools.partial(backward_kernel, n, last), grid=(nodes /...]
  transfers between devices with their start and end apart: 30 -> 30, of which waited for: 17 -> 12; matrix products, arithmetic and copies ran while one was open for 3% -> 3% of each run, Pallas kernels for 23% -> 18%
where the time goes in v2:
time: 197 us; the launch traced here: 196 us
  Pallas kernels  99.8 us (51%)
  starting transfers between devices  46.1 us (23%)
  waiting for transfers between devices  38.1 us (19%)
  local copies, waits for them, and re-layouts  7.8 us (4%)
  other arithmetic  3.53 us (2%)
    ppermute x28, waiting for transfers between devices, exchange(): return lax.ppermute(value, axis, [(i, i ^ mask) for i in range(n)])  38.1 us
    ppermute x28, starting transfers between devices, exchange(): return lax.ppermute(value, axis, [(i, i ^ mask) for i in range(n)])  33.1 us
    pallas_call x1, Pallas kernels, backward(): pl.pallas_call(functools.partial(backward_kernel, n, last), grid=(nodes /...  22.8 us
    pallas_call x2, Pallas kernels, weights_of(): pl.pallas_call(functools.partial(weights_kernel, pairs, part == 0), grid=...  19.5 us
    pallas_call x1, Pallas kernels, forward(): pl.pallas_call(forward_kernel, grid=(nodes // tile,), in_specs=[pl.BlockS...  18.3 us
    pallas_call x4, Pallas kernels, own_of(): pl.pallas_call(functools.partial(own_kernel, nodes, part, steps), grid=(s...  16.2 us
    pallas_call x1, Pallas kernels, grad_y_of(): pl.pallas_call(functools.partial(grad_y_kernel, nodes, scale, shift, part...  10.7 us
    all_to_all x1, starting transfers between devices, shards(): got = lax.all_to_all(sent, 'dp', split_axis=0, concat_axis=0, tiled=True)  6.96 us
  transfers between devices with their start and end apart: 30, of which 12 were waited for; matrix products, arithmetic and copies ran while one was open for 3% of the time, Pallas kernels for 18%

profile of v2, /device:TPU:0, one launch (start us, length us, event | category | flops | bytes accessed | tf_op | source)
XLA Modules:
  0.0 196.2 jit_solution(2482821482925802118)
XLA Ops:
  0.6 18.3 %forward.1 = (bf16[4096,1024]{1,0:T(8,128)(2,1)}, f32[4096,1024]{1,0:T(8,128)}, f32[4096,128]{1,0:T(8,128)}, bf16[4096,128]{1,0:T(8,128)(2,1)}, f32[128,128]{1,0:T(8,128)}) custom-call(bf16[4096,1024]{1,0:T(8,128)(2,1)} %x_ref.3, bf16[1024,1024]{1,0:T(8,128)(2,1)} %w_in_ref.1, bf16[1024,128]{1,0:T(8,128)(2,1)} %w_out_ref.3), custom_call_target="tpu_custom_call" | custom-call | flops 9663676416 | bytes 25165824 | tf_op jit(solution)/shard_map/forward/pallas_call | solution.py:68
  19.5 4.7 %send.1 = bf16[2048,128]{1,0:T(8,128)(2,1)} custom-call(s32[2048]{0:T(1024)} %index_ref.1, f32[4096,128]{1,0:T(8,128)} %get-tuple-element.49.y_ref.refs_2_.refs_4_), custom_call_target="tpu_custom_call" | custom-call | flops 2147483648 | bytes 1572864 | tf_op jit(solution)/shard_map/send/pallas_call | solution.py:111
  24.2 7.0 %all-to-all-start = ((bf16[32,64,128]{2,1,0:T(8,128)(2,1)}), bf16[32,64,128]{2,1,0:T(8,128)(2,1)S(1)}, u32[]{:S(2)}, u32[]{:S(2)}) async-start(bf16[32,64,128]{2,1,0:T(8,128)(2,1)} %bitcast.13), calls=%async_computation | async-start | bytes 1048576 | tf_op jit(solution)/shard_map/all_to_all | solution.py:553
  39.1 9.5 %weights.2 = (bf16[2048,2048]{1,0:T(8,128)(2,1)}, f32[2048,128]{1,0:T(8,128)}, f32[144,2048]{1,0:T(8,128)}, f32[128,128]{1,0:T(8,128)}) custom-call(s32[256,256]{1,0:T(8,128)} %reshape.20.refs_0_, f32[256,256]{1,0:T(8,128)} %reshape.21.refs_1_, f32[4096,128]{1,0:T(8,128)} %get-tuple-element.49.y_ref.refs_2_.refs_4_, bf16[4096,128]{1,0:T(8,128)(2,1)} %get-tuple-element.60.refs_3_), custom_call_target="tpu_custom_call" | custom-call | flops 2147483648 | bytes 8388608 | tf_op jit(solution)/shard_map/weights/pallas_call | solution.py:183
  53.1 10.0 %weights.3 = (bf16[2048,2048]{1,0:T(8,128)(2,1)}, f32[2048,128]{1,0:T(8,128)}, f32[144,2048]{1,0:T(8,128)}, f32[128,128]{1,0:T(8,128)}) custom-call(s32[256,256]{1,0:T(8,128)} %reshape.20.refs_0_, f32[256,256]{1,0:T(8,128)} %reshape.21.refs_1_, f32[4096,128]{1,0:T(8,128)} %get-tuple-element.49.y_ref.refs_2_.refs_4_, ...), custom_call_target="tpu_custom_call" | custom-call | flops 2147483648 | bytes 8388608 | tf_op jit(solution)/shard_map/weights/pallas_call | solution.py:183
  64.6 3.4 %back.1 = (bf16[2048,128]{1,0:T(8,128)(2,1)}, f32[128,128]{1,0:T(8,128)}) custom-call(bf16[2048,128]{1,0:T(8,128)(2,1)} %bitcast.6, f32[144,2048]{1,0:T(8,128)} %get-tuple-element.69.sums_ref, f32[128,128]{1,0:T(8,128)} %get-tuple-element.70.square_ref), custom_call_target="tpu_custom_call" | custom-call | flops 134217728 | bytes 1572864 | tf_op jit(solution)/shard_map/back/pallas_call | solution.py:221
  68.0 6.0 %all-to-all-start.1 = ((bf16[32,64,128]{2,1,0:T(8,128)(2,1)}), bf16[32,64,128]{2,1,0:T(8,128)(2,1)S(1)}, u32[]{:S(2)}, u32[]{:S(2)}) async-start(bf16[32,64,128]{2,1,0:T(8,128)(2,1)} %bitcast.12), calls=%async_computation.1 | async-start | bytes 1048576 | tf_op jit(solution)/shard_map/all_to_all | solution.py:571
  74.1 4.1 %own.4 = (f32[1024,128]{1,0:T(8,128)}, f32[128,128]{1,0:T(8,128)}) custom-call(bf16[2048,2048]{1,0:T(8,128)(2,1)} %get-tuple-element.54.weights_ref, f32[2048,128]{1,0:T(8,128)} %get-tuple-element.55.scaled_ref, bf16[2048,128]{1,0:T(8,128)(2,1)} %bitcast.7, f32[128,128]{1,0:T(8,128)} %add_add_fusion.2.matrix_ref), custom_call_target="tpu_custom_call" | custom-call | flops 536870912 | bytes 4194304 | tf_op jit(solution)/shard_map/own/pallas_call | solution.py:274
  78.2 2.6 %collective-permute-start.10 = (f32[128,128]{1,0:T(8,128)S(1)}, f32[128,128]{1,0:T(8,128)S(1)}, u32[]{:S(2)}, u32[]{:S(2)}) collective-permute-start(f32[128,128]{1,0:T(8,128)S(1)} %add.70), channel_id=1, source_target_pairs={{0,6},{1,7},{2,4},{3,5},{4,2},{5,3},{6,0},{7,1},{8,14},{9,15},{10,... | collective-permute-start | bytes 196616 | tf_op jit(solution)/shard_map/ppermute | solution.py:500
  81.8 4.1 %own.5 = (f32[1024,128]{1,0:T(8,128)}, f32[128,128]{1,0:T(8,128)}) custom-call(bf16[2048,2048]{1,0:T(8,128)(2,1)} %get-tuple-element.54.weights_ref, f32[2048,128]{1,0:T(8,128)} %get-tuple-element.55.scaled_ref, bf16[2048,128]{1,0:T(8,128)(2,1)} %bitcast.8, f32[128,128]{1,0:T(8,128)} %get-tuple-element.74.matrix_ref), custom_call_target="tpu_custom_call" | custom-call | flops 536870912 | bytes 4194304 | tf_op jit(solution)/shard_map/own/pallas_call | solution.py:274
  91.1 4.0 %own.6 = (f32[1024,128]{1,0:T(8,128)}, f32[128,128]{1,0:T(8,128)}) custom-call(bf16[2048,2048]{1,0:T(8,128)(2,1)} %get-tuple-element.76.weights_ref, f32[2048,128]{1,0:T(8,128)} %get-tuple-element.77.scaled_ref, bf16[2048,128]{1,0:T(8,128)(2,1)} %bitcast.9, f32[128,128]{1,0:T(8,128)} %get-tuple-element.78.matrix_ref), custom_call_target="tpu_custom_call" | custom-call | flops 536870912 | bytes 4194304 | tf_op jit(solution)/shard_map/own/pallas_call | solution.py:274
  95.1 4.0 %own.7 = (f32[1024,128]{1,0:T(8,128)}, f32[128,128]{1,0:T(8,128)}) custom-call(bf16[2048,2048]{1,0:T(8,128)(2,1)} %get-tuple-element.76.weights_ref, f32[2048,128]{1,0:T(8,128)} %get-tuple-element.77.scaled_ref, bf16[2048,128]{1,0:T(8,128)(2,1)} %bitcast.10, f32[128,128]{1,0:T(8,128)} %get-tuple-element.80.matrix_ref), custom_call_target="tpu_custom_call" | custom-call | flops 536870912 | bytes 4194304 | tf_op jit(solution)/shard_map/own/pallas_call | solution.py:274
  100.6 10.7 %grad_y.1.gy_ref = bf16[4096,128]{1,0:T(8,128)(2,1)} custom-call(f32[1024,128]{1,0:T(8,128)} %get-tuple-element.73.refs_0_, f32[1024,128]{1,0:T(8,128)} %get-tuple-element.75.refs_1_, f32[1024,128]{1,0:T(8,128)} %get-tuple-element.79.refs_2_, f32[1024,128]{1,0:T(8,128)} %get-tuple-element.81.refs_3_, f32[4096,128]{1,0:T(8,128)} %get-tuple-element.49.y_ref.refs_2_.refs_4_, ...), custom_call_target="tpu_custom_call" | custom-call | flops 2147483648 | bytes 4194304 | tf_op jit(solution)/shard_map/grad_y/pallas_call | solution.py:348
  111.3 22.8 %backward.1 = (f32[512,1152]{1,0:T(8,128)}, bf16[512,1152]{1,0:T(8,128)(2,1)}) custom-call(bf16[4096,1024]{1,0:T(8,128)(2,1)} %x_ref.3, f32[4096,1024]{1,0:T(8,128)} %get-tuple-element.48.slope_ref, bf16[4096,128]{1,0:T(8,128)(2,1)} %grad_y.1.gy_ref, bf16[1024,128]{1,0:T(8,128)(2,1)} %w_out_ref.3, s32[1]{0:T(128)} %bitcast.5.me_ref, ...), custom_call_target="tpu_custom_call" | custom-call | flops 10737418240 | bytes 25165824 | tf_op jit(solution)/shard_map/backward/pallas_call | solution.py:440
  134.1 3.1 %collective-permute-done.14 = bf16[512,1152]{1,0:T(8,128)(2,1)S(1)} collective-permute-done((bf16[512,1152]{1,0:T(8,128)(2,1)}, bf16[512,1152]{1,0:T(8,128)(2,1)S(1)}, u32[]{:S(2)}, u32[]{:S(2)}) %collective-permute-start.14) | collective-permute-done | bytes 1179680 | tf_op jit(solution)/shard_map/ppermute | solution.py:500
  142.7 6.4 %collective-permute-done.15 = bf16[128,1152]{1,0:T(8,128)(2,1)S(1)} collective-permute-done((bf16[128,1152]{1,0:T(8,128)(2,1)S(1)}, bf16[128,1152]{1,0:T(8,128)(2,1)S(1)}, u32[]{:S(2)}, u32[]{:S(2)}) %collective-permute-start.15) | collective-permute-done | bytes 294944 | tf_op jit(solution)/shard_map/ppermute | solution.py:500
  149.1 6.4 %collective-permute-done.16 = bf16[128,1152]{1,0:T(8,128)(2,1)S(1)} collective-permute-done((bf16[128,1152]{1,0:T(8,128)(2,1)S(1)}, bf16[128,1152]{1,0:T(8,128)(2,1)S(1)}, u32[]{:S(2)}, u32[]{:S(2)}) %collective-permute-start.16) | collective-permute-done | bytes 294944 | tf_op jit(solution)/shard_map/ppermute | solution.py:500
  156.6 3.2 %collective-permute-start.19 = (bf16[32,1152]{1,0:T(8,128)(2,1)S(1)}, bf16[32,1152]{1,0:T(8,128)(2,1)S(1)}, u32[]{:S(2)}, u32[]{:S(2)}) collective-permute-start(bf16[32,1152]{1,0:T(8,128)(2,1)S(1)} %get-tuple-element.111), channel_id=1, source_target_pairs={{0,16},{1,17},{2,18},{3,19},{4,20},{5,21},{6,22},{7,23},{8,24},{9,... | collective-permute-start | bytes 221192 | tf_op jit(solution)/shard_map/ppermute | solution.py:500
  160.5 3.3 %collective-permute-done.19 = bf16[32,1152]{1,0:T(8,128)(2,1)S(1)} collective-permute-done((bf16[32,1152]{1,0:T(8,128)(2,1)S(1)}, bf16[32,1152]{1,0:T(8,128)(2,1)S(1)}, u32[]{:S(2)}, u32[]{:S(2)}) %collective-permute-start.19) | collective-permute-done | bytes 73760 | tf_op jit(solution)/shard_map/ppermute | solution.py:500
  167.8 2.7 %collective-permute-start.23 = (bf16[32,1152]{1,0:T(8,128)(2,1)S(1)}, bf16[32,1152]{1,0:T(8,128)(2,1)S(1)}, u32[]{:S(2)}, u32[]{:S(2)}) collective-permute-start(bf16[32,1152]{1,0:T(8,128)(2,1)S(1)} %get-tuple-element.95), channel_id=1, source_target_pairs={{0,24},{1,25},{2,26},{3,27},{4,28},{5,29},{6,30},{7,31},{8,16},{9,... | collective-permute-start | bytes 221192 | tf_op jit(solution)/shard_map/ppermute | solution.py:500
  177.6 5.2 %collective-permute-done.24 = bf16[128,1152]{1,0:T(8,128)(2,1)S(1)} collective-permute-done((bf16[128,1152]{1,0:T(8,128)(2,1)S(1)}, bf16[128,1152]{1,0:T(8,128)(2,1)S(1)}, u32[]{:S(2)}, u32[]{:S(2)}) %collective-permute-start.24) | collective-permute-done | bytes 294944 | tf_op jit(solution)/shard_map/ppermute | solution.py:500
  182.9 4.5 %collective-permute-done.25 = bf16[128,1152]{1,0:T(8,128)(2,1)S(1)} collective-permute-done((bf16[128,1152]{1,0:T(8,128)(2,1)S(1)}, bf16[128,1152]{1,0:T(8,128)(2,1)S(1)}, u32[]{:S(2)}, u32[]{:S(2)}) %collective-permute-start.25) | collective-permute-done | bytes 294944 | tf_op jit(solution)/shard_map/ppermute | solution.py:500
  187.6 2.8 %collective-permute-done.27 = bf16[512,1152]{1,0:T(8,128)(2,1)S(1)} collective-permute-done((bf16[512,1152]{1,0:T(8,128)(2,1)S(1)}, bf16[512,1152]{1,0:T(8,128)(2,1)S(1)}, u32[]{:S(2)}, u32[]{:S(2)}) %collective-permute-start.27) | collective-permute-done | bytes 1179680 | tf_op jit(solution)/shard_map/ppermute | solution.py:500
  192.0 4.2 %unpack.1 = (f32[1024,1024]{1,0:T(8,128)}, f32[1024,128]{1,0:T(8,128)}) custom-call(bf16[1024,1152]{1,0:T(8,128)(2,1)} %copy-done.1, s32[1]{0:T(128)} %bitcast.5.me_ref), custom_call_target="tpu_custom_call" | custom-call | flops 1179648 | bytes 7077888 | tf_op jit(solution)/shard_map/unpack/pallas_call | solution.py:478
  (89 shorter events, 42.3 us)
Async XLA Ops:
  18.9 16.6 %collective-permute-start = (f32[128,128]{1,0:T(8,128)}, f32[128,128]{1,0:T(8,128)S(1)}, u32[]{:S(2)}, u32[]{:S(2)}) collective-permute-start(f32[128,128]{1,0:T(8,128)} %get-tuple-element.50), channel_id=1, source_target_pairs={{0,1},{1,0},{2,3},{3,2},{4,5},{5,4},{6,7},{7,6},{8,9},{9,8},{10,11... | collective-permute-start | bytes 196616 | tf_op jit(solution)/shard_map/ppermute | solution.py:500
  24.2 39.6 %all-to-all-start = ((bf16[32,64,128]{2,1,0:T(8,128)(2,1)}), bf16[32,64,128]{2,1,0:T(8,128)(2,1)S(1)}, u32[]{:S(2)}, u32[]{:S(2)}) async-start(bf16[32,64,128]{2,1,0:T(8,128)(2,1)} %bitcast.13), calls=%async_computation | async-start | bytes 1048576 | tf_op jit(solution)/shard_map/all_to_all | solution.py:553
  35.6 13.0 %collective-permute-start.1 = (f32[128,128]{1,0:T(8,128)S(1)}, f32[128,128]{1,0:T(8,128)S(1)}, u32[]{:S(2)}, u32[]{:S(2)}) collective-permute-start(f32[128,128]{1,0:T(8,128)S(1)} %add.63), channel_id=1, source_target_pairs={{0,2},{1,3},{2,0},{3,1},{4,6},{5,7},{6,4},{7,5},{8,10},{9,11},{10,... | collective-permute-start | bytes 196616 | tf_op jit(solution)/shard_map/ppermute | solution.py:500
  37.4 11.2 %collective-permute-start.2 = (f32[128,128]{1,0:T(8,128)S(1)}, f32[128,128]{1,0:T(8,128)S(1)}, u32[]{:S(2)}, u32[]{:S(2)}) collective-permute-start(f32[128,128]{1,0:T(8,128)S(1)} %add.63), channel_id=1, source_target_pairs={{0,4},{1,5},{2,6},{3,7},{4,0},{5,1},{6,2},{7,3},{8,12},{9,13},{10,... | collective-permute-start | bytes 196616 | tf_op jit(solution)/shard_map/ppermute | solution.py:500
  38.9 9.8 %collective-permute-start.3 = (f32[128,128]{1,0:T(8,128)S(1)}, f32[128,128]{1,0:T(8,128)S(1)}, u32[]{:S(2)}, u32[]{:S(2)}) collective-permute-start(f32[128,128]{1,0:T(8,128)S(1)} %add.63), channel_id=1, source_target_pairs={{0,6},{1,7},{2,4},{3,5},{4,2},{5,3},{6,0},{7,1},{8,14},{9,15},{10,... | collective-permute-start | bytes 196616 | tf_op jit(solution)/shard_map/ppermute | solution.py:500
  48.7 14.4 %collective-permute-start.4 = (f32[128,128]{1,0:T(8,128)S(1)}, f32[128,128]{1,0:T(8,128)S(1)}, u32[]{:S(2)}, u32[]{:S(2)}) collective-permute-start(f32[128,128]{1,0:T(8,128)S(1)} %add_add_fusion.3), channel_id=1, source_target_pairs={{0,8},{1,9},{2,10},{3,11},{4,12},{5,13},{6,14},{7,15},{8,0},{9,1},... | collective-permute-start | bytes 196616 | tf_op jit(solution)/shard_map/ppermute | solution.py:500
  50.5 12.6 %collective-permute-start.5 = (f32[128,128]{1,0:T(8,128)S(1)}, f32[128,128]{1,0:T(8,128)S(1)}, u32[]{:S(2)}, u32[]{:S(2)}) collective-permute-start(f32[128,128]{1,0:T(8,128)S(1)} %add_add_fusion.3), channel_id=1, source_target_pairs={{0,16},{1,17},{2,18},{3,19},{4,20},{5,21},{6,22},{7,23},{8,24},{9,... | collective-permute-start | bytes 196616 | tf_op jit(solution)/shard_map/ppermute | solution.py:500
  52.9 10.2 %collective-permute-start.6 = (f32[128,128]{1,0:T(8,128)S(1)}, f32[128,128]{1,0:T(8,128)S(1)}, u32[]{:S(2)}, u32[]{:S(2)}) collective-permute-start(f32[128,128]{1,0:T(8,128)S(1)} %add_add_fusion.3), channel_id=1, source_target_pairs={{0,24},{1,25},{2,26},{3,27},{4,28},{5,29},{6,30},{7,31},{8,16},{9,... | collective-permute-start | bytes 196616 | tf_op jit(solution)/shard_map/ppermute | solution.py:500
  68.0 31.8 %all-to-all-start.1 = ((bf16[32,64,128]{2,1,0:T(8,128)(2,1)}), bf16[32,64,128]{2,1,0:T(8,128)(2,1)S(1)}, u32[]{:S(2)}, u32[]{:S(2)}) async-start(bf16[32,64,128]{2,1,0:T(8,128)(2,1)} %bitcast.12), calls=%async_computation.1 | async-start | bytes 1048576 | tf_op jit(solution)/shard_map/all_to_all | solution.py:571
  78.2 7.6 %collective-permute-start.10 = (f32[128,128]{1,0:T(8,128)S(1)}, f32[128,128]{1,0:T(8,128)S(1)}, u32[]{:S(2)}, u32[]{:S(2)}) collective-permute-start(f32[128,128]{1,0:T(8,128)S(1)} %add.70), channel_id=1, source_target_pairs={{0,6},{1,7},{2,4},{3,5},{4,2},{5,3},{6,0},{7,1},{8,14},{9,15},{10,... | collective-permute-start | bytes 196616 | tf_op jit(solution)/shard_map/ppermute | solution.py:500
  80.9 5.0 %collective-permute-start.8 = (f32[128,128]{1,0:T(8,128)S(1)}, f32[128,128]{1,0:T(8,128)S(1)}, u32[]{:S(2)}, u32[]{:S(2)}) collective-permute-start(f32[128,128]{1,0:T(8,128)S(1)} %add.70), channel_id=1, source_target_pairs={{0,2},{1,3},{2,0},{3,1},{4,6},{5,7},{6,4},{7,5},{8,10},{9,11},{10,... | collective-permute-start | bytes 196616 | tf_op jit(solution)/shard_map/ppermute | solution.py:500
  86.3 12.9 %collective-permute-start.11 = (f32[128,128]{1,0:T(8,128)S(1)}, f32[128,128]{1,0:T(8,128)S(1)}, u32[]{:S(2)}, u32[]{:S(2)}) collective-permute-start(f32[128,128]{1,0:T(8,128)S(1)} %add_add_fusion.1), channel_id=1, source_target_pairs={{0,8},{1,9},{2,10},{3,11},{4,12},{5,13},{6,14},{7,15},{8,0},{9,1},... | collective-permute-start | bytes 196616 | tf_op jit(solution)/shard_map/ppermute | solution.py:500
  88.5 10.6 %collective-permute-start.12 = (f32[128,128]{1,0:T(8,128)S(1)}, f32[128,128]{1,0:T(8,128)S(1)}, u32[]{:S(2)}, u32[]{:S(2)}) collective-permute-start(f32[128,128]{1,0:T(8,128)S(1)} %add_add_fusion.1), channel_id=1, source_target_pairs={{0,16},{1,17},{2,18},{3,19},{4,20},{5,21},{6,22},{7,23},{8,24},{9,... | collective-permute-start | bytes 196616 | tf_op jit(solution)/shard_map/ppermute | solution.py:500
  90.2 9.0 %collective-permute-start.13 = (f32[128,128]{1,0:T(8,128)S(1)}, f32[128,128]{1,0:T(8,128)S(1)}, u32[]{:S(2)}, u32[]{:S(2)}) collective-permute-start(f32[128,128]{1,0:T(8,128)S(1)} %add_add_fusion.1), channel_id=1, source_target_pairs={{0,24},{1,25},{2,26},{3,27},{4,28},{5,29},{6,30},{7,31},{8,16},{9,... | collective-permute-start | bytes 196616 | tf_op jit(solution)/shard_map/ppermute | solution.py:500
  139.2 9.9 %collective-permute-start.15 = (bf16[128,1152]{1,0:T(8,128)(2,1)S(1)}, bf16[128,1152]{1,0:T(8,128)(2,1)S(1)}, u32[]{:S(2)}, u32[]{:S(2)}) collective-permute-start(bf16[128,1152]{1,0:T(8,128)(2,1)S(1)} %get-tuple-element.100), channel_id=1, source_target_pairs={{0,2},{1,3},{2,0},{3,1},{4,6},{5,7},{6,4},{7,5},{8,10},{9,11},{10,... | collective-permute-start | bytes 884744 | tf_op jit(solution)/shard_map/ppermute | solution.py:500
  140.4 15.1 %collective-permute-start.16 = (bf16[128,1152]{1,0:T(8,128)(2,1)S(1)}, bf16[128,1152]{1,0:T(8,128)(2,1)S(1)}, u32[]{:S(2)}, u32[]{:S(2)}) collective-permute-start(bf16[128,1152]{1,0:T(8,128)(2,1)S(1)} %get-tuple-element.102), channel_id=1, source_target_pairs={{0,4},{1,5},{2,6},{3,7},{4,0},{5,1},{6,2},{7,3},{8,12},{9,13},{10,... | collective-permute-start | bytes 884744 | tf_op jit(solution)/shard_map/ppermute | solution.py:500
  141.7 13.9 %collective-permute-start.17 = (bf16[128,1152]{1,0:T(8,128)(2,1)S(1)}, bf16[128,1152]{1,0:T(8,128)(2,1)S(1)}, u32[]{:S(2)}, u32[]{:S(2)}) collective-permute-start(bf16[128,1152]{1,0:T(8,128)(2,1)S(1)} %get-tuple-element.101), channel_id=1, source_target_pairs={{0,6},{1,7},{2,4},{3,5},{4,2},{5,3},{6,0},{7,1},{8,14},{9,15},{10,... | collective-permute-start | bytes 884744 | tf_op jit(solution)/shard_map/ppermute | solution.py:500
  156.6 7.3 %collective-permute-start.19 = (bf16[32,1152]{1,0:T(8,128)(2,1)S(1)}, bf16[32,1152]{1,0:T(8,128)(2,1)S(1)}, u32[]{:S(2)}, u32[]{:S(2)}) collective-permute-start(bf16[32,1152]{1,0:T(8,128)(2,1)S(1)} %get-tuple-element.111), channel_id=1, source_target_pairs={{0,16},{1,17},{2,18},{3,19},{4,20},{5,21},{6,22},{7,23},{8,24},{9,... | collective-permute-start | bytes 221192 | tf_op jit(solution)/shard_map/ppermute | solution.py:500
  159.8 6.2 %collective-permute-start.20 = (bf16[32,1152]{1,0:T(8,128)(2,1)S(1)}, bf16[32,1152]{1,0:T(8,128)(2,1)S(1)}, u32[]{:S(2)}, u32[]{:S(2)}) collective-permute-start(bf16[32,1152]{1,0:T(8,128)(2,1)S(1)} %get-tuple-element.110), channel_id=1, source_target_pairs={{0,24},{1,25},{2,26},{3,27},{4,28},{5,29},{6,30},{7,31},{8,16},{9,... | collective-permute-start | bytes 221192 | tf_op jit(solution)/shard_map/ppermute | solution.py:500
  166.0 5.3 %collective-permute-start.22 = (bf16[32,1152]{1,0:T(8,128)(2,1)S(1)}, bf16[32,1152]{1,0:T(8,128)(2,1)S(1)}, u32[]{:S(2)}, u32[]{:S(2)}) collective-permute-start(bf16[32,1152]{1,0:T(8,128)(2,1)S(1)} %get-tuple-element.95), channel_id=1, source_target_pairs={{0,16},{1,17},{2,18},{3,19},{4,20},{5,21},{6,22},{7,23},{8,24},{9,... | collective-permute-start | bytes 221192 | tf_op jit(solution)/shard_map/ppermute | solution.py:500
  167.8 6.2 %collective-permute-start.23 = (bf16[32,1152]{1,0:T(8,128)(2,1)S(1)}, bf16[32,1152]{1,0:T(8,128)(2,1)S(1)}, u32[]{:S(2)}, u32[]{:S(2)}) collective-permute-start(bf16[32,1152]{1,0:T(8,128)(2,1)S(1)} %get-tuple-element.95), channel_id=1, source_target_pairs={{0,24},{1,25},{2,26},{3,27},{4,28},{5,29},{6,30},{7,31},{8,16},{9,... | collective-permute-start | bytes 221192 | tf_op jit(solution)/shard_map/ppermute | solution.py:500
  174.0 8.8 %collective-permute-start.24 = (bf16[128,1152]{1,0:T(8,128)(2,1)S(1)}, bf16[128,1152]{1,0:T(8,128)(2,1)S(1)}, u32[]{:S(2)}, u32[]{:S(2)}) collective-permute-start(bf16[128,1152]{1,0:T(8,128)(2,1)S(1)} %pad_maximum_fusion), channel_id=1, source_target_pairs={{0,2},{1,3},{2,0},{3,1},{4,6},{5,7},{6,4},{7,5},{8,10},{9,11},{10,... | collective-permute-start | bytes 884744 | tf_op jit(solution)/shard_map/ppermute | solution.py:500
  175.5 11.9 %collective-permute-start.25 = (bf16[128,1152]{1,0:T(8,128)(2,1)S(1)}, bf16[128,1152]{1,0:T(8,128)(2,1)S(1)}, u32[]{:S(2)}, u32[]{:S(2)}) collective-permute-start(bf16[128,1152]{1,0:T(8,128)(2,1)S(1)} %pad_maximum_fusion), channel_id=1, source_target_pairs={{0,4},{1,5},{2,6},{3,7},{4,0},{5,1},{6,2},{7,3},{8,12},{9,13},{10,... | collective-permute-start | bytes 884744 | tf_op jit(solution)/shard_map/ppermute | solution.py:500
  176.3 11.1 %collective-permute-start.26 = (bf16[128,1152]{1,0:T(8,128)(2,1)S(1)}, bf16[128,1152]{1,0:T(8,128)(2,1)S(1)}, u32[]{:S(2)}, u32[]{:S(2)}) collective-permute-start(bf16[128,1152]{1,0:T(8,128)(2,1)S(1)} %pad_maximum_fusion), channel_id=1, source_target_pairs={{0,6},{1,7},{2,4},{3,5},{4,2},{5,3},{6,0},{7,1},{8,14},{9,15},{10,... | collective-permute-start | bytes 884744 | tf_op jit(solution)/shard_map/ppermute | solution.py:500
  (14 other events, 59.1 us)

commit v3 on v2

--- a/solution.py
+++ b/solution.py
@@ -299,40 +299,49 @@
     return first, (value - first.astype(F32)).astype(BF16)
 
 
-def grad_y_kernel(
-    nodes, scale, shift, parts, *refs
-):
+def set_right(nodes, scale, inverse_ref, spread_ref, right_ref):
+    width = inverse_ref.shape[0]
+    high = lax.Precision.HIGHEST
+    inverse = inverse_ref[...]
+    half = jnp.dot(inverse, spread_ref[...], precision=high, preferred_element_type=F32)
+    sandwich = jnp.dot(half, inverse, precision=high, preferred_element_type=F32)
+    for at, value in ((0, 2.0 * scale * inverse), (width, -2.0 * scale / nodes * sandwich)):
+        first, second = split(value)
+        right_ref[at:at + width, :width] = first
+        right_ref[at:at + width, width:] = second
+
+
+def grad_y_rows(shift, start, own, y, index, returned, right_ref):
+    tile, width = y.shape
+    at = lax.broadcasted_iota(jnp.int32, (tile, returned.shape[0]), 0) + start
+    spots = jnp.where(at == index, 1.0, 0.0)
+    times = jnp.sum(spots, axis=1, keepdims=True)
+    nearby = own + dot(spots.astype(BF16), returned) + shift * times * y
+    first, second = split(nearby)
+    y_first, y_second = split(y)
+    both = dot(jnp.concatenate([first, y_first], axis=1), right_ref[...])
+    rest = dot(jnp.concatenate([second, y_second], axis=1), right_ref[:, :width])
+    return (both[:, :width] + both[:, width:] + rest).astype(BF16)
+
+
+def grad_y_kernel(nodes, scale, shift, parts, *refs):
     own_refs = refs[:parts]
     y_ref, index_ref, returned_ref, inverse_ref, spread_ref, out_ref, right_ref = refs[parts:]
-    tile, width = y_ref.shape
-    count = returned_ref.shape[0]
+    tile = y_ref.shape[0]
     each = pl.num_programs(0) // parts
 
     @pl.when(pl.program_id(0) == 0)
     def _():
-        high = lax.Precision.HIGHEST
-        inverse = inverse_ref[...]
-        half = jnp.dot(inverse, spread_ref[...], precision=high, preferred_element_type=F32)
-        sandwich = jnp.dot(half, inverse, precision=high, preferred_element_type=F32)
-        for at, value in ((0, 2.0 * scale * inverse), (width, -2.0 * scale / nodes * sandwich)):
-            first, second = split(value)
-            right_ref[at:at + width, :width] = first
-            right_ref[at:at + width, width:] = second
+        set_right(nodes, scale, inverse_ref, spread_ref, right_ref)
 
     for part, own_ref in enumerate(own_refs):
 
         @pl.when(pl.program_id(0) // each == part)
         def _():
-            at = lax.broadcasted_iota(jnp.int32, (tile, count), 0) + pl.program_id(0) * tile
-            spots = jnp.where(at == index_ref[...], 1.0, 0.0)
-            times = jnp.sum(spots, axis=1, keepdims=True)
-            y = y_ref[...]
-            nearby = own_ref[...] + dot(spots.astype(BF16), returned_ref[...]) + shift * times * y
-            first, second = split(nearby)
-            y_first, y_second = split(y)
-            both = dot(jnp.concatenate([first, y_first], axis=1), right_ref[...])
-            rest = dot(jnp.concatenate([second, y_second], axis=1), right_ref[:, :width])
-            out_ref[...] = (both[:, :width] + both[:, width:] + rest).astype(BF16)
+            out_ref[...] = grad_y_rows(
+                shift, pl.program_id(0) * tile, own_ref[...], y_ref[...], index_ref[...],
+                returned_ref[...], right_ref
+            )
 
 
 def part_block(tile, width, part, each):
@@ -381,119 +390,176 @@
     return total
 
 
-def backward_kernel(n, last, x_ref, slope_ref, gy_ref, w_out_ref, me_ref, *rest):
-    if last:
-        hidden_ref, *outs, g_in, g_out = rest
-    else:
-        *outs, g_in = rest
-        g_out = None
-    gy = gy_ref[...]
+def add_grads(x_ref, hidden_ref, slope_ref, gy, w_out_ref, g_in, g_out):
+    units = g_in.shape[1]
+    step = min(512, units)
     x = x_ref[...]
-
+    for at in range(0, units, step):
+        back = dot_nt(gy, w_out_ref[at:at + step, :])
+        grad = (back * slope_ref[:, at:at + step]).astype(BF16)
+        g_in[:, at:at + step] += dot_tn(x, grad)
+    g_out[...] += dot_tn(hidden_ref[...], gy)
+
+
+def backward_kernel(x_ref, hidden_ref, slope_ref, gy_ref, w_out_ref, g_in, g_out):
     @pl.when(pl.program_id(0) == 0)
     def _():
         g_in[...] = jnp.zeros_like(g_in)
-        if last:
-            g_out[...] = jnp.zeros_like(g_out)
-
-    units = g_in.shape[1]
-    back = dot_nt(gy, w_out_ref[...])
-    grad = (back * slope_ref[...]).astype(BF16)
-    g_in[...] += dot_tn(x, grad)
-    if last:
-        g_out[...] += dot_tn(hidden_ref[...], gy)
-
-    @pl.when(pl.program_id(0) == pl.num_programs(0) - 1)
-    def _():
-        if n is None:
-            outs[0][...] = g_in[...]
-            if last:
-                outs[1][...] = g_out[...]
-        else:
-            me = me_ref[0]
-            chunk = g_in.shape[0] // n
-            for pair in range(n // 2):
-                for side, out in enumerate(outs):
-                    c = 2 * pair + (me + side) % 2
-                    at = pl.multiple_of((position(me ^ c, n) % (n // 2)) * chunk, chunk)
-                    rows = pl.ds(pl.multiple_of(c * chunk, chunk), chunk)
-                    out[pl.ds(at, chunk), :units] = g_in[rows, :].astype(out.dtype)
-                    if last:
-                        out[pl.ds(at, chunk), units:] = g_out[rows, :].astype(out.dtype)
-
-
-def backward(features, hidden, slope, gy, w_out, me, n, part, parts):
+        g_out[...] = jnp.zeros_like(g_out)
+
+    add_grads(x_ref, hidden_ref, slope_ref, gy_ref[...], w_out_ref, g_in, g_out)
+
+
+def backward(features, hidden, slope, gy, w_out):
     nodes, din = features.shape
-    all_units, width = w_out.shape
-    units = all_units // parts
-    last = part == parts - 1
+    units, width = w_out.shape
     tile = min(1024, nodes)
-    both = units + width if last else units
-    if n is None:
-        outs = [jax.ShapeDtypeStruct((din, units), F32)]
-        outs += [jax.ShapeDtypeStruct((all_units, width), F32)] if last else []
-    else:
-        outs = [
-            jax.ShapeDtypeStruct((din // 2, both), F32),
-            jax.ShapeDtypeStruct((din // 2, both), BF16),
-        ]
-    return pl.pallas_call(
-        functools.partial(backward_kernel, n, last),
+    shapes = [
+        jax.ShapeDtypeStruct((din, units), F32),
+        jax.ShapeDtypeStruct((units, width), F32),
+    ]
+    return pl.pallas_call(
+        backward_kernel,
         grid=(nodes // tile,),
         in_specs=[
             pl.BlockSpec((tile, din), lambda i: (i, 0)),
-            pl.BlockSpec((tile, units), lambda i: (i, part)),
-            pl.BlockSpec((tile, width), lambda i: (i, 0)),
-            pl.BlockSpec((units, width), lambda i: (part, 0)),
-            pl.BlockSpec(memory_space=pltpu.SMEM),
-        ]
-        + ([pl.BlockSpec((tile, all_units), lambda i: (i, 0))] if last else []),
-        out_specs=[pl.BlockSpec(o.shape, lambda i: (0, 0)) for o in outs],
-        out_shape=outs,
-        scratch_shapes=[pltpu.VMEM((din, units), F32)]
-        + ([pltpu.VMEM((all_units, width), F32)] if last else []),
-        compiler_params=params(),
-        cost_estimate=cost(2 * nodes * units * (din + 2 * width), 2 * nodes * (din + 2 * units)),
-        name="backward",
-    )(features, slope, gy, w_out, me, *([hidden] if last else []))
-
-
-def unpack_kernel(n, packed_ref, me_ref, g_in_ref, g_out_ref):
-    units = g_in_ref.shape[1]
-    rows = g_in_ref.shape[0]
-    chunk = packed_ref.shape[0] // n
-    me = me_ref[0]
-    first = pl.program_id(0) * (rows // chunk)
-    for c in range(rows // chunk):
-        at = pl.multiple_of(position(me ^ (first + c), n) * chunk, chunk)
-        part = packed_ref[pl.ds(at, chunk), :].astype(F32)
-        g_in_ref[c * chunk:(c + 1) * chunk, :] = part[:, :units]
-        g_out_ref[c * chunk:(c + 1) * chunk, :] = part[:, units:]
-
-
-def unpack(packed, me, n, width):
-    din, both = packed.shape
-    units = both - width
-    tile = din // 4
-    return pl.pallas_call(
-        functools.partial(unpack_kernel, n),
-        grid=(din // tile,),
-        in_specs=[
-            pl.BlockSpec((din, both), lambda i: (0, 0)),
-            pl.BlockSpec(memory_space=pltpu.SMEM),
-        ],
-        out_specs=[
+            pl.BlockSpec((tile, units), lambda i: (i, 0)),
             pl.BlockSpec((tile, units), lambda i: (i, 0)),
             pl.BlockSpec((tile, width), lambda i: (i, 0)),
-        ],
-        out_shape=[
-            jax.ShapeDtypeStruct((din, units), F32),
-            jax.ShapeDtypeStruct((din, width), F32),
-        ],
+            pl.BlockSpec((units, width), lambda i: (0, 0)),
+        ],
+        out_specs=[pl.BlockSpec(x.shape, lambda i: (0, 0)) for x in shapes],
+        out_shape=shapes,
         compiler_params=params(),
-        cost_estimate=cost(din * both, 6 * din * both),
+        cost_estimate=cost(2 * nodes * units * (din + 2 * width), 2 * nodes * (din + 3 * units)),
+        name="backward",
+    )(features, hidden, slope, gy, w_out)
+
+
+def packed_kernel(nodes, scale, shift, n, parts, *refs):
+    own_refs = refs[:parts]
+    y_ref, index_ref, returned_ref, inverse_ref, spread_ref = refs[parts:parts + 5]
+    x_ref, hidden_ref, slope_ref, w_out_ref, me_ref = refs[parts + 5:parts + 10]
+    *outs, g_in, g_out, gy_ref, right_ref = refs[parts + 10:]
+    tile = y_ref.shape[0]
+    some = min(512, tile)
+    each = pl.num_programs(0) // parts
+
+    @pl.when(pl.program_id(0) == 0)
+    def _():
+        set_right(nodes, scale, inverse_ref, spread_ref, right_ref)
+        g_in[...] = jnp.zeros_like(g_in)
+        g_out[...] = jnp.zeros_like(g_out)
+
+    for part, own_ref in enumerate(own_refs):
+
+        @pl.when(pl.program_id(0) // each == part)
+        def _():
+            for at in range(0, tile, some):
+                gy_ref[at:at + some, :] = grad_y_rows(
+                    shift, pl.program_id(0) * tile + at, own_ref[at:at + some, :],
+                    y_ref[at:at + some, :], index_ref[...], returned_ref[...], right_ref
+                )
+
+    add_grads(x_ref, hidden_ref, slope_ref, gy_ref[...], w_out_ref, g_in, g_out)
+
+    @pl.when(pl.program_id(0) == pl.num_programs(0) - 1)
+    def _():
+        me = me_ref[0]
+        units = g_in.shape[1]
+        chunk = g_in.shape[0] // n
+        for pair in range(n // 2):
+            for side, out in enumerate(outs):
+                c = 2 * pair + (me + side) % 2
+                at = pl.multiple_of((position(me ^ c, n) % (n // 2)) * chunk, chunk)
+                rows = pl.ds(pl.multiple_of(c * chunk, chunk), chunk)
+                out[pl.ds(at, chunk), :units] = g_in[rows, :].astype(out.dtype)
+                out[pl.ds(at, chunk), units:] = g_out[rows, :].astype(out.dtype)
+
+
+def packed_grads(
+    own, y, send_rows, returned, inverse, spread, features, hidden, slope, w_out, me,
+    nodes, scale, shift, n
+):
+    rows, din = features.shape
+    units, width = w_out.shape
+    count = returned.shape[0]
+    parts = len(own)
+    tile = min(1024, rows // parts)
+    each = rows // tile // parts
+    shapes = [
+        jax.ShapeDtypeStruct((din // 2, units + width), F32),
+        jax.ShapeDtypeStruct((din // 2, units + width), BF16),
+    ]
+    return pl.pallas_call(
+        functools.partial(packed_kernel, nodes, scale, shift, n, parts),
+        grid=(rows // tile,),
+        in_specs=[part_block(tile, width, part, each) for part in range(parts)]
+        + [
+            pl.BlockSpec((tile, width), lambda i: (i, 0)),
+            pl.BlockSpec((1, count), lambda i: (0, 0)),
+            pl.BlockSpec((count, width), lambda i: (0, 0)),
+            pl.BlockSpec((width, width), lambda i: (0, 0)),
+            pl.BlockSpec((width, width), lambda i: (0, 0)),
+            pl.BlockSpec((tile, din), lambda i: (i, 0)),
+            pl.BlockSpec((tile, units), lambda i: (i, 0)),
+            pl.BlockSpec((tile, units), lambda i: (i, 0)),
+            pl.BlockSpec((units, width), lambda i: (0, 0)),
+            pl.BlockSpec(memory_space=pltpu.SMEM),
+        ],
+        out_specs=[pl.BlockSpec(x.shape, lambda i: (0, 0)) for x in shapes],
+        out_shape=shapes,
+        scratch_shapes=[
+            pltpu.VMEM((din, units), F32),
+            pltpu.VMEM((units, width), F32),
+            pltpu.VMEM((tile, width), BF16),
+            pltpu.VMEM((2 * width, 2 * width), BF16),
+        ],
+        compiler_params=params(),
+        cost_estimate=cost(2 * rows * units * (din + 2 * width), 2 * rows * (din + 3 * units)),
+        name="packed_grads",
+    )(
+        *own, y, send_rows.reshape(1, count), returned, inverse, spread,
+        features, hidden, slope, w_out, me
+    )
+
+
+def unpack_kernel(places, lows, me_ref, *refs):
+    *pieces, g_in_ref, g_out_ref = refs
+    chunk, units = g_in_ref.shape[2:]
+    half = len(pieces) // 2
+    for k in range(half):
+
+        @pl.when(pl.program_id(0) == k)
+        def _():
+            for side, piece in enumerate((pieces[k], pieces[half + k])):
+                for t, place in enumerate(places):
+                    part = piece[t * chunk:(t + 1) * chunk, :].astype(F32)
+                    at = place ^ (me_ref[0] // lows)
+                    g_in_ref[at, (me_ref[0] + side) % 2] = part[:, :units]
+                    g_out_ref[at, (me_ref[0] + side) % 2] = part[:, units:]
+
+
+def unpack(pieces, spots, places, lows, me, shapes):
+    held = pl.BlockSpec(pieces[0].shape, lambda i, *_: (0, 0))
+
+    def spot(i, me_ref):
+        value = sum(jnp.where(i == k, x // 2, 0) for k, x in enumerate(spots))
+        return 0, value ^ (me_ref[0] % lows // 2), 0, 0
+
+    return pl.pallas_call(
+        functools.partial(unpack_kernel, places, lows),
+        grid_spec=pltpu.PrefetchScalarGridSpec(
+            num_scalar_prefetch=1,
+            grid=(len(pieces) // 2,),
+            in_specs=[held] * len(pieces),
+            out_specs=[pl.BlockSpec((x.shape[0], 2) + x.shape[2:], spot) for x in shapes],
+        ),
+        out_shape=shapes,
+        compiler_params=params(),
+        cost_estimate=cost(1e9, 0),
         name="unpack",
-    )(packed, me)
+    )(me, *pieces)
 
 
 def exchange(value, axis, n, mask):
@@ -520,11 +586,27 @@
     return total
 
 
-def gather_packed(value, axis, n):
-    for shift, radix in reversed(radices(n)):
+def gather_unpack(value, axis, n, me, units):
+    steps = radices(n)
+    for shift, radix in reversed(steps[2:]):
         parts = [value] + [exchange(value, axis, n, m << shift) for m in range(1, radix)]
         value = jnp.concatenate(parts, axis=0)
-    return value
+    shift, radix = steps[1]
+    lows = 2 * radix
+    rest = n // lows
+    chunk = value.shape[0] // rest
+    both = value.shape[1]
+    shapes = [
+        jax.ShapeDtypeStruct((rest, lows, chunk, size), F32) for size in (units, both - units)
+    ]
+    places = sorted(range(rest), key=lambda r: position(r * lows, n))
+    order = sorted(range(radix), key=lambda m: bin(m).count("1"))
+    here = [exchange(value, axis, n, m << shift) if m else value for m in order]
+    there = [exchange(piece, axis, n, 1) for piece in here]
+    pieces = here + there
+    spots = [m << shift for m in order]
+    outs = unpack(pieces, spots, places, lows, me, shapes)
+    return tuple(x.reshape(n * chunk, -1) for x in outs)
 
 
 def shards(features, w_in, w_out, send_rows, pair_src, pair_weight, pair_mask):
@@ -584,20 +666,20 @@
         spread = sum_step(spread, "dp", n_dp, step, marks[min(k, cuts - 1)])
     if n_mp > 1:
         spread = lax.psum(spread, "mp")
-    gy = grad_y_of(own, y, send_rows, returned, matrix, spread, shift, nodes, scale)
-    if n_mp > 1:
-        gy = lax.all_gather(gy, "mp", axis=0, tiled=True)
-
-    packable = n_dp & (n_dp - 1) == 0 and n_dp > 1 and din == units and din % (16 * n_dp) == 0
-    if not packable:
-        grads = backward(features, hidden, slope, gy, w_out, me, None, 0, 1)
-        return lax.psum(tuple(grads), "dp")
-    kept, given = backward(features, hidden, slope, gy, w_out, me, n_dp, 0, 1)
+    packable = n_dp & (n_dp - 1) == 0 and n_dp > 2 and din == units and din % (16 * n_dp) == 0
+    if not packable or n_mp > 1:
+        gy = grad_y_of(own, y, send_rows, returned, matrix, spread, shift, nodes, scale)
+        if n_mp > 1:
+            gy = lax.all_gather(gy, "mp", axis=0, tiled=True)
+        return lax.psum(tuple(backward(features, hidden, slope, gy, w_out)), "dp")
+    kept, given = packed_grads(
+        own, y, send_rows, returned, matrix, spread, features, hidden, slope, w_out, me,
+        nodes, scale, shift, n_dp
+    )
     value = kept + exchange(given, "dp", n_dp, 1).astype(F32)
     for step in radices(n_dp)[1:]:
         value = reduce_step(value, "dp", n_dp, step)
-    packed = gather_packed(value.astype(BF16), "dp", n_dp)
-    return tuple(unpack(packed, me, n_dp, width))
+    return gather_unpack(value.astype(BF16), "dp", n_dp, me, units)
 
 
 def solution(mesh):

time: 197 us -> 190 us (0.964)
  Pallas kernels: 99.8 us -> 94.9 us
    pallas_call x3 -> x2, Pallas kernels: 37.7 us -> 32.9 us  [the longest x1 28.7 us: packed_grads(): pl.pallas_call(functools.partial(packed_kernel, nodes, scale, shift, n, p...]
    ppermute x28 -> x31, waiting for transfers between devices: 38.1 us -> 36.9 us  [exchange(): return lax.ppermute(value, axis, [(i, i ^ mask) for i in range(n)])]
    ppermute x28 -> x31, starting transfers between devices: 33.1 us -> 33.6 us  [exchange(): return lax.ppermute(value, axis, [(i, i ^ mask) for i in range(n)])]
  transfers between devices with their start and end apart: 30 -> 33, of which waited for: 12 -> 13; matrix products, arithmetic and copies ran while one was open for 3% -> 3% of each run, Pallas kernels for 18% -> 19%
where the time goes in v3:
time: 190 us
  Pallas kernels  94.9 us (50%)
  starting transfers between devices  46.6 us (25%)
  waiting for transfers between devices  36.9 us (19%)
  local copies, waits for them, and re-layouts  7.05 us (4%)
  other arithmetic  3.53 us (2%)
    ppermute x31, waiting for transfers between devices, exchange(): return lax.ppermute(value, axis, [(i, i ^ mask) for i in range(n)])  36.9 us
    ppermute x31, starting transfers between devices, exchange(): return lax.ppermute(value, axis, [(i, i ^ mask) for i in range(n)])  33.6 us
    pallas_call x1, Pallas kernels, packed_grads(): pl.pallas_call(functools.partial(packed_kernel, nodes, scale, shift, n, p...  28.7 us
    pallas_call x2, Pallas kernels, weights_of(): pl.pallas_call(functools.partial(weights_kernel, pairs, part == 0), grid=...  19.4 us
    pallas_call x1, Pallas kernels, forward(): pl.pallas_call(forward_kernel, grid=(nodes // tile,), in_specs=[pl.BlockS...  18.3 us
    pallas_call x4, Pallas kernels, own_of(): pl.pallas_call(functools.partial(own_kernel, nodes, part, steps), grid=(s...  16.2 us
    all_to_all x1, starting transfers between devices, shards(): got = lax.all_to_all(sent, 'dp', split_axis=0, concat_axis=0, tiled=True)  6.95 us
    all_to_all x1, starting transfers between devices, shards(): lax.all_to_all(back, 'dp', split_axis=0, concat_axis=0, tiled=True)  6.01 us
  transfers between devices with their start and end apart: 33, of which 13 were waited for; matrix products, arithmetic and copies ran while one was open for 3% of the time, Pallas kernels for 19%

profile of v3, /device:TPU:0, one launch (start us, length us, event | category | flops | bytes accessed | tf_op | source)
XLA Modules:
  0.0 189.9 jit_solution(5997005684130225924)
XLA Ops:
  0.6 18.3 %forward.1 = (bf16[4096,1024]{1,0:T(8,128)(2,1)}, f32[4096,1024]{1,0:T(8,128)}, f32[4096,128]{1,0:T(8,128)}, bf16[4096,128]{1,0:T(8,128)(2,1)}, f32[128,128]{1,0:T(8,128)}) custom-call(bf16[4096,1024]{1,0:T(8,128)(2,1)} %refs_9_.1, bf16[1024,1024]{1,0:T(8,128)(2,1)} %w_in_ref.1, bf16[1024,128]{1,0:T(8,128)(2,1)} %refs_12_.1), custom_call_target="tpu_custom_call" | custom-call | flops 9663676416 | bytes 25165824 | tf_op jit(solution)/shard_map/forward/pallas_call | solution.py:68
  19.5 4.7 %send.1 = bf16[2048,128]{1,0:T(8,128)(2,1)} custom-call(s32[2048]{0:T(1024)} %index_ref.1, f32[4096,128]{1,0:T(8,128)} %get-tuple-element.50.y_ref.refs_2_.refs_4_), custom_call_target="tpu_custom_call" | custom-call | flops 2147483648 | bytes 1572864 | tf_op jit(solution)/shard_map/send/pallas_call | solution.py:111
  24.2 7.0 %all-to-all-start = ((bf16[32,64,128]{2,1,0:T(8,128)(2,1)}), bf16[32,64,128]{2,1,0:T(8,128)(2,1)S(1)}, u32[]{:S(2)}, u32[]{:S(2)}) async-start(bf16[32,64,128]{2,1,0:T(8,128)(2,1)} %bitcast.15), calls=%async_computation | async-start | bytes 1048576 | tf_op jit(solution)/shard_map/all_to_all | solution.py:635
  39.2 9.4 %weights.2 = (bf16[2048,2048]{1,0:T(8,128)(2,1)}, f32[2048,128]{1,0:T(8,128)}, f32[144,2048]{1,0:T(8,128)}, f32[128,128]{1,0:T(8,128)}) custom-call(s32[256,256]{1,0:T(8,128)} %reshape.27.refs_0_, f32[256,256]{1,0:T(8,128)} %reshape.28.refs_1_, f32[4096,128]{1,0:T(8,128)} %get-tuple-element.50.y_ref.refs_2_.refs_4_, bf16[4096,128]{1,0:T(8,128)(2,1)} %get-tuple-element.61.refs_3_), custom_call_target="tpu_custom_call" | custom-call | flops 2147483648 | bytes 8388608 | tf_op jit(solution)/shard_map/weights/pallas_call | solution.py:183
  50.5 2.4 %collective-permute-start.5 = (f32[128,128]{1,0:T(8,128)S(1)}, f32[128,128]{1,0:T(8,128)S(1)}, u32[]{:S(2)}, u32[]{:S(2)}) collective-permute-start(f32[128,128]{1,0:T(8,128)S(1)} %add_add_fusion.3), channel_id=1, source_target_pairs={{0,16},{1,17},{2,18},{3,19},{4,20},{5,21},{6,22},{7,23},{8,24},{9,... | collective-permute-start | bytes 196616 | tf_op jit(solution)/shard_map/ppermute | solution.py:566
  53.1 10.0 %weights.3 = (bf16[2048,2048]{1,0:T(8,128)(2,1)}, f32[2048,128]{1,0:T(8,128)}, f32[144,2048]{1,0:T(8,128)}, f32[128,128]{1,0:T(8,128)}) custom-call(s32[256,256]{1,0:T(8,128)} %reshape.27.refs_0_, f32[256,256]{1,0:T(8,128)} %reshape.28.refs_1_, f32[4096,128]{1,0:T(8,128)} %get-tuple-element.50.y_ref.refs_2_.refs_4_, ...), custom_call_target="tpu_custom_call" | custom-call | flops 2147483648 | bytes 8388608 | tf_op jit(solution)/shard_map/weights/pallas_call | solution.py:183
  64.6 3.4 %back.1 = (bf16[2048,128]{1,0:T(8,128)(2,1)}, f32[128,128]{1,0:T(8,128)}) custom-call(bf16[2048,128]{1,0:T(8,128)(2,1)} %bitcast.8, f32[144,2048]{1,0:T(8,128)} %get-tuple-element.70.sums_ref, f32[128,128]{1,0:T(8,128)} %get-tuple-element.71.square_ref), custom_call_target="tpu_custom_call" | custom-call | flops 134217728 | bytes 1572864 | tf_op jit(solution)/shard_map/back/pallas_call | solution.py:221
  68.0 6.0 %all-to-all-start.1 = ((bf16[32,64,128]{2,1,0:T(8,128)(2,1)}), bf16[32,64,128]{2,1,0:T(8,128)(2,1)S(1)}, u32[]{:S(2)}, u32[]{:S(2)}) async-start(bf16[32,64,128]{2,1,0:T(8,128)(2,1)} %bitcast.14), calls=%async_computation.1 | async-start | bytes 1048576 | tf_op jit(solution)/shard_map/all_to_all | solution.py:653
  74.1 4.1 %own.4 = (f32[1024,128]{1,0:T(8,128)}, f32[128,128]{1,0:T(8,128)}) custom-call(bf16[2048,2048]{1,0:T(8,128)(2,1)} %get-tuple-element.55.weights_ref, f32[2048,128]{1,0:T(8,128)} %get-tuple-element.56.scaled_ref, bf16[2048,128]{1,0:T(8,128)(2,1)} %bitcast.9, f32[128,128]{1,0:T(8,128)} %add_add_fusion.2.matrix_ref), custom_call_target="tpu_custom_call" | custom-call | flops 536870912 | bytes 4194304 | tf_op jit(solution)/shard_map/own/pallas_call | solution.py:274
  78.2 2.6 %collective-permute-start.10 = (f32[128,128]{1,0:T(8,128)S(1)}, f32[128,128]{1,0:T(8,128)S(1)}, u32[]{:S(2)}, u32[]{:S(2)}) collective-permute-start(f32[128,128]{1,0:T(8,128)S(1)} %add.70), channel_id=1, source_target_pairs={{0,6},{1,7},{2,4},{3,5},{4,2},{5,3},{6,0},{7,1},{8,14},{9,15},{10,... | collective-permute-start | bytes 196616 | tf_op jit(solution)/shard_map/ppermute | solution.py:566
  81.8 4.0 %own.5 = (f32[1024,128]{1,0:T(8,128)}, f32[128,128]{1,0:T(8,128)}) custom-call(bf16[2048,2048]{1,0:T(8,128)(2,1)} %get-tuple-element.55.weights_ref, f32[2048,128]{1,0:T(8,128)} %get-tuple-element.56.scaled_ref, bf16[2048,128]{1,0:T(8,128)(2,1)} %bitcast.10, f32[128,128]{1,0:T(8,128)} %get-tuple-element.75.matrix_ref), custom_call_target="tpu_custom_call" | custom-call | flops 536870912 | bytes 4194304 | tf_op jit(solution)/shard_map/own/pallas_call | solution.py:274
  91.1 4.0 %own.6 = (f32[1024,128]{1,0:T(8,128)}, f32[128,128]{1,0:T(8,128)}) custom-call(bf16[2048,2048]{1,0:T(8,128)(2,1)} %get-tuple-element.77.weights_ref, f32[2048,128]{1,0:T(8,128)} %get-tuple-element.78.scaled_ref, bf16[2048,128]{1,0:T(8,128)(2,1)} %bitcast.11, f32[128,128]{1,0:T(8,128)} %get-tuple-element.79.matrix_ref), custom_call_target="tpu_custom_call" | custom-call | flops 536870912 | bytes 4194304 | tf_op jit(solution)/shard_map/own/pallas_call | solution.py:274
  95.1 4.1 %own.7 = (f32[1024,128]{1,0:T(8,128)}, f32[128,128]{1,0:T(8,128)}) custom-call(bf16[2048,2048]{1,0:T(8,128)(2,1)} %get-tuple-element.77.weights_ref, f32[2048,128]{1,0:T(8,128)} %get-tuple-element.78.scaled_ref, bf16[2048,128]{1,0:T(8,128)(2,1)} %bitcast.12, f32[128,128]{1,0:T(8,128)} %get-tuple-element.81.matrix_ref), custom_call_target="tpu_custom_call" | custom-call | flops 536870912 | bytes 4194304 | tf_op jit(solution)/shard_map/own/pallas_call | solution.py:274
  100.6 28.7 %packed_grads.1 = (f32[512,1152]{1,0:T(8,128)}, bf16[512,1152]{1,0:T(8,128)(2,1)}) custom-call(f32[1024,128]{1,0:T(8,128)} %get-tuple-element.74.refs_0_, f32[1024,128]{1,0:T(8,128)} %get-tuple-element.76.refs_1_, f32[1024,128]{1,0:T(8,128)} %get-tuple-element.80.refs_2_, f32[1024,128]{1,0:T(8,128)} %get-tuple-element.82.refs_3_, ...), custom_call_target="tpu_custom_call" | custom-call | flops 10737418240 | bytes 33554432 | tf_op jit(solution)/shard_map/packed_grads/pallas_call | solution.py:494
  129.4 3.0 %collective-permute-done.14 = bf16[512,1152]{1,0:T(8,128)(2,1)S(1)} collective-permute-done((bf16[512,1152]{1,0:T(8,128)(2,1)}, bf16[512,1152]{1,0:T(8,128)(2,1)S(1)}, u32[]{:S(2)}, u32[]{:S(2)}) %collective-permute-start.14) | collective-permute-done | bytes 1179680 | tf_op jit(solution)/shard_map/ppermute | solution.py:566
  138.0 6.4 %collective-permute-done.15 = bf16[128,1152]{1,0:T(8,128)(2,1)S(1)} collective-permute-done((bf16[128,1152]{1,0:T(8,128)(2,1)S(1)}, bf16[128,1152]{1,0:T(8,128)(2,1)S(1)}, u32[]{:S(2)}, u32[]{:S(2)}) %collective-permute-start.15) | collective-permute-done | bytes 294944 | tf_op jit(solution)/shard_map/ppermute | solution.py:566
  144.4 6.4 %collective-permute-done.16 = bf16[128,1152]{1,0:T(8,128)(2,1)S(1)} collective-permute-done((bf16[128,1152]{1,0:T(8,128)(2,1)S(1)}, bf16[128,1152]{1,0:T(8,128)(2,1)S(1)}, u32[]{:S(2)}, u32[]{:S(2)}) %collective-permute-start.16) | collective-permute-done | bytes 294944 | tf_op jit(solution)/shard_map/ppermute | solution.py:566
  151.9 3.2 %collective-permute-start.19 = (bf16[32,1152]{1,0:T(8,128)(2,1)S(1)}, bf16[32,1152]{1,0:T(8,128)(2,1)S(1)}, u32[]{:S(2)}, u32[]{:S(2)}) collective-permute-start(bf16[32,1152]{1,0:T(8,128)(2,1)S(1)} %get-tuple-element.107), channel_id=1, source_target_pairs={{0,16},{1,17},{2,18},{3,19},{4,20},{5,21},{6,22},{7,23},{8,24},{9,... | collective-permute-start | bytes 221192 | tf_op jit(solution)/shard_map/ppermute | solution.py:566
  155.8 3.3 %collective-permute-done.19 = bf16[32,1152]{1,0:T(8,128)(2,1)S(1)} collective-permute-done((bf16[32,1152]{1,0:T(8,128)(2,1)S(1)}, bf16[32,1152]{1,0:T(8,128)(2,1)S(1)}, u32[]{:S(2)}, u32[]{:S(2)}) %collective-permute-start.19) | collective-permute-done | bytes 73760 | tf_op jit(solution)/shard_map/ppermute | solution.py:566
  163.0 2.8 %collective-permute-start.23 = (bf16[32,1152]{1,0:T(8,128)(2,1)S(1)}, bf16[32,1152]{1,0:T(8,128)(2,1)S(1)}, u32[]{:S(2)}, u32[]{:S(2)}) collective-permute-start(bf16[32,1152]{1,0:T(8,128)(2,1)S(1)} %fusion.4), channel_id=1, source_target_pairs={{0,24},{1,25},{2,26},{3,27},{4,28},{5,29},{6,30},{7,31},{8,16},{9,... | collective-permute-start | bytes 221192 | tf_op jit(solution)/shard_map/ppermute | solution.py:566
  166.7 2.5 %collective-permute-done.23 = bf16[32,1152]{1,0:T(8,128)(2,1)S(1)} collective-permute-done((bf16[32,1152]{1,0:T(8,128)(2,1)S(1)}, bf16[32,1152]{1,0:T(8,128)(2,1)S(1)}, u32[]{:S(2)}, u32[]{:S(2)}) %collective-permute-start.23) | collective-permute-done | bytes 73760 | tf_op jit(solution)/shard_map/ppermute | solution.py:566
  172.8 5.3 %collective-permute-done.24.refs_1_ = bf16[128,1152]{1,0:T(8,128)(2,1)S(1)} collective-permute-done((bf16[128,1152]{1,0:T(8,128)(2,1)S(1)}, bf16[128,1152]{1,0:T(8,128)(2,1)S(1)}, u32[]{:S(2)}, u32[]{:S(2)}) %collective-permute-start.24) | collective-permute-done | bytes 294944 | tf_op jit(solution)/shard_map/ppermute | solution.py:566
  178.1 4.6 %collective-permute-done.25.refs_2_ = bf16[128,1152]{1,0:T(8,128)(2,1)S(1)} collective-permute-done((bf16[128,1152]{1,0:T(8,128)(2,1)S(1)}, bf16[128,1152]{1,0:T(8,128)(2,1)S(1)}, u32[]{:S(2)}, u32[]{:S(2)}) %collective-permute-start.25) | collective-permute-done | bytes 294944 | tf_op jit(solution)/shard_map/ppermute | solution.py:566
  185.7 4.2 %unpack.1 = (f32[4,8,32,1024]{3,2,1,0:T(8,128)}, f32[4,8,32,128]{3,2,1,0:T(8,128)}) custom-call(s32[1]{0:T(128)} %bitcast.refs_13_.me_ref, bf16[128,1152]{1,0:T(8,128)(2,1)} %copy-done.2, bf16[128,1152]{1,0:T(8,128)(2,1)} %copy-done.8, bf16[128,1152]{1,0:T(8,128)(2,1)} %copy-done.9, bf16[128,1152]{1,0:T(8,128)(2,1)} %copy-done.10, ...), custom_call_target="tpu_custom_call" | custom-call | flops 1000000000 | tf_op jit(solution)/shard_map/unpack/pallas_call | solution.py:550
  (100 shorter events, 38.6 us)
Async XLA Ops:
  19.0 16.6 %collective-permute-start = (f32[128,128]{1,0:T(8,128)}, f32[128,128]{1,0:T(8,128)S(1)}, u32[]{:S(2)}, u32[]{:S(2)}) collective-permute-start(f32[128,128]{1,0:T(8,128)} %get-tuple-element.51), channel_id=1, source_target_pairs={{0,1},{1,0},{2,3},{3,2},{4,5},{5,4},{6,7},{7,6},{8,9},{9,8},{10,11... | collective-permute-start | bytes 196616 | tf_op jit(solution)/shard_map/ppermute | solution.py:566
  24.2 39.6 %all-to-all-start = ((bf16[32,64,128]{2,1,0:T(8,128)(2,1)}), bf16[32,64,128]{2,1,0:T(8,128)(2,1)S(1)}, u32[]{:S(2)}, u32[]{:S(2)}) async-start(bf16[32,64,128]{2,1,0:T(8,128)(2,1)} %bitcast.15), calls=%async_computation | async-start | bytes 1048576 | tf_op jit(solution)/shard_map/all_to_all | solution.py:635
  35.6 13.0 %collective-permute-start.1 = (f32[128,128]{1,0:T(8,128)S(1)}, f32[128,128]{1,0:T(8,128)S(1)}, u32[]{:S(2)}, u32[]{:S(2)}) collective-permute-start(f32[128,128]{1,0:T(8,128)S(1)} %add.63), channel_id=1, source_target_pairs={{0,2},{1,3},{2,0},{3,1},{4,6},{5,7},{6,4},{7,5},{8,10},{9,11},{10,... | collective-permute-start | bytes 196616 | tf_op jit(solution)/shard_map/ppermute | solution.py:566
  37.4 11.2 %collective-permute-start.2 = (f32[128,128]{1,0:T(8,128)S(1)}, f32[128,128]{1,0:T(8,128)S(1)}, u32[]{:S(2)}, u32[]{:S(2)}) collective-permute-start(f32[128,128]{1,0:T(8,128)S(1)} %add.63), channel_id=1, source_target_pairs={{0,4},{1,5},{2,6},{3,7},{4,0},{5,1},{6,2},{7,3},{8,12},{9,13},{10,... | collective-permute-start | bytes 196616 | tf_op jit(solution)/shard_map/ppermute | solution.py:566
  38.9 9.7 %collective-permute-start.3 = (f32[128,128]{1,0:T(8,128)S(1)}, f32[128,128]{1,0:T(8,128)S(1)}, u32[]{:S(2)}, u32[]{:S(2)}) collective-permute-start(f32[128,128]{1,0:T(8,128)S(1)} %add.63), channel_id=1, source_target_pairs={{0,6},{1,7},{2,4},{3,5},{4,2},{5,3},{6,0},{7,1},{8,14},{9,15},{10,... | collective-permute-start | bytes 196616 | tf_op jit(solution)/shard_map/ppermute | solution.py:566
  48.6 14.4 %collective-permute-start.4 = (f32[128,128]{1,0:T(8,128)S(1)}, f32[128,128]{1,0:T(8,128)S(1)}, u32[]{:S(2)}, u32[]{:S(2)}) collective-permute-start(f32[128,128]{1,0:T(8,128)S(1)} %add_add_fusion.3), channel_id=1, source_target_pairs={{0,8},{1,9},{2,10},{3,11},{4,12},{5,13},{6,14},{7,15},{8,0},{9,1},... | collective-permute-start | bytes 196616 | tf_op jit(solution)/shard_map/ppermute | solution.py:566
  50.5 12.6 %collective-permute-start.5 = (f32[128,128]{1,0:T(8,128)S(1)}, f32[128,128]{1,0:T(8,128)S(1)}, u32[]{:S(2)}, u32[]{:S(2)}) collective-permute-start(f32[128,128]{1,0:T(8,128)S(1)} %add_add_fusion.3), channel_id=1, source_target_pairs={{0,16},{1,17},{2,18},{3,19},{4,20},{5,21},{6,22},{7,23},{8,24},{9,... | collective-permute-start | bytes 196616 | tf_op jit(solution)/shard_map/ppermute | solution.py:566
  52.9 10.2 %collective-permute-start.6 = (f32[128,128]{1,0:T(8,128)S(1)}, f32[128,128]{1,0:T(8,128)S(1)}, u32[]{:S(2)}, u32[]{:S(2)}) collective-permute-start(f32[128,128]{1,0:T(8,128)S(1)} %add_add_fusion.3), channel_id=1, source_target_pairs={{0,24},{1,25},{2,26},{3,27},{4,28},{5,29},{6,30},{7,31},{8,16},{9,... | collective-permute-start | bytes 196616 | tf_op jit(solution)/shard_map/ppermute | solution.py:566
  68.0 31.9 %all-to-all-start.1 = ((bf16[32,64,128]{2,1,0:T(8,128)(2,1)}), bf16[32,64,128]{2,1,0:T(8,128)(2,1)S(1)}, u32[]{:S(2)}, u32[]{:S(2)}) async-start(bf16[32,64,128]{2,1,0:T(8,128)(2,1)} %bitcast.14), calls=%async_computation.1 | async-start | bytes 1048576 | tf_op jit(solution)/shard_map/all_to_all | solution.py:653
  78.2 7.6 %collective-permute-start.10 = (f32[128,128]{1,0:T(8,128)S(1)}, f32[128,128]{1,0:T(8,128)S(1)}, u32[]{:S(2)}, u32[]{:S(2)}) collective-permute-start(f32[128,128]{1,0:T(8,128)S(1)} %add.70), channel_id=1, source_target_pairs={{0,6},{1,7},{2,4},{3,5},{4,2},{5,3},{6,0},{7,1},{8,14},{9,15},{10,... | collective-permute-start | bytes 196616 | tf_op jit(solution)/shard_map/ppermute | solution.py:566
  86.3 12.9 %collective-permute-start.11 = (f32[128,128]{1,0:T(8,128)S(1)}, f32[128,128]{1,0:T(8,128)S(1)}, u32[]{:S(2)}, u32[]{:S(2)}) collective-permute-start(f32[128,128]{1,0:T(8,128)S(1)} %add_add_fusion.1), channel_id=1, source_target_pairs={{0,8},{1,9},{2,10},{3,11},{4,12},{5,13},{6,14},{7,15},{8,0},{9,1},... | collective-permute-start | bytes 196616 | tf_op jit(solution)/shard_map/ppermute | solution.py:566
  88.5 10.7 %collective-permute-start.12 = (f32[128,128]{1,0:T(8,128)S(1)}, f32[128,128]{1,0:T(8,128)S(1)}, u32[]{:S(2)}, u32[]{:S(2)}) collective-permute-start(f32[128,128]{1,0:T(8,128)S(1)} %add_add_fusion.1), channel_id=1, source_target_pairs={{0,16},{1,17},{2,18},{3,19},{4,20},{5,21},{6,22},{7,23},{8,24},{9,... | collective-permute-start | bytes 196616 | tf_op jit(solution)/shard_map/ppermute | solution.py:566
  90.2 9.0 %collective-permute-start.13 = (f32[128,128]{1,0:T(8,128)S(1)}, f32[128,128]{1,0:T(8,128)S(1)}, u32[]{:S(2)}, u32[]{:S(2)}) collective-permute-start(f32[128,128]{1,0:T(8,128)S(1)} %add_add_fusion.1), channel_id=1, source_target_pairs={{0,24},{1,25},{2,26},{3,27},{4,28},{5,29},{6,30},{7,31},{8,16},{9,... | collective-permute-start | bytes 196616 | tf_op jit(solution)/shard_map/ppermute | solution.py:566
  134.5 9.9 %collective-permute-start.15 = (bf16[128,1152]{1,0:T(8,128)(2,1)S(1)}, bf16[128,1152]{1,0:T(8,128)(2,1)S(1)}, u32[]{:S(2)}, u32[]{:S(2)}) collective-permute-start(bf16[128,1152]{1,0:T(8,128)(2,1)S(1)} %get-tuple-element.102), channel_id=1, source_target_pairs={{0,2},{1,3},{2,0},{3,1},{4,6},{5,7},{6,4},{7,5},{8,10},{9,11},{10,... | collective-permute-start | bytes 884744 | tf_op jit(solution)/shard_map/ppermute | solution.py:566
  135.7 15.1 %collective-permute-start.16 = (bf16[128,1152]{1,0:T(8,128)(2,1)S(1)}, bf16[128,1152]{1,0:T(8,128)(2,1)S(1)}, u32[]{:S(2)}, u32[]{:S(2)}) collective-permute-start(bf16[128,1152]{1,0:T(8,128)(2,1)S(1)} %get-tuple-element.104), channel_id=1, source_target_pairs={{0,4},{1,5},{2,6},{3,7},{4,0},{5,1},{6,2},{7,3},{8,12},{9,13},{10,... | collective-permute-start | bytes 884744 | tf_op jit(solution)/shard_map/ppermute | solution.py:566
  136.9 13.9 %collective-permute-start.17 = (bf16[128,1152]{1,0:T(8,128)(2,1)S(1)}, bf16[128,1152]{1,0:T(8,128)(2,1)S(1)}, u32[]{:S(2)}, u32[]{:S(2)}) collective-permute-start(bf16[128,1152]{1,0:T(8,128)(2,1)S(1)} %get-tuple-element.103), channel_id=1, source_target_pairs={{0,6},{1,7},{2,4},{3,5},{4,2},{5,3},{6,0},{7,1},{8,14},{9,15},{10,... | collective-permute-start | bytes 884744 | tf_op jit(solution)/shard_map/ppermute | solution.py:566
  151.9 7.2 %collective-permute-start.19 = (bf16[32,1152]{1,0:T(8,128)(2,1)S(1)}, bf16[32,1152]{1,0:T(8,128)(2,1)S(1)}, u32[]{:S(2)}, u32[]{:S(2)}) collective-permute-start(bf16[32,1152]{1,0:T(8,128)(2,1)S(1)} %get-tuple-element.107), channel_id=1, source_target_pairs={{0,16},{1,17},{2,18},{3,19},{4,20},{5,21},{6,22},{7,23},{8,24},{9,... | collective-permute-start | bytes 221192 | tf_op jit(solution)/shard_map/ppermute | solution.py:566
  155.1 6.2 %collective-permute-start.20 = (bf16[32,1152]{1,0:T(8,128)(2,1)S(1)}, bf16[32,1152]{1,0:T(8,128)(2,1)S(1)}, u32[]{:S(2)}, u32[]{:S(2)}) collective-permute-start(bf16[32,1152]{1,0:T(8,128)(2,1)S(1)} %get-tuple-element.106), channel_id=1, source_target_pairs={{0,24},{1,25},{2,26},{3,27},{4,28},{5,29},{6,30},{7,31},{8,16},{9,... | collective-permute-start | bytes 221192 | tf_op jit(solution)/shard_map/ppermute | solution.py:566
  161.4 5.3 %collective-permute-start.22 = (bf16[32,1152]{1,0:T(8,128)(2,1)S(1)}, bf16[32,1152]{1,0:T(8,128)(2,1)S(1)}, u32[]{:S(2)}, u32[]{:S(2)}) collective-permute-start(bf16[32,1152]{1,0:T(8,128)(2,1)S(1)} %fusion.4), channel_id=1, source_target_pairs={{0,16},{1,17},{2,18},{3,19},{4,20},{5,21},{6,22},{7,23},{8,24},{9,... | collective-permute-start | bytes 221192 | tf_op jit(solution)/shard_map/ppermute | solution.py:566
  163.0 6.2 %collective-permute-start.23 = (bf16[32,1152]{1,0:T(8,128)(2,1)S(1)}, bf16[32,1152]{1,0:T(8,128)(2,1)S(1)}, u32[]{:S(2)}, u32[]{:S(2)}) collective-permute-start(bf16[32,1152]{1,0:T(8,128)(2,1)S(1)} %fusion.4), channel_id=1, source_target_pairs={{0,24},{1,25},{2,26},{3,27},{4,28},{5,29},{6,30},{7,31},{8,16},{9,... | collective-permute-start | bytes 221192 | tf_op jit(solution)/shard_map/ppermute | solution.py:566
  169.2 8.9 %collective-permute-start.24 = (bf16[128,1152]{1,0:T(8,128)(2,1)S(1)}, bf16[128,1152]{1,0:T(8,128)(2,1)S(1)}, u32[]{:S(2)}, u32[]{:S(2)}) collective-permute-start(bf16[128,1152]{1,0:T(8,128)(2,1)S(1)} %pad_maximum_fusion.refs_0_), channel_id=1, source_target_pairs={{0,2},{1,3},{2,0},{3,1},{4,6},{5,7},{6,4},{7,5},{8,10},{9,11},{10,... | collective-permute-start | bytes 884744 | tf_op jit(solution)/shard_map/ppermute | solution.py:566
  170.8 11.9 %collective-permute-start.25 = (bf16[128,1152]{1,0:T(8,128)(2,1)S(1)}, bf16[128,1152]{1,0:T(8,128)(2,1)S(1)}, u32[]{:S(2)}, u32[]{:S(2)}) collective-permute-start(bf16[128,1152]{1,0:T(8,128)(2,1)S(1)} %pad_maximum_fusion.refs_0_), channel_id=1, source_target_pairs={{0,4},{1,5},{2,6},{3,7},{4,0},{5,1},{6,2},{7,3},{8,12},{9,13},{10,... | collective-permute-start | bytes 884744 | tf_op jit(solution)/shard_map/ppermute | solution.py:566
  171.7 11.0 %collective-permute-start.26 = (bf16[128,1152]{1,0:T(8,128)(2,1)S(1)}, bf16[128,1152]{1,0:T(8,128)(2,1)S(1)}, u32[]{:S(2)}, u32[]{:S(2)}) collective-permute-start(bf16[128,1152]{1,0:T(8,128)(2,1)S(1)} %pad_maximum_fusion.refs_0_), channel_id=1, source_target_pairs={{0,6},{1,7},{2,4},{3,5},{4,2},{5,3},{6,0},{7,1},{8,14},{9,15},{10,... | collective-permute-start | bytes 884744 | tf_op jit(solution)/shard_map/ppermute | solution.py:566
  172.8 10.4 %collective-permute-start.27 = (bf16[128,1152]{1,0:T(8,128)(2,1)S(1)}, bf16[128,1152]{1,0:T(8,128)(2,1)S(1)}, u32[]{:S(2)}, u32[]{:S(2)}) collective-permute-start(bf16[128,1152]{1,0:T(8,128)(2,1)S(1)} %pad_maximum_fusion.refs_0_), channel_id=1, source_target_pairs={{0,1},{1,0},{2,3},{3,2},{4,5},{5,4},{6,7},{7,6},{8,9},{9,8},{10,11... | collective-permute-start | bytes 884744 | tf_op jit(solution)/shard_map/ppermute | solution.py:566
  (24 other events, 99.0 us)

commit v4 on v3

--- a/solution.py
+++ b/solution.py
@@ -13,13 +13,11 @@
 LANES = 128
 STEPS = 8
 SHIFT = 0.3
-VMEM_BYTES = 56 * 1024 * 1024
-
-
-def params(steps=1):
-    return pltpu.CompilerParams(
-        dimension_semantics=("arbitrary",) * steps, vmem_limit_bytes=VMEM_BYTES
-    )
+MIB = 1024 * 1024
+
+
+def params(mib=56):
+    return pltpu.CompilerParams(vmem_limit_bytes=mib * MIB)
 
 
 def cost(flops, read):
@@ -116,7 +114,7 @@
         ],
         out_shape=jax.ShapeDtypeStruct((count, width), BF16),
         scratch_shapes=[pltpu.VMEM((count, width), F32)],
-        compiler_params=pltpu.CompilerParams(vmem_limit_bytes=VMEM_BYTES),
+        compiler_params=params(),
         cost_estimate=cost(2 * rows * count * width, 2 * width * (rows + count)),
         name="send",
     )(send_rows, y)
@@ -172,7 +170,7 @@
     rows, width = y.shape[0] // parts, y.shape[1]
     per = src.shape[1]
     members = per // pairs
-    groups = min(32, src.shape[0] // parts)
+    groups = min(64, src.shape[0] // parts)
     tile = groups * members
     skip = part * (rows // tile)
     sums = [
@@ -220,31 +218,32 @@
     count, width = got.shape
     return pl.pallas_call(
         functools.partial(back_kernel, shift),
+        in_specs=[pl.BlockSpec(memory_space=pltpu.VMEM)] * 3,
         out_shape=[
             jax.ShapeDtypeStruct((count, width), BF16),
             jax.ShapeDtypeStruct((width, width), F32),
         ],
-        compiler_params=pltpu.CompilerParams(vmem_limit_bytes=VMEM_BYTES),
+        compiler_params=params(),
         cost_estimate=cost(4 * count * width * width, 6 * count * width),
         name="back",
     )(got, sums, square)
 
 
-def own_kernel(nodes, part, count, weights_ref, scaled_ref, got_ref, matrix_ref, own_ref, inverse_ref):
+def own_kernel(nodes, done, count, weights_ref, scaled_ref, got_ref, matrix_ref, own_ref, inverse_ref):
     width = inverse_ref.shape[0]
     each = width // STEPS
 
     @pl.when(pl.program_id(0) == 0)
     def _():
         matrix = matrix_ref[...]
-        inverse_ref[...] = matrix * (1.0 / nodes) if part == 0 else matrix
+        inverse_ref[...] = matrix if done else matrix * (1.0 / nodes)
 
     for step in range(count):
 
         @pl.when(pl.program_id(0) == step)
         def _():
             own_ref[...] = scaled_ref[...] - dot(weights_ref[...], got_ref[...])
-            start = (part * count + step) * each
+            start = (done + step) * each
             inverse_ref[...] = eliminate(inverse_ref[...], start, each)
 
 
@@ -267,17 +266,16 @@
     return matrix
 
 
-def own_of(weights, scaled, got, matrix, nodes, part, parts, skip, rows):
+def own_of(weights, scaled, got, matrix, nodes, done, steps, skip, tile):
     count, width = got.shape
-    steps = STEPS // parts
-    tile = rows // steps
-    return pl.pallas_call(
-        functools.partial(own_kernel, nodes, part, steps),
+    rows = steps * tile
+    return pl.pallas_call(
+        functools.partial(own_kernel, nodes, done, steps),
         grid=(steps,),
         in_specs=[
-            pl.BlockSpec((tile, count), lambda i: (i + skip // tile, 0)),
-            pl.BlockSpec((tile, width), lambda i: (i + skip // tile, 0)),
-            pl.BlockSpec((count, width), lambda i: (0, 0)),
+            pl.BlockSpec((tile, count), lambda i: (i + skip, 0)),
+            pl.BlockSpec((tile, width), lambda i: (i + skip, 0)),
+            pl.BlockSpec(memory_space=pltpu.VMEM),
             pl.BlockSpec((width, width), lambda i: (0, 0)),
         ],
         out_specs=[
@@ -324,19 +322,19 @@
     return (both[:, :width] + both[:, width:] + rest).astype(BF16)
 
 
-def grad_y_kernel(nodes, scale, shift, parts, *refs):
+def grad_y_kernel(nodes, scale, shift, places, *refs):
+    parts = len(places)
     own_refs = refs[:parts]
     y_ref, index_ref, returned_ref, inverse_ref, spread_ref, out_ref, right_ref = refs[parts:]
     tile = y_ref.shape[0]
-    each = pl.num_programs(0) // parts
 
     @pl.when(pl.program_id(0) == 0)
     def _():
         set_right(nodes, scale, inverse_ref, spread_ref, right_ref)
 
-    for part, own_ref in enumerate(own_refs):
-
-        @pl.when(pl.program_id(0) // each == part)
+    for place, own_ref in zip(places, own_refs):
+
+        @pl.when(in_span(*place))
         def _():
             out_ref[...] = grad_y_rows(
                 shift, pl.program_id(0) * tile, own_ref[...], y_ref[...], index_ref[...],
@@ -344,20 +342,31 @@
             )
 
 
-def part_block(tile, width, part, each):
-    return pl.BlockSpec((tile, width), lambda i: (jnp.clip(i - part * each, 0, each - 1), 0))
+def spans(arrays, tile):
+    result, first = [], 0
+    for x in arrays:
+        result.append((first, x.shape[0] // tile))
+        first += x.shape[0] // tile
+    return result
+
+
+def span_block(tile, width, first, each):
+    return pl.BlockSpec((tile, width), lambda i: (jnp.clip(i - first, 0, each - 1), 0))
+
+
+def in_span(first, each):
+    return (pl.program_id(0) >= first) & (pl.program_id(0) < first + each)
 
 
 def grad_y_of(own, y, send_rows, returned, inverse, spread, shift, nodes, scale):
     rows, width = y.shape
     count = returned.shape[0]
-    parts = len(own)
-    tile = min(512, rows // parts)
-    each = rows // tile // parts
-    return pl.pallas_call(
-        functools.partial(grad_y_kernel, nodes, scale, shift, parts),
+    tile = min(512, own[0].shape[0])
+    places = spans(own, tile)
+    return pl.pallas_call(
+        functools.partial(grad_y_kernel, nodes, scale, shift, places),
         grid=(rows // tile,),
-        in_specs=[part_block(tile, width, part, each) for part in range(parts)]
+        in_specs=[span_block(tile, width, *place) for place in places]
         + [
             pl.BlockSpec((tile, width), lambda i: (i, 0)),
             pl.BlockSpec((1, count), lambda i: (0, 0)),
@@ -436,14 +445,14 @@
     )(features, hidden, slope, gy, w_out)
 
 
-def packed_kernel(nodes, scale, shift, n, parts, *refs):
+def packed_kernel(nodes, scale, shift, n, places, *refs):
+    parts = len(places)
     own_refs = refs[:parts]
     y_ref, index_ref, returned_ref, inverse_ref, spread_ref = refs[parts:parts + 5]
     x_ref, hidden_ref, slope_ref, w_out_ref, me_ref = refs[parts + 5:parts + 10]
     *outs, g_in, g_out, gy_ref, right_ref = refs[parts + 10:]
     tile = y_ref.shape[0]
     some = min(512, tile)
-    each = pl.num_programs(0) // parts
 
     @pl.when(pl.program_id(0) == 0)
     def _():
@@ -451,9 +460,9 @@
         g_in[...] = jnp.zeros_like(g_in)
         g_out[...] = jnp.zeros_like(g_out)
 
-    for part, own_ref in enumerate(own_refs):
-
-        @pl.when(pl.program_id(0) // each == part)
+    for place, own_ref in zip(places, own_refs):
+
+        @pl.when(in_span(*place))
         def _():
             for at in range(0, tile, some):
                 gy_ref[at:at + some, :] = grad_y_rows(
@@ -484,21 +493,20 @@
     rows, din = features.shape
     units, width = w_out.shape
     count = returned.shape[0]
-    parts = len(own)
-    tile = min(1024, rows // parts)
-    each = rows // tile // parts
+    tile = min(1024, own[0].shape[0])
+    places = spans(own, tile)
     shapes = [
         jax.ShapeDtypeStruct((din // 2, units + width), F32),
         jax.ShapeDtypeStruct((din // 2, units + width), BF16),
     ]
     return pl.pallas_call(
-        functools.partial(packed_kernel, nodes, scale, shift, n, parts),
+        functools.partial(packed_kernel, nodes, scale, shift, n, places),
         grid=(rows // tile,),
-        in_specs=[part_block(tile, width, part, each) for part in range(parts)]
+        in_specs=[span_block(tile, width, *place) for place in places]
         + [
             pl.BlockSpec((tile, width), lambda i: (i, 0)),
             pl.BlockSpec((1, count), lambda i: (0, 0)),
-            pl.BlockSpec((count, width), lambda i: (0, 0)),
+            pl.BlockSpec(memory_space=pltpu.VMEM),
             pl.BlockSpec((width, width), lambda i: (0, 0)),
             pl.BlockSpec((width, width), lambda i: (0, 0)),
             pl.BlockSpec((tile, din), lambda i: (i, 0)),
@@ -515,7 +523,7 @@
             pltpu.VMEM((tile, width), BF16),
             pltpu.VMEM((2 * width, 2 * width), BF16),
         ],
-        compiler_params=params(),
+        compiler_params=params(50),
         cost_estimate=cost(2 * rows * units * (din + 2 * width), 2 * rows * (din + 3 * units)),
         name="packed_grads",
     )(
@@ -541,7 +549,7 @@
 
 
 def unpack(pieces, spots, places, lows, me, shapes):
-    held = pl.BlockSpec(pieces[0].shape, lambda i, *_: (0, 0))
+    held = pl.BlockSpec(memory_space=pltpu.VMEM)
 
     def spot(i, me_ref):
         value = sum(jnp.where(i == k, x // 2, 0) for k, x in enumerate(spots))
@@ -556,7 +564,7 @@
             out_specs=[pl.BlockSpec((x.shape[0], 2) + x.shape[2:], spot) for x in shapes],
         ),
         out_shape=shapes,
-        compiler_params=params(),
+        compiler_params=params(12),
         cost_estimate=cost(1e9, 0),
         name="unpack",
     )(me, *pieces)
@@ -653,17 +661,18 @@
     returned = lax.all_to_all(back, "dp", split_axis=0, concat_axis=0, tiled=True)
     matrix, _ = lax.optimization_barrier((gram, back))
     own, marks = [], []
-    cuts = 4 if rows % (4 * 256) == 0 else 1
-    for cut in range(cuts):
-        part, skip = divmod(cut * (rows // cuts), rows // parts)
+    half = STEPS // parts
+    cuts = [(0, 2), (2, 2), (4, 4)] if parts == 2 else [(0, STEPS)]
+    for done, taken in cuts:
+        part, skip = divmod(done, half)
         piece, matrix = own_of(
-            weights[part], scaled[part], got, matrix, nodes, cut, cuts, skip, rows // cuts
+            weights[part], scaled[part], got, matrix, nodes, done, taken, skip, rows // STEPS
         )
         own.append(piece)
         marks.append(matrix)
     steps = [None] if n_dp & (n_dp - 1) else radices(n_dp)
     for k, step in enumerate(steps):
-        spread = sum_step(spread, "dp", n_dp, step, marks[min(k, cuts - 1)])
+        spread = sum_step(spread, "dp", n_dp, step, marks[min(k, len(marks) - 1)])
     if n_mp > 1:
         spread = lax.psum(spread, "mp")
     packable = n_dp & (n_dp - 1) == 0 and n_dp > 2 and din == units and din % (16 * n_dp) == 0

time: 190 us -> 185 us (0.974)
  Pallas kernels: 94.9 us -> 90 us
    pallas_call x5 -> x4, Pallas kernels: 19.6 us -> 18.3 us  [the longest x3 14.9 us: own_of(): pl.pallas_call(functools.partial(own_kernel, nodes, done, steps), grid=(s...]
  transfers between devices with their start and end apart: 33 -> 33, of which waited for: 13 -> 13; matrix products, arithmetic and copies ran while one was open for 3% -> 3% of each run, Pallas kernels for 19% -> 18%
where the time goes in v4:
time: 185 us
  Pallas kernels  90 us (49%)
  starting transfers between devices  46.5 us (25%)
  waiting for transfers between devices  36.9 us (20%)
  local copies, waits for them, and re-layouts  7.27 us (4%)
  other arithmetic  2.93 us (2%)
    ppermute x31, waiting for transfers between devices, exchange(): return lax.ppermute(value, axis, [(i, i ^ mask) for i in range(n)])  36.9 us
    ppermute x31, starting transfers between devices, exchange(): return lax.ppermute(value, axis, [(i, i ^ mask) for i in range(n)])  33.5 us
    pallas_call x1, Pallas kernels, packed_grads(): pl.pallas_call(functools.partial(packed_kernel, nodes, scale, shift, n, p...  27 us
    pallas_call x2, Pallas kernels, weights_of(): pl.pallas_call(functools.partial(weights_kernel, pairs, part == 0), grid=...  19.1 us
    pallas_call x1, Pallas kernels, forward(): pl.pallas_call(forward_kernel, grid=(nodes // tile,), in_specs=[pl.BlockS...  18.3 us
    pallas_call x3, Pallas kernels, own_of(): pl.pallas_call(functools.partial(own_kernel, nodes, done, steps), grid=(s...  14.9 us
    all_to_all x1, starting transfers between devices, shards(): got = lax.all_to_all(sent, 'dp', split_axis=0, concat_axis=0, tiled=True)  7.14 us
    all_to_all x1, starting transfers between devices, shards(): lax.all_to_all(back, 'dp', split_axis=0, concat_axis=0, tiled=True)  5.88 us
  transfers between devices with their start and end apart: 33, of which 13 were waited for; matrix products, arithmetic and copies ran while one was open for 3% of the time, Pallas kernels for 18%

profile of v4, /device:TPU:0, one launch (start us, length us, event | category | flops | bytes accessed | tf_op | source)
XLA Modules:
  0.0 184.6 jit_solution(16749988544569556245)
XLA Ops:
  0.6 18.3 %forward.1 = (bf16[4096,1024]{1,0:T(8,128)(2,1)}, f32[4096,1024]{1,0:T(8,128)}, f32[4096,128]{1,0:T(8,128)}, bf16[4096,128]{1,0:T(8,128)(2,1)}, f32[128,128]{1,0:T(8,128)}) custom-call(bf16[4096,1024]{1,0:T(8,128)(2,1)} %refs_8_.1, bf16[1024,1024]{1,0:T(8,128)(2,1)} %w_in_ref.1, bf16[1024,128]{1,0:T(8,128)(2,1)} %refs_11_.1), custom_call_target="tpu_custom_call" | custom-call | flops 9663676416 | bytes 25165824 | tf_op jit(solution)/shard_map/forward/pallas_call | solution.py:66
  19.5 4.7 %send.1 = bf16[2048,128]{1,0:T(8,128)(2,1)} custom-call(s32[2048]{0:T(1024)} %index_ref.1, f32[4096,128]{1,0:T(8,128)} %get-tuple-element.48.y_ref.refs_2_.refs_3_), custom_call_target="tpu_custom_call" | custom-call | flops 2147483648 | bytes 1572864 | tf_op jit(solution)/shard_map/send/pallas_call | solution.py:109
  24.2 7.1 %all-to-all-start = ((bf16[32,64,128]{2,1,0:T(8,128)(2,1)}), bf16[32,64,128]{2,1,0:T(8,128)(2,1)S(1)}, u32[]{:S(2)}, u32[]{:S(2)}) async-start(bf16[32,64,128]{2,1,0:T(8,128)(2,1)} %bitcast.15), calls=%async_computation | async-start | bytes 1048576 | tf_op jit(solution)/shard_map/all_to_all | solution.py:643
  39.3 9.3 %weights.2 = (bf16[2048,2048]{1,0:T(8,128)(2,1)}, f32[2048,128]{1,0:T(8,128)}, f32[144,2048]{1,0:T(8,128)}, f32[128,128]{1,0:T(8,128)}) custom-call(s32[256,256]{1,0:T(8,128)} %reshape.27.refs_0_, f32[256,256]{1,0:T(8,128)} %reshape.28.refs_1_, f32[4096,128]{1,0:T(8,128)} %get-tuple-element.48.y_ref.refs_2_.refs_3_, bf16[4096,128]{1,0:T(8,128)(2,1)} %get-tuple-element.59.refs_3_), custom_call_target="tpu_custom_call" | custom-call | flops 2147483648 | bytes 8388608 | tf_op jit(solution)/shard_map/weights/pallas_call | solution.py:181
  50.3 2.4 %collective-permute-start.5 = (f32[128,128]{1,0:T(8,128)S(1)}, f32[128,128]{1,0:T(8,128)S(1)}, u32[]{:S(2)}, u32[]{:S(2)}) collective-permute-start(f32[128,128]{1,0:T(8,128)S(1)} %add_add_fusion.3), channel_id=1, source_target_pairs={{0,16},{1,17},{2,18},{3,19},{4,20},{5,21},{6,22},{7,23},{8,24},{9,... | collective-permute-start | bytes 196616 | tf_op jit(solution)/shard_map/ppermute | solution.py:574
  53.1 9.7 %weights.3 = (bf16[2048,2048]{1,0:T(8,128)(2,1)}, f32[2048,128]{1,0:T(8,128)}, f32[144,2048]{1,0:T(8,128)}, f32[128,128]{1,0:T(8,128)}) custom-call(s32[256,256]{1,0:T(8,128)} %reshape.27.refs_0_, f32[256,256]{1,0:T(8,128)} %reshape.28.refs_1_, f32[4096,128]{1,0:T(8,128)} %get-tuple-element.48.y_ref.refs_2_.refs_3_, ...), custom_call_target="tpu_custom_call" | custom-call | flops 2147483648 | bytes 8388608 | tf_op jit(solution)/shard_map/weights/pallas_call | solution.py:181
  64.4 3.4 %back.1 = (bf16[2048,128]{1,0:T(8,128)(2,1)}, f32[128,128]{1,0:T(8,128)}) custom-call(bf16[2048,128]{1,0:T(8,128)(2,1)} %bitcast.10, f32[144,2048]{1,0:T(8,128)} %get-tuple-element.68.sums_ref, f32[128,128]{1,0:T(8,128)} %get-tuple-element.69.square_ref), custom_call_target="tpu_custom_call" | custom-call | flops 134217728 | bytes 1572864 | tf_op jit(solution)/shard_map/back/pallas_call | solution.py:219
  67.8 5.9 %all-to-all-start.1 = ((bf16[32,64,128]{2,1,0:T(8,128)(2,1)}), bf16[32,64,128]{2,1,0:T(8,128)(2,1)S(1)}, u32[]{:S(2)}, u32[]{:S(2)}) async-start(bf16[32,64,128]{2,1,0:T(8,128)(2,1)} %bitcast.14), calls=%async_computation.1 | async-start | bytes 1048576 | tf_op jit(solution)/shard_map/all_to_all | solution.py:661
  73.8 4.1 %own.3 = (f32[1024,128]{1,0:T(8,128)}, f32[128,128]{1,0:T(8,128)}) custom-call(bf16[2048,2048]{1,0:T(8,128)(2,1)} %get-tuple-element.53.weights_ref, f32[2048,128]{1,0:T(8,128)} %get-tuple-element.54.scaled_ref, bf16[2048,128]{1,0:T(8,128)(2,1)} %bitcast.11, f32[128,128]{1,0:T(8,128)} %add_add_fusion.2.matrix_ref), custom_call_target="tpu_custom_call" | custom-call | flops 536870912 | bytes 4194304 | tf_op jit(solution)/shard_map/own/pallas_call | solution.py:272
  77.9 2.6 %collective-permute-start.10 = (f32[128,128]{1,0:T(8,128)S(1)}, f32[128,128]{1,0:T(8,128)S(1)}, u32[]{:S(2)}, u32[]{:S(2)}) collective-permute-start(f32[128,128]{1,0:T(8,128)S(1)} %add.70), channel_id=1, source_target_pairs={{0,6},{1,7},{2,4},{3,5},{4,2},{5,3},{6,0},{7,1},{8,14},{9,15},{10,... | collective-permute-start | bytes 196616 | tf_op jit(solution)/shard_map/ppermute | solution.py:574
  81.4 4.0 %own.4 = (f32[1024,128]{1,0:T(8,128)}, f32[128,128]{1,0:T(8,128)}) custom-call(bf16[2048,2048]{1,0:T(8,128)(2,1)} %get-tuple-element.53.weights_ref, f32[2048,128]{1,0:T(8,128)} %get-tuple-element.54.scaled_ref, bf16[2048,128]{1,0:T(8,128)(2,1)} %bitcast.12, f32[128,128]{1,0:T(8,128)} %get-tuple-element.73.matrix_ref), custom_call_target="tpu_custom_call" | custom-call | flops 536870912 | bytes 4194304 | tf_op jit(solution)/shard_map/own/pallas_call | solution.py:272
  85.9 2.2 %collective-permute-start.11 = (f32[128,128]{1,0:T(8,128)S(1)}, f32[128,128]{1,0:T(8,128)S(1)}, u32[]{:S(2)}, u32[]{:S(2)}) collective-permute-start(f32[128,128]{1,0:T(8,128)S(1)} %add_add_fusion.1), channel_id=1, source_target_pairs={{0,8},{1,9},{2,10},{3,11},{4,12},{5,13},{6,14},{7,15},{8,0},{9,1},... | collective-permute-start | bytes 196616 | tf_op jit(solution)/shard_map/ppermute | solution.py:574
  90.7 6.8 %own.5 = (f32[2048,128]{1,0:T(8,128)}, f32[128,128]{1,0:T(8,128)}) custom-call(bf16[2048,2048]{1,0:T(8,128)(2,1)} %get-tuple-element.75.weights_ref, f32[2048,128]{1,0:T(8,128)} %get-tuple-element.76.scaled_ref, bf16[2048,128]{1,0:T(8,128)(2,1)} %bitcast.13, f32[128,128]{1,0:T(8,128)} %get-tuple-element.77.matrix_ref), custom_call_target="tpu_custom_call" | custom-call | flops 1073741824 | bytes 8388608 | tf_op jit(solution)/shard_map/own/pallas_call | solution.py:272
  99.7 27.0 %packed_grads.1 = (f32[512,1152]{1,0:T(8,128)}, bf16[512,1152]{1,0:T(8,128)(2,1)}) custom-call(f32[1024,128]{1,0:T(8,128)S(1)} %copy-done.1, f32[1024,128]{1,0:T(8,128)S(1)} %copy-done.2, f32[2048,128]{1,0:T(8,128)S(1)} %copy-done, f32[4096,128]{1,0:T(8,128)} %get-tuple-element.48.y_ref.refs_2_.refs_3_, s32[1,2048]{1,0:T(1,128)S(1)} %bitcast.9, ...), custom_call_target="tpu_custom_call" | custom-call | flops 10737418240 | bytes 33554432 | tf_op jit(solution)/shard_map/packed_grads/pallas_call | solution.py:502
  126.7 3.1 %collective-permute-done.14 = bf16[512,1152]{1,0:T(8,128)(2,1)S(1)} collective-permute-done((bf16[512,1152]{1,0:T(8,128)(2,1)}, bf16[512,1152]{1,0:T(8,128)(2,1)S(1)}, u32[]{:S(2)}, u32[]{:S(2)}) %collective-permute-start.14) | collective-permute-done | bytes 1179680 | tf_op jit(solution)/shard_map/ppermute | solution.py:574
  135.3 6.4 %collective-permute-done.15 = bf16[128,1152]{1,0:T(8,128)(2,1)S(1)} collective-permute-done((bf16[128,1152]{1,0:T(8,128)(2,1)S(1)}, bf16[128,1152]{1,0:T(8,128)(2,1)S(1)}, u32[]{:S(2)}, u32[]{:S(2)}) %collective-permute-start.15) | collective-permute-done | bytes 294944 | tf_op jit(solution)/shard_map/ppermute | solution.py:574
  141.7 6.4 %collective-permute-done.16 = bf16[128,1152]{1,0:T(8,128)(2,1)S(1)} collective-permute-done((bf16[128,1152]{1,0:T(8,128)(2,1)S(1)}, bf16[128,1152]{1,0:T(8,128)(2,1)S(1)}, u32[]{:S(2)}, u32[]{:S(2)}) %collective-permute-start.16) | collective-permute-done | bytes 294944 | tf_op jit(solution)/shard_map/ppermute | solution.py:574
  149.1 3.2 %collective-permute-start.19 = (bf16[32,1152]{1,0:T(8,128)(2,1)S(1)}, bf16[32,1152]{1,0:T(8,128)(2,1)S(1)}, u32[]{:S(2)}, u32[]{:S(2)}) collective-permute-start(bf16[32,1152]{1,0:T(8,128)(2,1)S(1)} %get-tuple-element.103), channel_id=1, source_target_pairs={{0,16},{1,17},{2,18},{3,19},{4,20},{5,21},{6,22},{7,23},{8,24},{9,... | collective-permute-start | bytes 221192 | tf_op jit(solution)/shard_map/ppermute | solution.py:574
  153.1 3.3 %collective-permute-done.19 = bf16[32,1152]{1,0:T(8,128)(2,1)S(1)} collective-permute-done((bf16[32,1152]{1,0:T(8,128)(2,1)S(1)}, bf16[32,1152]{1,0:T(8,128)(2,1)S(1)}, u32[]{:S(2)}, u32[]{:S(2)}) %collective-permute-start.19) | collective-permute-done | bytes 73760 | tf_op jit(solution)/shard_map/ppermute | solution.py:574
  160.3 2.7 %collective-permute-start.23 = (bf16[32,1152]{1,0:T(8,128)(2,1)S(1)}, bf16[32,1152]{1,0:T(8,128)(2,1)S(1)}, u32[]{:S(2)}, u32[]{:S(2)}) collective-permute-start(bf16[32,1152]{1,0:T(8,128)(2,1)S(1)} %fusion.4), channel_id=1, source_target_pairs={{0,24},{1,25},{2,26},{3,27},{4,28},{5,29},{6,30},{7,31},{8,16},{9,... | collective-permute-start | bytes 221192 | tf_op jit(solution)/shard_map/ppermute | solution.py:574
  164.0 2.5 %collective-permute-done.23 = bf16[32,1152]{1,0:T(8,128)(2,1)S(1)} collective-permute-done((bf16[32,1152]{1,0:T(8,128)(2,1)S(1)}, bf16[32,1152]{1,0:T(8,128)(2,1)S(1)}, u32[]{:S(2)}, u32[]{:S(2)}) %collective-permute-start.23) | collective-permute-done | bytes 73760 | tf_op jit(solution)/shard_map/ppermute | solution.py:574
  170.1 5.3 %collective-permute-done.24.refs_1_ = bf16[128,1152]{1,0:T(8,128)(2,1)S(1)} collective-permute-done((bf16[128,1152]{1,0:T(8,128)(2,1)S(1)}, bf16[128,1152]{1,0:T(8,128)(2,1)S(1)}, u32[]{:S(2)}, u32[]{:S(2)}) %collective-permute-start.24) | collective-permute-done | bytes 294944 | tf_op jit(solution)/shard_map/ppermute | solution.py:574
  175.4 4.6 %collective-permute-done.25.refs_2_ = bf16[128,1152]{1,0:T(8,128)(2,1)S(1)} collective-permute-done((bf16[128,1152]{1,0:T(8,128)(2,1)S(1)}, bf16[128,1152]{1,0:T(8,128)(2,1)S(1)}, u32[]{:S(2)}, u32[]{:S(2)}) %collective-permute-start.25) | collective-permute-done | bytes 294944 | tf_op jit(solution)/shard_map/ppermute | solution.py:574
  182.0 2.6 %unpack.1 = (f32[4,8,32,1024]{3,2,1,0:T(8,128)}, f32[4,8,32,128]{3,2,1,0:T(8,128)}) custom-call(s32[1]{0:T(128)} %bitcast.refs_12_.me_ref, bf16[128,1152]{1,0:T(8,128)(2,1)S(1)} %pad_maximum_fusion.refs_0_, bf16[128,1152]{1,0:T(8,128)(2,1)S(1)} %collective-permute-done.24.refs_1_, bf16[128,1152]{1,0:T(8,128)(2,1)S(1)} %collective-permute-done.25.refs_2_, ...), custom_call_target="tpu_custom_call" | custom-call | flops 1000000000 | tf_op jit(solution)/shard_map/unpack/pallas_call | solution.py:558
  (93 shorter events, 35.8 us)
Async XLA Ops:
  19.0 16.8 %collective-permute-start = (f32[128,128]{1,0:T(8,128)}, f32[128,128]{1,0:T(8,128)S(1)}, u32[]{:S(2)}, u32[]{:S(2)}) collective-permute-start(f32[128,128]{1,0:T(8,128)} %get-tuple-element.49), channel_id=1, source_target_pairs={{0,1},{1,0},{2,3},{3,2},{4,5},{5,4},{6,7},{7,6},{8,9},{9,8},{10,11... | collective-permute-start | bytes 196616 | tf_op jit(solution)/shard_map/ppermute | solution.py:574
  24.2 39.4 %all-to-all-start = ((bf16[32,64,128]{2,1,0:T(8,128)(2,1)}), bf16[32,64,128]{2,1,0:T(8,128)(2,1)S(1)}, u32[]{:S(2)}, u32[]{:S(2)}) async-start(bf16[32,64,128]{2,1,0:T(8,128)(2,1)} %bitcast.15), calls=%async_computation | async-start | bytes 1048576 | tf_op jit(solution)/shard_map/all_to_all | solution.py:643
  35.8 12.9 %collective-permute-start.1 = (f32[128,128]{1,0:T(8,128)S(1)}, f32[128,128]{1,0:T(8,128)S(1)}, u32[]{:S(2)}, u32[]{:S(2)}) collective-permute-start(f32[128,128]{1,0:T(8,128)S(1)} %add.63), channel_id=1, source_target_pairs={{0,2},{1,3},{2,0},{3,1},{4,6},{5,7},{6,4},{7,5},{8,10},{9,11},{10,... | collective-permute-start | bytes 196616 | tf_op jit(solution)/shard_map/ppermute | solution.py:574
  37.4 11.2 %collective-permute-start.2 = (f32[128,128]{1,0:T(8,128)S(1)}, f32[128,128]{1,0:T(8,128)S(1)}, u32[]{:S(2)}, u32[]{:S(2)}) collective-permute-start(f32[128,128]{1,0:T(8,128)S(1)} %add.63), channel_id=1, source_target_pairs={{0,4},{1,5},{2,6},{3,7},{4,0},{5,1},{6,2},{7,3},{8,12},{9,13},{10,... | collective-permute-start | bytes 196616 | tf_op jit(solution)/shard_map/ppermute | solution.py:574
  38.9 9.8 %collective-permute-start.3 = (f32[128,128]{1,0:T(8,128)S(1)}, f32[128,128]{1,0:T(8,128)S(1)}, u32[]{:S(2)}, u32[]{:S(2)}) collective-permute-start(f32[128,128]{1,0:T(8,128)S(1)} %add.63), channel_id=1, source_target_pairs={{0,6},{1,7},{2,4},{3,5},{4,2},{5,3},{6,0},{7,1},{8,14},{9,15},{10,... | collective-permute-start | bytes 196616 | tf_op jit(solution)/shard_map/ppermute | solution.py:574
  48.7 14.2 %collective-permute-start.4 = (f32[128,128]{1,0:T(8,128)S(1)}, f32[128,128]{1,0:T(8,128)S(1)}, u32[]{:S(2)}, u32[]{:S(2)}) collective-permute-start(f32[128,128]{1,0:T(8,128)S(1)} %add_add_fusion.3), channel_id=1, source_target_pairs={{0,8},{1,9},{2,10},{3,11},{4,12},{5,13},{6,14},{7,15},{8,0},{9,1},... | collective-permute-start | bytes 196616 | tf_op jit(solution)/shard_map/ppermute | solution.py:574
  50.3 12.6 %collective-permute-start.5 = (f32[128,128]{1,0:T(8,128)S(1)}, f32[128,128]{1,0:T(8,128)S(1)}, u32[]{:S(2)}, u32[]{:S(2)}) collective-permute-start(f32[128,128]{1,0:T(8,128)S(1)} %add_add_fusion.3), channel_id=1, source_target_pairs={{0,16},{1,17},{2,18},{3,19},{4,20},{5,21},{6,22},{7,23},{8,24},{9,... | collective-permute-start | bytes 196616 | tf_op jit(solution)/shard_map/ppermute | solution.py:574
  52.8 10.1 %collective-permute-start.6 = (f32[128,128]{1,0:T(8,128)S(1)}, f32[128,128]{1,0:T(8,128)S(1)}, u32[]{:S(2)}, u32[]{:S(2)}) collective-permute-start(f32[128,128]{1,0:T(8,128)S(1)} %add_add_fusion.3), channel_id=1, source_target_pairs={{0,24},{1,25},{2,26},{3,27},{4,28},{5,29},{6,30},{7,31},{8,16},{9,... | collective-permute-start | bytes 196616 | tf_op jit(solution)/shard_map/ppermute | solution.py:574
  67.8 29.8 %all-to-all-start.1 = ((bf16[32,64,128]{2,1,0:T(8,128)(2,1)}), bf16[32,64,128]{2,1,0:T(8,128)(2,1)S(1)}, u32[]{:S(2)}, u32[]{:S(2)}) async-start(bf16[32,64,128]{2,1,0:T(8,128)(2,1)} %bitcast.14), calls=%async_computation.1 | async-start | bytes 1048576 | tf_op jit(solution)/shard_map/all_to_all | solution.py:661
  77.9 7.6 %collective-permute-start.10 = (f32[128,128]{1,0:T(8,128)S(1)}, f32[128,128]{1,0:T(8,128)S(1)}, u32[]{:S(2)}, u32[]{:S(2)}) collective-permute-start(f32[128,128]{1,0:T(8,128)S(1)} %add.70), channel_id=1, source_target_pairs={{0,6},{1,7},{2,4},{3,5},{4,2},{5,3},{6,0},{7,1},{8,14},{9,15},{10,... | collective-permute-start | bytes 196616 | tf_op jit(solution)/shard_map/ppermute | solution.py:574
  85.9 11.6 %collective-permute-start.11 = (f32[128,128]{1,0:T(8,128)S(1)}, f32[128,128]{1,0:T(8,128)S(1)}, u32[]{:S(2)}, u32[]{:S(2)}) collective-permute-start(f32[128,128]{1,0:T(8,128)S(1)} %add_add_fusion.1), channel_id=1, source_target_pairs={{0,8},{1,9},{2,10},{3,11},{4,12},{5,13},{6,14},{7,15},{8,0},{9,1},... | collective-permute-start | bytes 196616 | tf_op jit(solution)/shard_map/ppermute | solution.py:574
  88.2 9.4 %collective-permute-start.12 = (f32[128,128]{1,0:T(8,128)S(1)}, f32[128,128]{1,0:T(8,128)S(1)}, u32[]{:S(2)}, u32[]{:S(2)}) collective-permute-start(f32[128,128]{1,0:T(8,128)S(1)} %add_add_fusion.1), channel_id=1, source_target_pairs={{0,16},{1,17},{2,18},{3,19},{4,20},{5,21},{6,22},{7,23},{8,24},{9,... | collective-permute-start | bytes 196616 | tf_op jit(solution)/shard_map/ppermute | solution.py:574
  89.8 7.7 %collective-permute-start.13 = (f32[128,128]{1,0:T(8,128)S(1)}, f32[128,128]{1,0:T(8,128)S(1)}, u32[]{:S(2)}, u32[]{:S(2)}) collective-permute-start(f32[128,128]{1,0:T(8,128)S(1)} %add_add_fusion.1), channel_id=1, source_target_pairs={{0,24},{1,25},{2,26},{3,27},{4,28},{5,29},{6,30},{7,31},{8,16},{9,... | collective-permute-start | bytes 196616 | tf_op jit(solution)/shard_map/ppermute | solution.py:574
  131.8 9.9 %collective-permute-start.15 = (bf16[128,1152]{1,0:T(8,128)(2,1)S(1)}, bf16[128,1152]{1,0:T(8,128)(2,1)S(1)}, u32[]{:S(2)}, u32[]{:S(2)}) collective-permute-start(bf16[128,1152]{1,0:T(8,128)(2,1)S(1)} %get-tuple-element.98), channel_id=1, source_target_pairs={{0,2},{1,3},{2,0},{3,1},{4,6},{5,7},{6,4},{7,5},{8,10},{9,11},{10,... | collective-permute-start | bytes 884744 | tf_op jit(solution)/shard_map/ppermute | solution.py:574
  133.0 15.1 %collective-permute-start.16 = (bf16[128,1152]{1,0:T(8,128)(2,1)S(1)}, bf16[128,1152]{1,0:T(8,128)(2,1)S(1)}, u32[]{:S(2)}, u32[]{:S(2)}) collective-permute-start(bf16[128,1152]{1,0:T(8,128)(2,1)S(1)} %get-tuple-element.100), channel_id=1, source_target_pairs={{0,4},{1,5},{2,6},{3,7},{4,0},{5,1},{6,2},{7,3},{8,12},{9,13},{10,... | collective-permute-start | bytes 884744 | tf_op jit(solution)/shard_map/ppermute | solution.py:574
  134.2 13.9 %collective-permute-start.17 = (bf16[128,1152]{1,0:T(8,128)(2,1)S(1)}, bf16[128,1152]{1,0:T(8,128)(2,1)S(1)}, u32[]{:S(2)}, u32[]{:S(2)}) collective-permute-start(bf16[128,1152]{1,0:T(8,128)(2,1)S(1)} %get-tuple-element.99), channel_id=1, source_target_pairs={{0,6},{1,7},{2,4},{3,5},{4,2},{5,3},{6,0},{7,1},{8,14},{9,15},{10,... | collective-permute-start | bytes 884744 | tf_op jit(solution)/shard_map/ppermute | solution.py:574
  149.1 7.2 %collective-permute-start.19 = (bf16[32,1152]{1,0:T(8,128)(2,1)S(1)}, bf16[32,1152]{1,0:T(8,128)(2,1)S(1)}, u32[]{:S(2)}, u32[]{:S(2)}) collective-permute-start(bf16[32,1152]{1,0:T(8,128)(2,1)S(1)} %get-tuple-element.103), channel_id=1, source_target_pairs={{0,16},{1,17},{2,18},{3,19},{4,20},{5,21},{6,22},{7,23},{8,24},{9,... | collective-permute-start | bytes 221192 | tf_op jit(solution)/shard_map/ppermute | solution.py:574
  152.4 6.2 %collective-permute-start.20 = (bf16[32,1152]{1,0:T(8,128)(2,1)S(1)}, bf16[32,1152]{1,0:T(8,128)(2,1)S(1)}, u32[]{:S(2)}, u32[]{:S(2)}) collective-permute-start(bf16[32,1152]{1,0:T(8,128)(2,1)S(1)} %get-tuple-element.102), channel_id=1, source_target_pairs={{0,24},{1,25},{2,26},{3,27},{4,28},{5,29},{6,30},{7,31},{8,16},{9,... | collective-permute-start | bytes 221192 | tf_op jit(solution)/shard_map/ppermute | solution.py:574
  158.6 5.3 %collective-permute-start.22 = (bf16[32,1152]{1,0:T(8,128)(2,1)S(1)}, bf16[32,1152]{1,0:T(8,128)(2,1)S(1)}, u32[]{:S(2)}, u32[]{:S(2)}) collective-permute-start(bf16[32,1152]{1,0:T(8,128)(2,1)S(1)} %fusion.4), channel_id=1, source_target_pairs={{0,16},{1,17},{2,18},{3,19},{4,20},{5,21},{6,22},{7,23},{8,24},{9,... | collective-permute-start | bytes 221192 | tf_op jit(solution)/shard_map/ppermute | solution.py:574
  160.3 6.2 %collective-permute-start.23 = (bf16[32,1152]{1,0:T(8,128)(2,1)S(1)}, bf16[32,1152]{1,0:T(8,128)(2,1)S(1)}, u32[]{:S(2)}, u32[]{:S(2)}) collective-permute-start(bf16[32,1152]{1,0:T(8,128)(2,1)S(1)} %fusion.4), channel_id=1, source_target_pairs={{0,24},{1,25},{2,26},{3,27},{4,28},{5,29},{6,30},{7,31},{8,16},{9,... | collective-permute-start | bytes 221192 | tf_op jit(solution)/shard_map/ppermute | solution.py:574
  166.5 8.9 %collective-permute-start.24 = (bf16[128,1152]{1,0:T(8,128)(2,1)S(1)}, bf16[128,1152]{1,0:T(8,128)(2,1)S(1)}, u32[]{:S(2)}, u32[]{:S(2)}) collective-permute-start(bf16[128,1152]{1,0:T(8,128)(2,1)S(1)} %pad_maximum_fusion.refs_0_), channel_id=1, source_target_pairs={{0,2},{1,3},{2,0},{3,1},{4,6},{5,7},{6,4},{7,5},{8,10},{9,11},{10,... | collective-permute-start | bytes 884744 | tf_op jit(solution)/shard_map/ppermute | solution.py:574
  168.0 11.9 %collective-permute-start.25 = (bf16[128,1152]{1,0:T(8,128)(2,1)S(1)}, bf16[128,1152]{1,0:T(8,128)(2,1)S(1)}, u32[]{:S(2)}, u32[]{:S(2)}) collective-permute-start(bf16[128,1152]{1,0:T(8,128)(2,1)S(1)} %pad_maximum_fusion.refs_0_), channel_id=1, source_target_pairs={{0,4},{1,5},{2,6},{3,7},{4,0},{5,1},{6,2},{7,3},{8,12},{9,13},{10,... | collective-permute-start | bytes 884744 | tf_op jit(solution)/shard_map/ppermute | solution.py:574
  168.9 11.0 %collective-permute-start.26 = (bf16[128,1152]{1,0:T(8,128)(2,1)S(1)}, bf16[128,1152]{1,0:T(8,128)(2,1)S(1)}, u32[]{:S(2)}, u32[]{:S(2)}) collective-permute-start(bf16[128,1152]{1,0:T(8,128)(2,1)S(1)} %pad_maximum_fusion.refs_0_), channel_id=1, source_target_pairs={{0,6},{1,7},{2,4},{3,5},{4,2},{5,3},{6,0},{7,1},{8,14},{9,15},{10,... | collective-permute-start | bytes 884744 | tf_op jit(solution)/shard_map/ppermute | solution.py:574
  170.1 10.4 %collective-permute-start.27 = (bf16[128,1152]{1,0:T(8,128)(2,1)S(1)}, bf16[128,1152]{1,0:T(8,128)(2,1)S(1)}, u32[]{:S(2)}, u32[]{:S(2)}) collective-permute-start(bf16[128,1152]{1,0:T(8,128)(2,1)S(1)} %pad_maximum_fusion.refs_0_), channel_id=1, source_target_pairs={{0,1},{1,0},{2,3},{3,2},{4,5},{5,4},{6,7},{7,6},{8,9},{9,8},{10,11... | collective-permute-start | bytes 884744 | tf_op jit(solution)/shard_map/ppermute | solution.py:574
  (21 other events, 97.5 us)

commit v5 on v4

--- a/solution.py
+++ b/solution.py
@@ -11,7 +11,7 @@
 F32 = jnp.float32
 BF16 = jnp.bfloat16
 LANES = 128
-STEPS = 8
+STEPS = 4
 SHIFT = 0.3
 MIB = 1024 * 1024
 
@@ -662,7 +662,8 @@
     matrix, _ = lax.optimization_barrier((gram, back))
     own, marks = [], []
     half = STEPS // parts
-    cuts = [(0, 2), (2, 2), (4, 4)] if parts == 2 else [(0, STEPS)]
+    some = STEPS // 4
+    cuts = [(0, some), (some, some), (half, half)] if parts == 2 else [(0, STEPS)]
     for done, taken in cuts:
         part, skip = divmod(done, half)
         piece, matrix = own_of(

time: 185 us -> 186 us (level)
  transfers between devices with their start and end apart: 33 -> 33, of which waited for: 13 -> 13; matrix products, arithmetic and copies ran while one was open for 3% -> 3% of each run, Pallas kernels for 18% -> 19%
where the time goes in v5:
time: 186 us; the launch traced here: 185 us
  Pallas kernels  90.6 us (49%)
  starting transfers between devices  46.2 us (25%)
  waiting for transfers between devices  37.3 us (20%)
  local copies, waits for them, and re-layouts  7.27 us (4%)
  other arithmetic  2.93 us (2%)
    ppermute x31, waiting for transfers between devices, exchange(): return lax.ppermute(value, axis, [(i, i ^ mask) for i in range(n)])  37.3 us
    ppermute x31, starting transfers between devices, exchange(): return lax.ppermute(value, axis, [(i, i ^ mask) for i in range(n)])  33.2 us
    pallas_call x1, Pallas kernels, packed_grads(): pl.pallas_call(functools.partial(packed_kernel, nodes, scale, shift, n, p...  27 us
    pallas_call x2, Pallas kernels, weights_of(): pl.pallas_call(functools.partial(weights_kernel, pairs, part == 0), grid=...  19.1 us
    pallas_call x1, Pallas kernels, forward(): pl.pallas_call(forward_kernel, grid=(nodes // tile,), in_specs=[pl.BlockS...  18.3 us
    pallas_call x3, Pallas kernels, own_of(): pl.pallas_call(functools.partial(own_kernel, nodes, done, steps), grid=(s...  15.5 us
    all_to_all x1, starting transfers between devices, shards(): got = lax.all_to_all(sent, 'dp', split_axis=0, concat_axis=0, tiled=True)  7.14 us
    all_to_all x1, starting transfers between devices, shards(): lax.all_to_all(back, 'dp', split_axis=0, concat_axis=0, tiled=True)  5.88 us
  transfers between devices with their start and end apart: 33, of which 13 were waited for; matrix products, arithmetic and copies ran while one was open for 3% of the time, Pallas kernels for 19%

profile of v5, /device:TPU:0, one launch (start us, length us, event | category | flops | bytes accessed | tf_op | source)
XLA Modules:
  0.0 185.2 jit_solution(11769818116744622039)
XLA Ops:
  0.6 18.3 %forward.1 = (bf16[4096,1024]{1,0:T(8,128)(2,1)}, f32[4096,1024]{1,0:T(8,128)}, f32[4096,128]{1,0:T(8,128)}, bf16[4096,128]{1,0:T(8,128)(2,1)}, f32[128,128]{1,0:T(8,128)}) custom-call(bf16[4096,1024]{1,0:T(8,128)(2,1)} %refs_8_.1, bf16[1024,1024]{1,0:T(8,128)(2,1)} %w_in_ref.1, bf16[1024,128]{1,0:T(8,128)(2,1)} %refs_11_.1), custom_call_target="tpu_custom_call" | custom-call | flops 9663676416 | bytes 25165824 | tf_op jit(solution)/shard_map/forward/pallas_call | solution.py:66
  19.5 4.7 %send.1 = bf16[2048,128]{1,0:T(8,128)(2,1)} custom-call(s32[2048]{0:T(1024)} %index_ref.1, f32[4096,128]{1,0:T(8,128)} %get-tuple-element.48.y_ref.refs_2_.refs_3_), custom_call_target="tpu_custom_call" | custom-call | flops 2147483648 | bytes 1572864 | tf_op jit(solution)/shard_map/send/pallas_call | solution.py:109
  24.2 7.1 %all-to-all-start = ((bf16[32,64,128]{2,1,0:T(8,128)(2,1)}), bf16[32,64,128]{2,1,0:T(8,128)(2,1)S(1)}, u32[]{:S(2)}, u32[]{:S(2)}) async-start(bf16[32,64,128]{2,1,0:T(8,128)(2,1)} %bitcast.15), calls=%async_computation | async-start | bytes 1048576 | tf_op jit(solution)/shard_map/all_to_all | solution.py:643
  39.3 9.3 %weights.2 = (bf16[2048,2048]{1,0:T(8,128)(2,1)}, f32[2048,128]{1,0:T(8,128)}, f32[144,2048]{1,0:T(8,128)}, f32[128,128]{1,0:T(8,128)}) custom-call(s32[256,256]{1,0:T(8,128)} %reshape.27.refs_0_, f32[256,256]{1,0:T(8,128)} %reshape.28.refs_1_, f32[4096,128]{1,0:T(8,128)} %get-tuple-element.48.y_ref.refs_2_.refs_3_, bf16[4096,128]{1,0:T(8,128)(2,1)} %get-tuple-element.59.refs_3_), custom_call_target="tpu_custom_call" | custom-call | flops 2147483648 | bytes 8388608 | tf_op jit(solution)/shard_map/weights/pallas_call | solution.py:181
  50.3 2.4 %collective-permute-start.5 = (f32[128,128]{1,0:T(8,128)S(1)}, f32[128,128]{1,0:T(8,128)S(1)}, u32[]{:S(2)}, u32[]{:S(2)}) collective-permute-start(f32[128,128]{1,0:T(8,128)S(1)} %add_add_fusion.3), channel_id=1, source_target_pairs={{0,16},{1,17},{2,18},{3,19},{4,20},{5,21},{6,22},{7,23},{8,24},{9,... | collective-permute-start | bytes 196616 | tf_op jit(solution)/shard_map/ppermute | solution.py:574
  53.1 9.7 %weights.3 = (bf16[2048,2048]{1,0:T(8,128)(2,1)}, f32[2048,128]{1,0:T(8,128)}, f32[144,2048]{1,0:T(8,128)}, f32[128,128]{1,0:T(8,128)}) custom-call(s32[256,256]{1,0:T(8,128)} %reshape.27.refs_0_, f32[256,256]{1,0:T(8,128)} %reshape.28.refs_1_, f32[4096,128]{1,0:T(8,128)} %get-tuple-element.48.y_ref.refs_2_.refs_3_, ...), custom_call_target="tpu_custom_call" | custom-call | flops 2147483648 | bytes 8388608 | tf_op jit(solution)/shard_map/weights/pallas_call | solution.py:181
  64.4 3.4 %back.1 = (bf16[2048,128]{1,0:T(8,128)(2,1)}, f32[128,128]{1,0:T(8,128)}) custom-call(bf16[2048,128]{1,0:T(8,128)(2,1)} %bitcast.10, f32[144,2048]{1,0:T(8,128)} %get-tuple-element.68.sums_ref, f32[128,128]{1,0:T(8,128)} %get-tuple-element.69.square_ref), custom_call_target="tpu_custom_call" | custom-call | flops 134217728 | bytes 1572864 | tf_op jit(solution)/shard_map/back/pallas_call | solution.py:219
  67.8 5.9 %all-to-all-start.1 = ((bf16[32,64,128]{2,1,0:T(8,128)(2,1)}), bf16[32,64,128]{2,1,0:T(8,128)(2,1)S(1)}, u32[]{:S(2)}, u32[]{:S(2)}) async-start(bf16[32,64,128]{2,1,0:T(8,128)(2,1)} %bitcast.14), calls=%async_computation.1 | async-start | bytes 1048576 | tf_op jit(solution)/shard_map/all_to_all | solution.py:661
  73.8 4.6 %own.3 = (f32[1024,128]{1,0:T(8,128)}, f32[128,128]{1,0:T(8,128)}) custom-call(bf16[2048,2048]{1,0:T(8,128)(2,1)} %get-tuple-element.53.weights_ref, f32[2048,128]{1,0:T(8,128)} %get-tuple-element.54.scaled_ref, bf16[2048,128]{1,0:T(8,128)(2,1)} %bitcast.11, f32[128,128]{1,0:T(8,128)} %add_add_fusion.2.matrix_ref), custom_call_target="tpu_custom_call" | custom-call | flops 536870912 | bytes 4194304 | tf_op jit(solution)/shard_map/own/pallas_call | solution.py:272
  78.4 2.6 %collective-permute-start.10 = (f32[128,128]{1,0:T(8,128)S(1)}, f32[128,128]{1,0:T(8,128)S(1)}, u32[]{:S(2)}, u32[]{:S(2)}) collective-permute-start(f32[128,128]{1,0:T(8,128)S(1)} %add.70), channel_id=1, source_target_pairs={{0,6},{1,7},{2,4},{3,5},{4,2},{5,3},{6,0},{7,1},{8,14},{9,15},{10,... | collective-permute-start | bytes 196616 | tf_op jit(solution)/shard_map/ppermute | solution.py:574
  82.0 4.6 %own.4 = (f32[1024,128]{1,0:T(8,128)}, f32[128,128]{1,0:T(8,128)}) custom-call(bf16[2048,2048]{1,0:T(8,128)(2,1)} %get-tuple-element.53.weights_ref, f32[2048,128]{1,0:T(8,128)} %get-tuple-element.54.scaled_ref, bf16[2048,128]{1,0:T(8,128)(2,1)} %bitcast.12, f32[128,128]{1,0:T(8,128)} %get-tuple-element.73.matrix_ref), custom_call_target="tpu_custom_call" | custom-call | flops 536870912 | bytes 4194304 | tf_op jit(solution)/shard_map/own/pallas_call | solution.py:272
  88.4 2.4 %collective-permute-start.12 = (f32[128,128]{1,0:T(8,128)S(1)}, f32[128,128]{1,0:T(8,128)S(1)}, u32[]{:S(2)}, u32[]{:S(2)}) collective-permute-start(f32[128,128]{1,0:T(8,128)S(1)} %add_add_fusion.1), channel_id=1, source_target_pairs={{0,16},{1,17},{2,18},{3,19},{4,20},{5,21},{6,22},{7,23},{8,24},{9,... | collective-permute-start | bytes 196616 | tf_op jit(solution)/shard_map/ppermute | solution.py:574
  91.1 6.2 %own.5 = (f32[2048,128]{1,0:T(8,128)}, f32[128,128]{1,0:T(8,128)}) custom-call(bf16[2048,2048]{1,0:T(8,128)(2,1)} %get-tuple-element.75.weights_ref, f32[2048,128]{1,0:T(8,128)} %get-tuple-element.76.scaled_ref, bf16[2048,128]{1,0:T(8,128)(2,1)} %bitcast.13, f32[128,128]{1,0:T(8,128)} %get-tuple-element.77.matrix_ref), custom_call_target="tpu_custom_call" | custom-call | flops 1073741824 | bytes 8388608 | tf_op jit(solution)/shard_map/own/pallas_call | solution.py:272
  99.5 27.0 %packed_grads.1 = (f32[512,1152]{1,0:T(8,128)}, bf16[512,1152]{1,0:T(8,128)(2,1)}) custom-call(f32[1024,128]{1,0:T(8,128)S(1)} %copy-done.1, f32[1024,128]{1,0:T(8,128)S(1)} %copy-done.2, f32[2048,128]{1,0:T(8,128)S(1)} %copy-done, f32[4096,128]{1,0:T(8,128)} %get-tuple-element.48.y_ref.refs_2_.refs_3_, s32[1,2048]{1,0:T(1,128)S(1)} %bitcast.9, ...), custom_call_target="tpu_custom_call" | custom-call | flops 10737418240 | bytes 33554432 | tf_op jit(solution)/shard_map/packed_grads/pallas_call | solution.py:502
  126.5 3.1 %collective-permute-done.14 = bf16[512,1152]{1,0:T(8,128)(2,1)S(1)} collective-permute-done((bf16[512,1152]{1,0:T(8,128)(2,1)}, bf16[512,1152]{1,0:T(8,128)(2,1)S(1)}, u32[]{:S(2)}, u32[]{:S(2)}) %collective-permute-start.14) | collective-permute-done | bytes 1179680 | tf_op jit(solution)/shard_map/ppermute | solution.py:574
  135.1 6.4 %collective-permute-done.15 = bf16[128,1152]{1,0:T(8,128)(2,1)S(1)} collective-permute-done((bf16[128,1152]{1,0:T(8,128)(2,1)S(1)}, bf16[128,1152]{1,0:T(8,128)(2,1)S(1)}, u32[]{:S(2)}, u32[]{:S(2)}) %collective-permute-start.15) | collective-permute-done | bytes 294944 | tf_op jit(solution)/shard_map/ppermute | solution.py:574
  141.5 6.9 %collective-permute-done.16 = bf16[128,1152]{1,0:T(8,128)(2,1)S(1)} collective-permute-done((bf16[128,1152]{1,0:T(8,128)(2,1)S(1)}, bf16[128,1152]{1,0:T(8,128)(2,1)S(1)}, u32[]{:S(2)}, u32[]{:S(2)}) %collective-permute-start.16) | collective-permute-done | bytes 294944 | tf_op jit(solution)/shard_map/ppermute | solution.py:574
  149.2 3.3 %collective-permute-start.19 = (bf16[32,1152]{1,0:T(8,128)(2,1)S(1)}, bf16[32,1152]{1,0:T(8,128)(2,1)S(1)}, u32[]{:S(2)}, u32[]{:S(2)}) collective-permute-start(bf16[32,1152]{1,0:T(8,128)(2,1)S(1)} %get-tuple-element.103), channel_id=1, source_target_pairs={{0,16},{1,17},{2,18},{3,19},{4,20},{5,21},{6,22},{7,23},{8,24},{9,... | collective-permute-start | bytes 221192 | tf_op jit(solution)/shard_map/ppermute | solution.py:574
  153.6 3.3 %collective-permute-done.19 = bf16[32,1152]{1,0:T(8,128)(2,1)S(1)} collective-permute-done((bf16[32,1152]{1,0:T(8,128)(2,1)S(1)}, bf16[32,1152]{1,0:T(8,128)(2,1)S(1)}, u32[]{:S(2)}, u32[]{:S(2)}) %collective-permute-start.19) | collective-permute-done | bytes 73760 | tf_op jit(solution)/shard_map/ppermute | solution.py:574
  160.9 2.4 %collective-permute-start.23 = (bf16[32,1152]{1,0:T(8,128)(2,1)S(1)}, bf16[32,1152]{1,0:T(8,128)(2,1)S(1)}, u32[]{:S(2)}, u32[]{:S(2)}) collective-permute-start(bf16[32,1152]{1,0:T(8,128)(2,1)S(1)} %fusion.4), channel_id=1, source_target_pairs={{0,24},{1,25},{2,26},{3,27},{4,28},{5,29},{6,30},{7,31},{8,16},{9,... | collective-permute-start | bytes 221192 | tf_op jit(solution)/shard_map/ppermute | solution.py:574
  164.8 2.4 %collective-permute-done.23 = bf16[32,1152]{1,0:T(8,128)(2,1)S(1)} collective-permute-done((bf16[32,1152]{1,0:T(8,128)(2,1)S(1)}, bf16[32,1152]{1,0:T(8,128)(2,1)S(1)}, u32[]{:S(2)}, u32[]{:S(2)}) %collective-permute-start.23) | collective-permute-done | bytes 73760 | tf_op jit(solution)/shard_map/ppermute | solution.py:574
  170.7 5.6 %collective-permute-done.24.refs_1_ = bf16[128,1152]{1,0:T(8,128)(2,1)S(1)} collective-permute-done((bf16[128,1152]{1,0:T(8,128)(2,1)S(1)}, bf16[128,1152]{1,0:T(8,128)(2,1)S(1)}, u32[]{:S(2)}, u32[]{:S(2)}) %collective-permute-start.24) | collective-permute-done | bytes 294944 | tf_op jit(solution)/shard_map/ppermute | solution.py:574
  176.3 4.3 %collective-permute-done.25.refs_2_ = bf16[128,1152]{1,0:T(8,128)(2,1)S(1)} collective-permute-done((bf16[128,1152]{1,0:T(8,128)(2,1)S(1)}, bf16[128,1152]{1,0:T(8,128)(2,1)S(1)}, u32[]{:S(2)}, u32[]{:S(2)}) %collective-permute-start.25) | collective-permute-done | bytes 294944 | tf_op jit(solution)/shard_map/ppermute | solution.py:574
  182.6 2.6 %unpack.1 = (f32[4,8,32,1024]{3,2,1,0:T(8,128)}, f32[4,8,32,128]{3,2,1,0:T(8,128)}) custom-call(s32[1]{0:T(128)} %bitcast.refs_12_.me_ref, bf16[128,1152]{1,0:T(8,128)(2,1)S(1)} %pad_maximum_fusion.refs_0_, bf16[128,1152]{1,0:T(8,128)(2,1)S(1)} %collective-permute-done.24.refs_1_, bf16[128,1152]{1,0:T(8,128)(2,1)S(1)} %collective-permute-done.25.refs_2_, ...), custom_call_target="tpu_custom_call" | custom-call | flops 1000000000 | tf_op jit(solution)/shard_map/unpack/pallas_call | solution.py:558
  (93 shorter events, 35.6 us)
Async XLA Ops:
  19.0 16.8 %collective-permute-start = (f32[128,128]{1,0:T(8,128)}, f32[128,128]{1,0:T(8,128)S(1)}, u32[]{:S(2)}, u32[]{:S(2)}) collective-permute-start(f32[128,128]{1,0:T(8,128)} %get-tuple-element.49), channel_id=1, source_target_pairs={{0,1},{1,0},{2,3},{3,2},{4,5},{5,4},{6,7},{7,6},{8,9},{9,8},{10,11... | collective-permute-start | bytes 196616 | tf_op jit(solution)/shard_map/ppermute | solution.py:574
  24.2 39.4 %all-to-all-start = ((bf16[32,64,128]{2,1,0:T(8,128)(2,1)}), bf16[32,64,128]{2,1,0:T(8,128)(2,1)S(1)}, u32[]{:S(2)}, u32[]{:S(2)}) async-start(bf16[32,64,128]{2,1,0:T(8,128)(2,1)} %bitcast.15), calls=%async_computation | async-start | bytes 1048576 | tf_op jit(solution)/shard_map/all_to_all | solution.py:643
  35.8 12.9 %collective-permute-start.1 = (f32[128,128]{1,0:T(8,128)S(1)}, f32[128,128]{1,0:T(8,128)S(1)}, u32[]{:S(2)}, u32[]{:S(2)}) collective-permute-start(f32[128,128]{1,0:T(8,128)S(1)} %add.63), channel_id=1, source_target_pairs={{0,2},{1,3},{2,0},{3,1},{4,6},{5,7},{6,4},{7,5},{8,10},{9,11},{10,... | collective-permute-start | bytes 196616 | tf_op jit(solution)/shard_map/ppermute | solution.py:574
  37.4 11.2 %collective-permute-start.2 = (f32[128,128]{1,0:T(8,128)S(1)}, f32[128,128]{1,0:T(8,128)S(1)}, u32[]{:S(2)}, u32[]{:S(2)}) collective-permute-start(f32[128,128]{1,0:T(8,128)S(1)} %add.63), channel_id=1, source_target_pairs={{0,4},{1,5},{2,6},{3,7},{4,0},{5,1},{6,2},{7,3},{8,12},{9,13},{10,... | collective-permute-start | bytes 196616 | tf_op jit(solution)/shard_map/ppermute | solution.py:574
  38.9 9.8 %collective-permute-start.3 = (f32[128,128]{1,0:T(8,128)S(1)}, f32[128,128]{1,0:T(8,128)S(1)}, u32[]{:S(2)}, u32[]{:S(2)}) collective-permute-start(f32[128,128]{1,0:T(8,128)S(1)} %add.63), channel_id=1, source_target_pairs={{0,6},{1,7},{2,4},{3,5},{4,2},{5,3},{6,0},{7,1},{8,14},{9,15},{10,... | collective-permute-start | bytes 196616 | tf_op jit(solution)/shard_map/ppermute | solution.py:574
  48.7 14.2 %collective-permute-start.4 = (f32[128,128]{1,0:T(8,128)S(1)}, f32[128,128]{1,0:T(8,128)S(1)}, u32[]{:S(2)}, u32[]{:S(2)}) collective-permute-start(f32[128,128]{1,0:T(8,128)S(1)} %add_add_fusion.3), channel_id=1, source_target_pairs={{0,8},{1,9},{2,10},{3,11},{4,12},{5,13},{6,14},{7,15},{8,0},{9,1},... | collective-permute-start | bytes 196616 | tf_op jit(solution)/shard_map/ppermute | solution.py:574
  50.3 12.6 %collective-permute-start.5 = (f32[128,128]{1,0:T(8,128)S(1)}, f32[128,128]{1,0:T(8,128)S(1)}, u32[]{:S(2)}, u32[]{:S(2)}) collective-permute-start(f32[128,128]{1,0:T(8,128)S(1)} %add_add_fusion.3), channel_id=1, source_target_pairs={{0,16},{1,17},{2,18},{3,19},{4,20},{5,21},{6,22},{7,23},{8,24},{9,... | collective-permute-start | bytes 196616 | tf_op jit(solution)/shard_map/ppermute | solution.py:574
  52.8 10.1 %collective-permute-start.6 = (f32[128,128]{1,0:T(8,128)S(1)}, f32[128,128]{1,0:T(8,128)S(1)}, u32[]{:S(2)}, u32[]{:S(2)}) collective-permute-start(f32[128,128]{1,0:T(8,128)S(1)} %add_add_fusion.3), channel_id=1, source_target_pairs={{0,24},{1,25},{2,26},{3,27},{4,28},{5,29},{6,30},{7,31},{8,16},{9,... | collective-permute-start | bytes 196616 | tf_op jit(solution)/shard_map/ppermute | solution.py:574
  67.8 29.6 %all-to-all-start.1 = ((bf16[32,64,128]{2,1,0:T(8,128)(2,1)}), bf16[32,64,128]{2,1,0:T(8,128)(2,1)S(1)}, u32[]{:S(2)}, u32[]{:S(2)}) async-start(bf16[32,64,128]{2,1,0:T(8,128)(2,1)} %bitcast.14), calls=%async_computation.1 | async-start | bytes 1048576 | tf_op jit(solution)/shard_map/all_to_all | solution.py:661
  78.4 8.2 %collective-permute-start.10 = (f32[128,128]{1,0:T(8,128)S(1)}, f32[128,128]{1,0:T(8,128)S(1)}, u32[]{:S(2)}, u32[]{:S(2)}) collective-permute-start(f32[128,128]{1,0:T(8,128)S(1)} %add.70), channel_id=1, source_target_pairs={{0,6},{1,7},{2,4},{3,5},{4,2},{5,3},{6,0},{7,1},{8,14},{9,15},{10,... | collective-permute-start | bytes 196616 | tf_op jit(solution)/shard_map/ppermute | solution.py:574
  86.7 10.7 %collective-permute-start.11 = (f32[128,128]{1,0:T(8,128)S(1)}, f32[128,128]{1,0:T(8,128)S(1)}, u32[]{:S(2)}, u32[]{:S(2)}) collective-permute-start(f32[128,128]{1,0:T(8,128)S(1)} %add_add_fusion.1), channel_id=1, source_target_pairs={{0,8},{1,9},{2,10},{3,11},{4,12},{5,13},{6,14},{7,15},{8,0},{9,1},... | collective-permute-start | bytes 196616 | tf_op jit(solution)/shard_map/ppermute | solution.py:574
  88.4 8.9 %collective-permute-start.12 = (f32[128,128]{1,0:T(8,128)S(1)}, f32[128,128]{1,0:T(8,128)S(1)}, u32[]{:S(2)}, u32[]{:S(2)}) collective-permute-start(f32[128,128]{1,0:T(8,128)S(1)} %add_add_fusion.1), channel_id=1, source_target_pairs={{0,16},{1,17},{2,18},{3,19},{4,20},{5,21},{6,22},{7,23},{8,24},{9,... | collective-permute-start | bytes 196616 | tf_op jit(solution)/shard_map/ppermute | solution.py:574
  90.8 6.5 %collective-permute-start.13 = (f32[128,128]{1,0:T(8,128)S(1)}, f32[128,128]{1,0:T(8,128)S(1)}, u32[]{:S(2)}, u32[]{:S(2)}) collective-permute-start(f32[128,128]{1,0:T(8,128)S(1)} %add_add_fusion.1), channel_id=1, source_target_pairs={{0,24},{1,25},{2,26},{3,27},{4,28},{5,29},{6,30},{7,31},{8,16},{9,... | collective-permute-start | bytes 196616 | tf_op jit(solution)/shard_map/ppermute | solution.py:574
  131.6 9.9 %collective-permute-start.15 = (bf16[128,1152]{1,0:T(8,128)(2,1)S(1)}, bf16[128,1152]{1,0:T(8,128)(2,1)S(1)}, u32[]{:S(2)}, u32[]{:S(2)}) collective-permute-start(bf16[128,1152]{1,0:T(8,128)(2,1)S(1)} %get-tuple-element.98), channel_id=1, source_target_pairs={{0,2},{1,3},{2,0},{3,1},{4,6},{5,7},{6,4},{7,5},{8,10},{9,11},{10,... | collective-permute-start | bytes 884744 | tf_op jit(solution)/shard_map/ppermute | solution.py:574
  133.3 15.1 %collective-permute-start.16 = (bf16[128,1152]{1,0:T(8,128)(2,1)S(1)}, bf16[128,1152]{1,0:T(8,128)(2,1)S(1)}, u32[]{:S(2)}, u32[]{:S(2)}) collective-permute-start(bf16[128,1152]{1,0:T(8,128)(2,1)S(1)} %get-tuple-element.100), channel_id=1, source_target_pairs={{0,4},{1,5},{2,6},{3,7},{4,0},{5,1},{6,2},{7,3},{8,12},{9,13},{10,... | collective-permute-start | bytes 884744 | tf_op jit(solution)/shard_map/ppermute | solution.py:574
  134.8 13.6 %collective-permute-start.17 = (bf16[128,1152]{1,0:T(8,128)(2,1)S(1)}, bf16[128,1152]{1,0:T(8,128)(2,1)S(1)}, u32[]{:S(2)}, u32[]{:S(2)}) collective-permute-start(bf16[128,1152]{1,0:T(8,128)(2,1)S(1)} %get-tuple-element.99), channel_id=1, source_target_pairs={{0,6},{1,7},{2,4},{3,5},{4,2},{5,3},{6,0},{7,1},{8,14},{9,15},{10,... | collective-permute-start | bytes 884744 | tf_op jit(solution)/shard_map/ppermute | solution.py:574
  149.2 7.7 %collective-permute-start.19 = (bf16[32,1152]{1,0:T(8,128)(2,1)S(1)}, bf16[32,1152]{1,0:T(8,128)(2,1)S(1)}, u32[]{:S(2)}, u32[]{:S(2)}) collective-permute-start(bf16[32,1152]{1,0:T(8,128)(2,1)S(1)} %get-tuple-element.103), channel_id=1, source_target_pairs={{0,16},{1,17},{2,18},{3,19},{4,20},{5,21},{6,22},{7,23},{8,24},{9,... | collective-permute-start | bytes 221192 | tf_op jit(solution)/shard_map/ppermute | solution.py:574
  152.6 6.2 %collective-permute-start.20 = (bf16[32,1152]{1,0:T(8,128)(2,1)S(1)}, bf16[32,1152]{1,0:T(8,128)(2,1)S(1)}, u32[]{:S(2)}, u32[]{:S(2)}) collective-permute-start(bf16[32,1152]{1,0:T(8,128)(2,1)S(1)} %get-tuple-element.102), channel_id=1, source_target_pairs={{0,24},{1,25},{2,26},{3,27},{4,28},{5,29},{6,30},{7,31},{8,16},{9,... | collective-permute-start | bytes 221192 | tf_op jit(solution)/shard_map/ppermute | solution.py:574
  158.8 5.9 %collective-permute-start.22 = (bf16[32,1152]{1,0:T(8,128)(2,1)S(1)}, bf16[32,1152]{1,0:T(8,128)(2,1)S(1)}, u32[]{:S(2)}, u32[]{:S(2)}) collective-permute-start(bf16[32,1152]{1,0:T(8,128)(2,1)S(1)} %fusion.4), channel_id=1, source_target_pairs={{0,16},{1,17},{2,18},{3,19},{4,20},{5,21},{6,22},{7,23},{8,24},{9,... | collective-permute-start | bytes 221192 | tf_op jit(solution)/shard_map/ppermute | solution.py:574
  160.9 6.3 %collective-permute-start.23 = (bf16[32,1152]{1,0:T(8,128)(2,1)S(1)}, bf16[32,1152]{1,0:T(8,128)(2,1)S(1)}, u32[]{:S(2)}, u32[]{:S(2)}) collective-permute-start(bf16[32,1152]{1,0:T(8,128)(2,1)S(1)} %fusion.4), channel_id=1, source_target_pairs={{0,24},{1,25},{2,26},{3,27},{4,28},{5,29},{6,30},{7,31},{8,16},{9,... | collective-permute-start | bytes 221192 | tf_op jit(solution)/shard_map/ppermute | solution.py:574
  167.2 9.1 %collective-permute-start.24 = (bf16[128,1152]{1,0:T(8,128)(2,1)S(1)}, bf16[128,1152]{1,0:T(8,128)(2,1)S(1)}, u32[]{:S(2)}, u32[]{:S(2)}) collective-permute-start(bf16[128,1152]{1,0:T(8,128)(2,1)S(1)} %pad_maximum_fusion.refs_0_), channel_id=1, source_target_pairs={{0,2},{1,3},{2,0},{3,1},{4,6},{5,7},{6,4},{7,5},{8,10},{9,11},{10,... | collective-permute-start | bytes 884744 | tf_op jit(solution)/shard_map/ppermute | solution.py:574
  168.6 11.9 %collective-permute-start.25 = (bf16[128,1152]{1,0:T(8,128)(2,1)S(1)}, bf16[128,1152]{1,0:T(8,128)(2,1)S(1)}, u32[]{:S(2)}, u32[]{:S(2)}) collective-permute-start(bf16[128,1152]{1,0:T(8,128)(2,1)S(1)} %pad_maximum_fusion.refs_0_), channel_id=1, source_target_pairs={{0,4},{1,5},{2,6},{3,7},{4,0},{5,1},{6,2},{7,3},{8,12},{9,13},{10,... | collective-permute-start | bytes 884744 | tf_op jit(solution)/shard_map/ppermute | solution.py:574
  169.2 11.3 %collective-permute-start.26 = (bf16[128,1152]{1,0:T(8,128)(2,1)S(1)}, bf16[128,1152]{1,0:T(8,128)(2,1)S(1)}, u32[]{:S(2)}, u32[]{:S(2)}) collective-permute-start(bf16[128,1152]{1,0:T(8,128)(2,1)S(1)} %pad_maximum_fusion.refs_0_), channel_id=1, source_target_pairs={{0,6},{1,7},{2,4},{3,5},{4,2},{5,3},{6,0},{7,1},{8,14},{9,15},{10,... | collective-permute-start | bytes 884744 | tf_op jit(solution)/shard_map/ppermute | solution.py:574
  170.7 10.4 %collective-permute-start.27 = (bf16[128,1152]{1,0:T(8,128)(2,1)S(1)}, bf16[128,1152]{1,0:T(8,128)(2,1)S(1)}, u32[]{:S(2)}, u32[]{:S(2)}) collective-permute-start(bf16[128,1152]{1,0:T(8,128)(2,1)S(1)} %pad_maximum_fusion.refs_0_), channel_id=1, source_target_pairs={{0,1},{1,0},{2,3},{3,2},{4,5},{5,4},{6,7},{7,6},{8,9},{9,8},{10,11... | collective-permute-start | bytes 884744 | tf_op jit(solution)/shard_map/ppermute | solution.py:574
  (21 other events, 98.0 us)
